TPU v7x, 32 devices: a whole 2x2x4 slice. The times are simulated.
32 devices in a mesh: seq: 8 (over z, y), sub: 4 (over x, core).
Axes of the slice: x: 2, y: 2, z: 4, core: 2. Of those that a mesh axis runs over, the one named last changes fastest.
Arguments:
- queries: bfloat16 [4096, 1024], P(('seq', 'sub')), may hold values from -6 to 6
- key_vectors: bfloat16 [4096, 1024], P(('seq', 'sub')), may hold values from -6 to 6
- values: bfloat16 [4096, 2048], P(('seq', 'sub')), may hold values from -6 to 6
- log_decay: float32 [16, 4096], P(None, ('seq', 'sub')), may hold values from -0.85 to 0, as said below
- write_rate: float32 [16, 4096], P(None, ('seq', 'sub')), may hold values from 0 to 1
- passage_lengths: int32 [8], replicated, may hold values from 1 to 2048, 4096 in all
- norm_gain: float32 [128], replicated, may hold values from 0.1 to 1.9
Outputs:
- head_outputs: bfloat16 [4096, 2048], P(('seq', 'sub'))
Inputs may be any that keep to these rules, and one draw needn't show every extreme that they name: `passage_lengths`: 8 segment lengths that add up to 4096; the longest holds exactly 2048 tokens. `log_decay`: never positive.
All inputs are finite; a program needn't handle non-finite values.
Results may differ from a plain program's by a relative error of at most 0.001.
Values sent between devices are 32-bit elements; how exact they have to be, the bound alone decides.
No kernel may reach another device: no remote copies, remote signals or barrier semaphores. Data moves between devices by JAX's collectives and lax.ppermute only.
A program may use at most 192 MiB of HBM per device.

v0:
```python
import functools

import jax
import jax.numpy as jnp
from jax import lax
from jax.experimental import pallas as pl
from jax.experimental.pallas import tpu as pltpu
from jax.sharding import PartitionSpec as P

D = 128
VALUE_HEADS = 16
HK = 8
BLOCK = 128
AXES = ("seq", "sub")
CHIPS = 4
GROUP = 2 * CHIPS
PHASES = ((0, 1),)
LONGEST = {4096: 2048, 65536: 8192}

f32 = jnp.float32
bf16 = jnp.bfloat16
VMEM = pl.BlockSpec(memory_space=pltpu.VMEM)
SMEM = pl.BlockSpec(memory_space=pltpu.SMEM)


def head_of(core, chip, part):
    return 8 * core + 2 * chip + part


def my_rank(n_sub):
    return lax.axis_index("seq") * n_sub + lax.axis_index("sub")


def mm(a, b):
    return lax.dot_general(a, b, (((1,), (0,)), ((), ())), preferred_element_type=f32)


def mm_nt(a, b, precision=None):
    return lax.dot_general(
        a, b, (((1,), (1,)), ((), ())), preferred_element_type=f32, precision=precision
    )


def split(x):
    high = x.astype(bf16)
    return high, (x - high.astype(f32)).astype(bf16)


def mm3(a, b):
    a_high, a_low = split(a)
    b_high, b_low = split(b)
    return mm(a_high, b_high) + (mm(a_high, b_low) + mm(a_low, b_high))


def mm2(a, b):
    a_high, a_low = split(a)
    return mm(a_high, b) + mm(a_low, b)


def compose(later, early):
    both = mm3(later[:, :D], early)
    return jnp.concatenate([both[:, :D], both[:, D:] + later[:, D:]], axis=1)


def iota(axis):
    return lax.broadcasted_iota(jnp.int32, (BLOCK, BLOCK), axis)


def token_masks(lengths_ref, n_sub):
    first = my_rank(n_sub) * BLOCK
    row_at = first + lax.broadcasted_iota(jnp.int32, (1, BLOCK), 1)
    col_at = first + lax.broadcasted_iota(jnp.int32, (BLOCK, 1), 0)

    def one(i, carried):
        start, row, col, before = carried
        row = row + (row_at >= start).astype(jnp.int32)
        col = col + (col_at >= start).astype(jnp.int32)
        before = before + (first > start).astype(jnp.int32)
        return start + lengths_ref[i], row, col, before

    zero = jnp.int32(0)
    _, row, col, before = lax.fori_loop(
        0,
        lengths_ref.shape[0],
        one,
        (zero, jnp.zeros((1, BLOCK), jnp.int32), jnp.zeros((BLOCK, 1), jnp.int32), zero),
    )
    return row, col, before


def gates(decay_ref, rate_ref):
    decay = decay_ref[...]
    lower = (iota(0) >= iota(1)).astype(f32)
    eye = (iota(0) == iota(1)).astype(f32)
    highest = lax.Precision.HIGHEST
    sum_row = mm_nt(decay, lower, highest)
    sum_col = mm_nt(lower, decay, highest)
    rate_row = rate_ref[...]
    rate_col = mm_nt(eye, rate_row, highest)
    return sum_row, sum_col, rate_row, rate_col


def key_norms(key, key_t):
    wide = key.astype(f32)
    col = lax.rsqrt(jnp.sum(wide * wide, axis=1, keepdims=True) + 1e-06)
    wide_t = key_t.astype(f32)
    row = lax.rsqrt(jnp.sum(wide_t * wide_t, axis=0, keepdims=True) + 1e-06)
    return col, row


def maps_kernel(
    parts, n_sub, lengths_ref, k_ref, v_ref, decay_ref, rate_ref, keep_ref, send_ref, inverse_ref
):
    core = lax.rem(my_rank(n_sub), 2)
    seg_row, seg_col, before = token_masks(lengths_ref, n_sub)
    sum_row, sum_col, rate_row, rate_col = gates(decay_ref, rate_ref)
    apart = iota(0) ^ iota(1)
    strict = (iota(0) > iota(1)) & (seg_row == seg_col)
    eye = (apart == 0).astype(f32)
    reaches = (seg_row == before).astype(f32)
    last = seg_row[:, BLOCK - 1 :]
    ends_col = (seg_col == last).astype(f32)

    for core_of in range(2):
        for chip in range(CHIPS):
            j = 4 * core_of + chip
            key = k_ref[:, j * D : (j + 1) * D]
            key_t = key.T
            n_col, n_row = key_norms(key, key_t)
            gram = mm(key, key_t) * n_row
            for place, part in enumerate(parts):
                h = head_of(core_of, chip, part)
                s_row, s_col = sum_row[h : h + 1, :], sum_col[:, h : h + 1]
                b_row, b_col = rate_row[h : h + 1, :], rate_col[:, h : h + 1]
                between = jnp.exp(jnp.minimum(s_col - s_row, 0.0))
                system = jnp.where(strict, between * gram * (b_col * n_col), 0.0)
                solved = eye - jnp.where(apart == 1, system, 0.0)
                size = 2
                while size < BLOCK:
                    corner = jnp.where((apart >= size) & (apart < 2 * size), system, 0.0)
                    solved = solved - mm3(solved, mm3(corner, solved))
                    size = 2 * size
                inverse_ref[h // 2, place] = solved
                from_row = jnp.exp(s_row) * reaches
                to_end = jnp.exp(s_col[BLOCK - 1 :, :] - s_col) * ends_col
                value = v_ref[:, h * D : (h + 1) * D]
                fresh = mm2(solved * b_row, value)
                wy = mm2(solved * (b_row * from_row * n_row), key)
                scaled = jnp.concatenate([wy, fresh], axis=1) * (to_end * n_col)
                high, low = split(scaled)
                both = mm(key_t, high) + mm(key_t, low)
                whole = from_row[:, BLOCK - 1 :]
                pair = jnp.concatenate([whole * eye - both[:, :D], both[:, D:]], axis=1)

                @pl.when(core == core_of)
                def _():
                    keep_ref[chip, place] = pair

                @pl.when(core != core_of)
                def _():
                    send_ref[chip, place] = pair


def chip_kernel(n_sub, keep_ref, recv_ref, *out_refs):
    rank = my_rank(n_sub)
    core, chip = lax.rem(rank, 2), lax.rem(rank // 2, CHIPS)
    first = core == 0
    for slot in range(CHIPS):
        other = chip ^ slot
        for place in range(keep_ref.shape[1]):
            mine, theirs = keep_ref[other, place], recv_ref[other, place]
            early = jnp.where(first, mine, theirs)
            late = jnp.where(first, theirs, mine)
            out_refs[slot][place] = compose(late, early)


def group_kernel(n_sub, r0, r1, r2, r3, total_map_ref, total_add_ref, ahead_ref, held):
    rank = my_rank(n_sub)
    chip = lax.rem(rank // 2, CHIPS)
    for slot, ref in enumerate((r0, r1, r2, r3)):
        held[chip ^ slot] = ref[...]
    for place in range(r0.shape[0]):
        one = held[0, place]
        two = compose(held[1, place], one)
        upper = compose(held[3, place], held[2, place])
        total = compose(upper, two)
        total_map_ref[place] = total[:, :D]
        total_add_ref[place] = total[:, D:]
        ahead_ref[place, 0] = one
        ahead_ref[place, 1] = two
        ahead_ref[place, 2] = compose(held[2, place], two)


def step_kernel(map_ref, add_ref, state_ref, out_ref):
    for place in range(map_ref.shape[0]):
        out_ref[place] = add_ref[place] + mm3(map_ref[place], state_ref[place])


def spread_kernel(n_sub, ahead_ref, state_ref, o0, o1, o2, o3, held):
    rank = my_rank(n_sub)
    chip = lax.rem(rank // 2, CHIPS)
    for place in range(state_ref.shape[0]):
        state = state_ref[place]
        held[0, place] = state
        for i in range(CHIPS - 1):
            held[i + 1, place] = (
                mm3(ahead_ref[place, i, :, :D], state) + ahead_ref[place, i, :, D:]
            )
    for slot, ref in enumerate((o0, o1, o2, o3)):
        ref[...] = held[chip ^ slot]


def readout_kernel(
    n_sub,
    n_phases,
    lengths_ref,
    q_ref,
    k_ref,
    v_ref,
    decay_ref,
    rate_ref,
    *refs,
):
    inverse_refs = refs[:n_phases]
    recv_refs = refs[n_phases : 2 * n_phases]
    extra_refs = refs[2 * n_phases : 3 * n_phases]
    read_ref = refs[3 * n_phases]
    core = lax.rem(my_rank(n_sub), 2)
    seg_row, seg_col, before = token_masks(lengths_ref, n_sub)
    sum_row, sum_col, rate_row, rate_col = gates(decay_ref, rate_ref)
    lower = (iota(0) >= iota(1)) & (seg_row == seg_col)
    reaches_row = (seg_row == before).astype(f32)
    reaches_col = (seg_col == before).astype(f32)
    per_phase = 2 // n_phases
    for j in range(HK):
        key = k_ref[:, j * D : (j + 1) * D]
        key_t = key.T
        n_col, n_row = key_norms(key, key_t)
        query = q_ref[:, j * D : (j + 1) * D]
        wide = query.astype(f32)
        q_col = lax.rsqrt(jnp.sum(wide * wide, axis=1, keepdims=True) + 1e-06)
        cross = mm(query, key_t) * n_row
        for part in range(2):
            h = 2 * j + part
            phase, place = part // per_phase, part % per_phase
            s_row, s_col = sum_row[h : h + 1, :], sum_col[:, h : h + 1]
            b_row = rate_row[h : h + 1, :]
            between = jnp.exp(jnp.minimum(s_col - s_row, 0.0))
            scores = jnp.where(lower, between * cross * q_col, 0.0)
            mixed = mm3(scores, inverse_refs[phase][j, place])
            from_row = jnp.exp(s_row) * reaches_row
            from_col = jnp.exp(s_col) * reaches_col
            fresh = mm2(mixed * b_row, v_ref[:, h * D : (h + 1) * D])
            through = wide * (from_col * q_col) - mm2(mixed * (b_row * from_row * n_row), key)

            @pl.when(core == 0)
            def _():
                read_ref[h] = jnp.concatenate([through, fresh], axis=1)

            @pl.when(core == 1)
            def _():
                source = recv_refs[phase] if j >= 4 else extra_refs[phase]
                both = mm3(through, source[j % 4, place])
                read_ref[h] = jnp.concatenate([both[:, :D], both[:, D:] + fresh], axis=1)


def output_kernel(n_sub, n_phases, gain_ref, read_ref, *refs):
    out_ref = refs[-1]
    rank = my_rank(n_sub)
    core, chip = lax.rem(rank, 2), lax.rem(rank // 2, CHIPS)
    per_phase = 2 // n_phases
    gain = gain_ref[...]
    for phase in range(n_phases):
        for swapped in range(2):
            for slot in range(CHIPS):
                states = refs[(phase * 2 + swapped) * CHIPS + slot]
                for place in range(per_phase):
                    h = head_of(core ^ swapped, chip ^ slot, phase * per_phase + place)
                    read = read_ref[h]
                    raw = mm3(read[:, :D], states[place]) + read[:, D:]
                    scale = lax.rsqrt(jnp.mean(raw * raw, axis=1, keepdims=True) + 1e-06)
                    at = pl.multiple_of(h * D, D)
                    out_ref[:, pl.ds(at, D)] = (raw * scale * gain).astype(bf16)


def call(kernel, outs, args, scratch=(), specs=None, flops=0, name=None):
    moved = sum(a.size * a.dtype.itemsize for a in args)
    moved += sum(o.size * o.dtype.itemsize for o in jax.tree.leaves(outs))
    return pl.pallas_call(
        kernel,
        out_shape=outs,
        in_specs=[VMEM] * len(args) if specs is None else specs,
        out_specs=jax.tree.map(lambda o: VMEM, outs),
        scratch_shapes=list(scratch),
        compiler_params=pltpu.CompilerParams(vmem_limit_bytes=32 * 2**20),
        cost_estimate=pl.CostEstimate(flops=flops, bytes_accessed=moved, transcendentals=0),
        name=name,
    )(*args)


def like(*shape):
    return jax.ShapeDtypeStruct(shape, f32)


def on_device(
    n_dev,
    n_sub,
    queries,
    key_vectors,
    values,
    log_decay,
    write_rate,
    passage_lengths,
    norm_gain,
):
    assert values.shape[0] == BLOCK
    tokens = n_dev * BLOCK
    longest = LONGEST.get(tokens, tokens)
    reach = min(-(-longest // (GROUP * BLOCK)), n_dev // GROUP)
    n_phases = len(PHASES)
    n = 2 // n_phases
    swap_pairs = [(i, i ^ 1) for i in range(n_dev)]
    up_pairs = [(i, i + 1) for i in range(0, n_dev, 2)]
    next_pairs = [(i, i + GROUP) for i in range(n_dev - GROUP)]

    def chip_pairs(slot):
        return [(i, i ^ (2 * slot)) for i in range(n_dev)]

    def permute(x, pairs):
        return lax.ppermute(x, AXES, pairs)

    step = 2 * BLOCK**3
    inverses, recvs, extras, states = [], [], [], []
    for parts in PHASES:
        keep, send, inverse = call(
            functools.partial(maps_kernel, parts, n_sub),
            (like(CHIPS, n, D, 2 * D), like(CHIPS, n, D, 2 * D), like(HK, n, BLOCK, BLOCK)),
            (passage_lengths, key_vectors, values, log_decay, write_rate),
            specs=[SMEM, VMEM, VMEM, VMEM, VMEM],
            flops=8 * n * 44 * step,
            name="maps",
        )
        recv = permute(send, swap_pairs)
        extra = permute(keep, up_pairs)
        inverses.append(inverse)
        recvs.append(recv)
        extras.append(extra)
        slots = call(
            functools.partial(chip_kernel, n_sub),
            (like(n, D, 2 * D),) * CHIPS,
            (keep, recv),
            flops=4 * n * 6 * step,
            name="chip",
        )
        got = [slots[0]] + [permute(slots[s], chip_pairs(s)) for s in range(1, CHIPS)]
        total_map, total_add, ahead = call(
            functools.partial(group_kernel, n_sub),
            (like(n, D, D), like(n, D, D), like(n, 3, D, 2 * D)),
            got,
            scratch=(pltpu.VMEM((CHIPS, n, D, 2 * D), f32),),
            flops=n * 24 * step,
            name="group",
        )
        state = total_add
        for _ in range(reach - 1):
            state = permute(state, next_pairs)
            state = call(
                step_kernel,
                like(n, D, D),
                (total_map, total_add, state),
                flops=n * 3 * step,
                name="step",
            )
        state = permute(state, next_pairs)
        outs = call(
            functools.partial(spread_kernel, n_sub),
            (like(n, D, D),) * CHIPS,
            (ahead, state),
            scratch=(pltpu.VMEM((CHIPS, n, D, D), f32),),
            flops=n * 9 * step,
            name="spread",
        )
        own = [outs[0]] + [permute(outs[s], chip_pairs(s)) for s in range(1, CHIPS)]
        states += own + [permute(x, swap_pairs) for x in own]

    read = call(
        functools.partial(readout_kernel, n_sub, n_phases),
        like(VALUE_HEADS, BLOCK, 2 * D),
        (
            passage_lengths,
            queries,
            key_vectors,
            values,
            log_decay,
            write_rate,
            *inverses,
            *recvs,
            *extras,
        ),
        specs=[SMEM] + [VMEM] * (5 + 3 * n_phases),
        flops=16 * 13 * step,
        name="readout",
    )
    return call(
        functools.partial(output_kernel, n_sub, n_phases),
        jax.ShapeDtypeStruct((BLOCK, VALUE_HEADS * D), bf16),
        (norm_gain.reshape(1, D), read, *states),
        flops=16 * 3 * step,
        name="output",
    )


def solution(mesh):
    n_sub = mesh.shape["sub"]
    n_dev = mesh.shape["seq"] * n_sub
    tokens = P(AXES, None)
    heads = P(None, AXES)
    return jax.shard_map(
        functools.partial(on_device, n_dev, n_sub),
        mesh=mesh,
        in_specs=(tokens, tokens, tokens, heads, heads, P(), P()),
        out_specs=tokens,
        check_vma=False,
    )
```

profile of v0, /device:TPU:25, one launch (start us, length us, event | category | flops | bytes accessed | tf_op | source)
XLA Modules:
  0.0 102.8 jit_solution(16386442045584589887)
XLA Ops:
  0.0 1.0 %copy-done = bf16[128,2048]{1,0:T(8,128)(2,1)S(1)} copy-done((bf16[128,2048]{1,0:T(8,128)(2,1)S(1)}, bf16[128,2048]{1,0:T(8,128)(2,1)}, u32[]{:S(2)}) %copy-start) | copy-done | bytes 524312
  1.0 0.9 copy-done.3
  2.0 0.7 copy-done.5
  2.7 0.7 copy-done.7
  3.4 0.7 copy-done.9
  4.0 42.4 %maps.1 = (f32[4,2,128,256]{3,2,1,0:T(8,128)S(1)}, f32[4,2,128,256]{3,2,1,0:T(8,128)S(1)}, f32[8,2,128,128]{3,2,1,0:T(8,128)S(1)}) custom-call(s32[8]{0:T(128)S(1)} %copy-done.9, bf16[128,1024]{1,0:T(8,128)(2,1)S(1)} %copy-done.3, bf16[128,2048]{1,0:T(8,128)(2,1)S(1)} %copy-done, f32[16,128]{1,0:T(8,128)S(1)} %copy-done.5, f32[16,128]{1,0:T(8,128)S(1)} %copy-done.7), custom_call_target="tpu_custom_call" | custom-call | flops 2952790016 | bytes 3948576 | tf_op jit(solution)/shard_map/maps/pallas_call | solution.py:289
  46.4 0.7 collective-permute-start
  47.2 1.4 %collective-permute-start.1 = (f32[4,2,128,256]{3,2,1,0:T(8,128)S(1)}, f32[4,2,128,256]{3,2,1,0:T(8,128)S(1)}, u32[]{:S(2)}, u32[]{:S(2)}) collective-permute-start(f32[4,2,128,256]{3,2,1,0:T(8,128)S(1)} %get-tuple-element.21.keep_ref), channel_id=1, source_target_pairs={{0,1},{2,3},{4,5},{6,7},{8,9},{10,11},{12,13},{14,15},{16,17},{18,... | collective-permute-start | bytes 3145736 | tf_op jit(solution)/shard_map/ppermute | solution.py:330
  48.6 0.8 collective-permute-done.refs_1_.recv_ref
  49.4 0.6 chip.1
  50.1 1.3 %collective-permute-start.2 = (f32[2,128,256]{2,1,0:T(8,128)S(1)}, f32[2,128,256]{2,1,0:T(8,128)S(1)}, u32[]{:S(2)}, u32[]{:S(2)}) collective-permute-start(f32[2,128,256]{2,1,0:T(8,128)S(1)} %get-tuple-element.23), channel_id=1, source_target_pairs={{0,2},{1,3},{2,0},{3,1},{4,6},{5,7},{6,4},{7,5},{8,10},{9,11},{10,... | collective-permute-start | bytes 786440 | tf_op jit(solution)/shard_map/ppermute | solution.py:330
  51.3 1.2 %collective-permute-start.3 = (f32[2,128,256]{2,1,0:T(8,128)S(1)}, f32[2,128,256]{2,1,0:T(8,128)S(1)}, u32[]{:S(2)}, u32[]{:S(2)}) collective-permute-start(f32[2,128,256]{2,1,0:T(8,128)S(1)} %get-tuple-element.24), channel_id=1, source_target_pairs={{0,4},{1,5},{2,6},{3,7},{4,0},{5,1},{6,2},{7,3},{8,12},{9,13},{10,... | collective-permute-start | bytes 786440 | tf_op jit(solution)/shard_map/ppermute | solution.py:330
  52.6 0.2 collective-permute-start.4
  52.8 4.8 %collective-permute-done.2.r1 = f32[2,128,256]{2,1,0:T(8,128)S(1)} collective-permute-done((f32[2,128,256]{2,1,0:T(8,128)S(1)}, f32[2,128,256]{2,1,0:T(8,128)S(1)}, u32[]{:S(2)}, u32[]{:S(2)}) %collective-permute-start.2) | collective-permute-done | bytes 262176 | tf_op jit(solution)/shard_map/ppermute | solution.py:330
  57.6 0.9 collective-permute-done.3.r2
  58.5 5.7 %collective-permute-done.4.r3 = f32[2,128,256]{2,1,0:T(8,128)S(1)} collective-permute-done((f32[2,128,256]{2,1,0:T(8,128)S(1)}, f32[2,128,256]{2,1,0:T(8,128)S(1)}, u32[]{:S(2)}, u32[]{:S(2)}) %collective-permute-start.4) | collective-permute-done | bytes 262176 | tf_op jit(solution)/shard_map/ppermute | solution.py:330
  64.2 0.9 group.1
  65.2 1.3 %collective-permute-start.5 = (f32[2,128,128]{2,1,0:T(8,128)S(1)}, f32[2,128,128]{2,1,0:T(8,128)S(1)}, u32[]{:S(2)}, u32[]{:S(2)}) collective-permute-start(f32[2,128,128]{2,1,0:T(8,128)S(1)} %get-tuple-element.28.add_ref), channel_id=1, source_target_pairs={{0,8},{1,9},{2,10},{3,11},{4,12},{5,13},{6,14},{7,15},{8,16},{9,17... | collective-permute-start | bytes 393224 | tf_op jit(solution)/shard_map/ppermute | solution.py:330
  66.5 4.4 %collective-permute-done.5.state_ref = f32[2,128,128]{2,1,0:T(8,128)S(1)} collective-permute-done((f32[2,128,128]{2,1,0:T(8,128)S(1)}, f32[2,128,128]{2,1,0:T(8,128)S(1)}, u32[]{:S(2)}, u32[]{:S(2)}) %collective-permute-start.5) | collective-permute-done | bytes 131104 | tf_op jit(solution)/shard_map/ppermute | solution.py:330
  70.9 0.2 step.1
  71.1 1.3 %collective-permute-start.6 = (f32[2,128,128]{2,1,0:T(8,128)S(1)}, f32[2,128,128]{2,1,0:T(8,128)S(1)}, u32[]{:S(2)}, u32[]{:S(2)}) collective-permute-start(f32[2,128,128]{2,1,0:T(8,128)S(1)} %step.1), channel_id=1, source_target_pairs={{0,8},{1,9},{2,10},{3,11},{4,12},{5,13},{6,14},{7,15},{8,16},{9,17... | collective-permute-start | bytes 393224 | tf_op jit(solution)/shard_map/ppermute | solution.py:330
  72.4 4.4 %collective-permute-done.6.state_ref = f32[2,128,128]{2,1,0:T(8,128)S(1)} collective-permute-done((f32[2,128,128]{2,1,0:T(8,128)S(1)}, f32[2,128,128]{2,1,0:T(8,128)S(1)}, u32[]{:S(2)}, u32[]{:S(2)}) %collective-permute-start.6) | collective-permute-done | bytes 131104 | tf_op jit(solution)/shard_map/ppermute | solution.py:330
  76.8 0.3 spread.1
  77.2 1.2 %collective-permute-start.7 = (f32[2,128,128]{2,1,0:T(8,128)S(1)}, f32[2,128,128]{2,1,0:T(8,128)S(1)}, u32[]{:S(2)}, u32[]{:S(2)}) collective-permute-start(f32[2,128,128]{2,1,0:T(8,128)S(1)} %get-tuple-element.30), channel_id=1, source_target_pairs={{0,2},{1,3},{2,0},{3,1},{4,6},{5,7},{6,4},{7,5},{8,10},{9,11},{10,... | collective-permute-start | bytes 393224 | tf_op jit(solution)/shard_map/ppermute | solution.py:330
  78.4 0.3 collective-permute-start.8
  78.7 1.2 %collective-permute-start.9 = (f32[2,128,128]{2,1,0:T(8,128)S(1)}, f32[2,128,128]{2,1,0:T(8,128)S(1)}, u32[]{:S(2)}, u32[]{:S(2)}) collective-permute-start(f32[2,128,128]{2,1,0:T(8,128)S(1)} %get-tuple-element.32), channel_id=1, source_target_pairs={{0,6},{1,7},{2,4},{3,5},{4,2},{5,3},{6,0},{7,1},{8,14},{9,15},{10,... | collective-permute-start | bytes 393224 | tf_op jit(solution)/shard_map/ppermute | solution.py:330
  79.9 4.6 %collective-permute-start.10 = (f32[2,128,128]{2,1,0:T(8,128)S(1)}, f32[2,128,128]{2,1,0:T(8,128)S(1)}, u32[]{:S(2)}, u32[]{:S(2)}) collective-permute-start(f32[2,128,128]{2,1,0:T(8,128)S(1)} %get-tuple-element.29.refs_0_), channel_id=1, source_target_pairs={{0,1},{1,0},{2,3},{3,2},{4,5},{5,4},{6,7},{7,6},{8,9},{9,8},{10,11... | collective-permute-start | bytes 393224 | tf_op jit(solution)/shard_map/ppermute | solution.py:330
  84.5 1.5 %collective-permute-start.11 = (f32[2,128,128]{2,1,0:T(8,128)S(1)}, f32[2,128,128]{2,1,0:T(8,128)S(1)}, u32[]{:S(2)}, u32[]{:S(2)}) collective-permute-start(f32[2,128,128]{2,1,0:T(8,128)S(1)} %collective-permute-done.7.refs_1_), channel_id=1, source_target_pairs={{0,1},{1,0},{2,3},{3,2},{4,5},{5,4},{6,7},{7,6},{8,9},{9,8},{10,11... | collective-permute-start | bytes 393224 | tf_op jit(solution)/shard_map/ppermute | solution.py:330
  85.9 1.2 %collective-permute-start.12 = (f32[2,128,128]{2,1,0:T(8,128)S(1)}, f32[2,128,128]{2,1,0:T(8,128)S(1)}, u32[]{:S(2)}, u32[]{:S(2)}) collective-permute-start(f32[2,128,128]{2,1,0:T(8,128)S(1)} %collective-permute-done.8.refs_2_), channel_id=1, source_target_pairs={{0,1},{1,0},{2,3},{3,2},{4,5},{5,4},{6,7},{7,6},{8,9},{9,8},{10,11... | collective-permute-start | bytes 393224 | tf_op jit(solution)/shard_map/ppermute | solution.py:330
  87.2 1.7 %collective-permute-start.13 = (f32[2,128,128]{2,1,0:T(8,128)S(1)}, f32[2,128,128]{2,1,0:T(8,128)S(1)}, u32[]{:S(2)}, u32[]{:S(2)}) collective-permute-start(f32[2,128,128]{2,1,0:T(8,128)S(1)} %collective-permute-done.9.refs_3_), channel_id=1, source_target_pairs={{0,1},{1,0},{2,3},{3,2},{4,5},{5,4},{6,7},{7,6},{8,9},{9,8},{10,11... | collective-permute-start | bytes 393224 | tf_op jit(solution)/shard_map/ppermute | solution.py:330
  89.0 12.1 %readout.1.read_ref = f32[16,128,256]{2,1,0:T(8,128)S(1)} custom-call(s32[8]{0:T(128)S(1)} %copy-done.10, bf16[128,1024]{1,0:T(8,128)(2,1)S(1)} %copy-done.2, bf16[128,1024]{1,0:T(8,128)(2,1)S(1)} %copy-done.4, bf16[128,2048]{1,0:T(8,128)(2,1)S(1)} %copy-done.1, f32[16,128]{1,0:T(8,128)S(1)} %copy-done.6, f32[16,128]{1,0:T(8,128)S(1)} %copy-done.8, ...), custom_call_target="tpu_custom_call" | custom-call | flops 872415232 | bytes 6307872 | tf_op jit(solution)/shard_map/readout/pallas_call | solution.py:289
  101.2 1.6 %output.1 = bf16[128,2048]{1,0:T(8,128)(2,1)} custom-call(f32[1,128]{1,0:T(1,128)S(1)} %bitcast.1, f32[16,128,256]{2,1,0:T(8,128)S(1)} %readout.1.read_ref, f32[2,128,128]{2,1,0:T(8,128)S(1)} %get-tuple-element.29.refs_0_, f32[2,128,128]{2,1,0:T(8,128)S(1)} %collective-permute-done.7.refs_1_, f32[2,128,128]{2,1,0:T(8,128)S(1)} %collective-permute-done.8.refs_2_, ...), custom_call_target="tpu_custom_call" | custom-call | flops 201326592 | bytes 3670528 | tf_op jit(solution)/shard_map/output/pallas_call | solution.py:289
  (27 shorter events, 0.1 us)
Async XLA Ops:
  0.0 1.0 %copy-start = (bf16[128,2048]{1,0:T(8,128)(2,1)S(1)}, bf16[128,2048]{1,0:T(8,128)(2,1)}, u32[]{:S(2)}) copy-start(bf16[128,2048]{1,0:T(8,128)(2,1)} %v_ref.3) | copy-start | bytes 1572868
  1.0 0.9 copy-start.3
  2.0 0.7 copy-start.5
  2.7 0.7 copy-start.7
  3.4 0.7 copy-start.9
  46.4 3.0 %collective-permute-start = (f32[4,2,128,256]{3,2,1,0:T(8,128)S(1)}, f32[4,2,128,256]{3,2,1,0:T(8,128)S(1)}, u32[]{:S(2)}, u32[]{:S(2)}) collective-permute-start(f32[4,2,128,256]{3,2,1,0:T(8,128)S(1)} %get-tuple-element.20), channel_id=1, source_target_pairs={{0,1},{1,0},{2,3},{3,2},{4,5},{5,4},{6,7},{7,6},{8,9},{9,8},{10,11... | collective-permute-start | bytes 3145736 | tf_op jit(solution)/shard_map/ppermute | solution.py:330
  47.1 41.8 %copy-start.1 = (bf16[128,2048]{1,0:T(8,128)(2,1)S(1)}, bf16[128,2048]{1,0:T(8,128)(2,1)}, u32[]{:S(2)}) copy-start(bf16[128,2048]{1,0:T(8,128)(2,1)} %v_ref.3) | copy-start | bytes 1572868
  47.1 41.8 %copy-start.2 = (bf16[128,1024]{1,0:T(8,128)(2,1)S(1)}, bf16[128,1024]{1,0:T(8,128)(2,1)}, u32[]{:S(2)}) copy-start(bf16[128,1024]{1,0:T(8,128)(2,1)} %q_ref.1) | copy-start | bytes 786436
  47.1 41.8 %copy-start.4 = (bf16[128,1024]{1,0:T(8,128)(2,1)S(1)}, bf16[128,1024]{1,0:T(8,128)(2,1)}, u32[]{:S(2)}) copy-start(bf16[128,1024]{1,0:T(8,128)(2,1)} %k_ref.3) | copy-start | bytes 786436
  47.1 41.8 %copy-start.6 = (f32[16,128]{1,0:T(8,128)S(1)}, f32[16,128]{1,0:T(8,128)}, u32[]{:S(2)}) copy-start(f32[16,128]{1,0:T(8,128)} %decay_ref.3) | copy-start | bytes 24580
  47.2 41.8 %copy-start.8 = (f32[16,128]{1,0:T(8,128)S(1)}, f32[16,128]{1,0:T(8,128)}, u32[]{:S(2)}) copy-start(f32[16,128]{1,0:T(8,128)} %rate_ref.3) | copy-start | bytes 24580
  47.2 41.8 %copy-start.10 = (s32[8]{0:T(128)S(1)}, s32[8]{0:T(128)}, u32[]{:S(2)}) copy-start(s32[8]{0:T(128)} %lengths_ref.3) | copy-start | bytes 100
  47.2 41.7 %collective-permute-start.1 = (f32[4,2,128,256]{3,2,1,0:T(8,128)S(1)}, f32[4,2,128,256]{3,2,1,0:T(8,128)S(1)}, u32[]{:S(2)}, u32[]{:S(2)}) collective-permute-start(f32[4,2,128,256]{3,2,1,0:T(8,128)S(1)} %get-tuple-element.21.keep_ref), channel_id=1, source_target_pairs={{0,1},{2,3},{4,5},{6,7},{8,9},{10,11},{12,13},{14,15},{16,17},{18,... | collective-permute-start | bytes 3145736 | tf_op jit(solution)/shard_map/ppermute | solution.py:330
  50.1 7.6 %collective-permute-start.2 = (f32[2,128,256]{2,1,0:T(8,128)S(1)}, f32[2,128,256]{2,1,0:T(8,128)S(1)}, u32[]{:S(2)}, u32[]{:S(2)}) collective-permute-start(f32[2,128,256]{2,1,0:T(8,128)S(1)} %get-tuple-element.23), channel_id=1, source_target_pairs={{0,2},{1,3},{2,0},{3,1},{4,6},{5,7},{6,4},{7,5},{8,10},{9,11},{10,... | collective-permute-start | bytes 786440 | tf_op jit(solution)/shard_map/ppermute | solution.py:330
  51.3 7.2 %collective-permute-start.3 = (f32[2,128,256]{2,1,0:T(8,128)S(1)}, f32[2,128,256]{2,1,0:T(8,128)S(1)}, u32[]{:S(2)}, u32[]{:S(2)}) collective-permute-start(f32[2,128,256]{2,1,0:T(8,128)S(1)} %get-tuple-element.24), channel_id=1, source_target_pairs={{0,4},{1,5},{2,6},{3,7},{4,0},{5,1},{6,2},{7,3},{8,12},{9,13},{10,... | collective-permute-start | bytes 786440 | tf_op jit(solution)/shard_map/ppermute | solution.py:330
  52.6 11.7 %collective-permute-start.4 = (f32[2,128,256]{2,1,0:T(8,128)S(1)}, f32[2,128,256]{2,1,0:T(8,128)S(1)}, u32[]{:S(2)}, u32[]{:S(2)}) collective-permute-start(f32[2,128,256]{2,1,0:T(8,128)S(1)} %get-tuple-element.25), channel_id=1, source_target_pairs={{0,6},{1,7},{2,4},{3,5},{4,2},{5,3},{6,0},{7,1},{8,14},{9,15},{10,... | collective-permute-start | bytes 786440 | tf_op jit(solution)/shard_map/ppermute | solution.py:330
  65.2 5.7 %collective-permute-start.5 = (f32[2,128,128]{2,1,0:T(8,128)S(1)}, f32[2,128,128]{2,1,0:T(8,128)S(1)}, u32[]{:S(2)}, u32[]{:S(2)}) collective-permute-start(f32[2,128,128]{2,1,0:T(8,128)S(1)} %get-tuple-element.28.add_ref), channel_id=1, source_target_pairs={{0,8},{1,9},{2,10},{3,11},{4,12},{5,13},{6,14},{7,15},{8,16},{9,17... | collective-permute-start | bytes 393224 | tf_op jit(solution)/shard_map/ppermute | solution.py:330
  71.1 5.7 %collective-permute-start.6 = (f32[2,128,128]{2,1,0:T(8,128)S(1)}, f32[2,128,128]{2,1,0:T(8,128)S(1)}, u32[]{:S(2)}, u32[]{:S(2)}) collective-permute-start(f32[2,128,128]{2,1,0:T(8,128)S(1)} %step.1), channel_id=1, source_target_pairs={{0,8},{1,9},{2,10},{3,11},{4,12},{5,13},{6,14},{7,15},{8,16},{9,17... | collective-permute-start | bytes 393224 | tf_op jit(solution)/shard_map/ppermute | solution.py:330
  77.2 7.3 %collective-permute-start.7 = (f32[2,128,128]{2,1,0:T(8,128)S(1)}, f32[2,128,128]{2,1,0:T(8,128)S(1)}, u32[]{:S(2)}, u32[]{:S(2)}) collective-permute-start(f32[2,128,128]{2,1,0:T(8,128)S(1)} %get-tuple-element.30), channel_id=1, source_target_pairs={{0,2},{1,3},{2,0},{3,1},{4,6},{5,7},{6,4},{7,5},{8,10},{9,11},{10,... | collective-permute-start | bytes 393224 | tf_op jit(solution)/shard_map/ppermute | solution.py:330
  78.4 7.6 %collective-permute-start.8 = (f32[2,128,128]{2,1,0:T(8,128)S(1)}, f32[2,128,128]{2,1,0:T(8,128)S(1)}, u32[]{:S(2)}, u32[]{:S(2)}) collective-permute-start(f32[2,128,128]{2,1,0:T(8,128)S(1)} %get-tuple-element.31), channel_id=1, source_target_pairs={{0,4},{1,5},{2,6},{3,7},{4,0},{5,1},{6,2},{7,3},{8,12},{9,13},{10,... | collective-permute-start | bytes 393224 | tf_op jit(solution)/shard_map/ppermute | solution.py:330
  78.7 8.5 %collective-permute-start.9 = (f32[2,128,128]{2,1,0:T(8,128)S(1)}, f32[2,128,128]{2,1,0:T(8,128)S(1)}, u32[]{:S(2)}, u32[]{:S(2)}) collective-permute-start(f32[2,128,128]{2,1,0:T(8,128)S(1)} %get-tuple-element.32), channel_id=1, source_target_pairs={{0,6},{1,7},{2,4},{3,5},{4,2},{5,3},{6,0},{7,1},{8,14},{9,15},{10,... | collective-permute-start | bytes 393224 | tf_op jit(solution)/shard_map/ppermute | solution.py:330
  79.9 21.2 %collective-permute-start.10 = (f32[2,128,128]{2,1,0:T(8,128)S(1)}, f32[2,128,128]{2,1,0:T(8,128)S(1)}, u32[]{:S(2)}, u32[]{:S(2)}) collective-permute-start(f32[2,128,128]{2,1,0:T(8,128)S(1)} %get-tuple-element.29.refs_0_), channel_id=1, source_target_pairs={{0,1},{1,0},{2,3},{3,2},{4,5},{5,4},{6,7},{7,6},{8,9},{9,8},{10,11... | collective-permute-start | bytes 393224 | tf_op jit(solution)/shard_map/ppermute | solution.py:330
  84.5 16.6 %collective-permute-start.11 = (f32[2,128,128]{2,1,0:T(8,128)S(1)}, f32[2,128,128]{2,1,0:T(8,128)S(1)}, u32[]{:S(2)}, u32[]{:S(2)}) collective-permute-start(f32[2,128,128]{2,1,0:T(8,128)S(1)} %collective-permute-done.7.refs_1_), channel_id=1, source_target_pairs={{0,1},{1,0},{2,3},{3,2},{4,5},{5,4},{6,7},{7,6},{8,9},{9,8},{10,11... | collective-permute-start | bytes 393224 | tf_op jit(solution)/shard_map/ppermute | solution.py:330
  85.9 15.2 %collective-permute-start.12 = (f32[2,128,128]{2,1,0:T(8,128)S(1)}, f32[2,128,128]{2,1,0:T(8,128)S(1)}, u32[]{:S(2)}, u32[]{:S(2)}) collective-permute-start(f32[2,128,128]{2,1,0:T(8,128)S(1)} %collective-permute-done.8.refs_2_), channel_id=1, source_target_pairs={{0,1},{1,0},{2,3},{3,2},{4,5},{5,4},{6,7},{7,6},{8,9},{9,8},{10,11... | collective-permute-start | bytes 393224 | tf_op jit(solution)/shard_map/ppermute | solution.py:330
  87.2 14.0 %collective-permute-start.13 = (f32[2,128,128]{2,1,0:T(8,128)S(1)}, f32[2,128,128]{2,1,0:T(8,128)S(1)}, u32[]{:S(2)}, u32[]{:S(2)}) collective-permute-start(f32[2,128,128]{2,1,0:T(8,128)S(1)} %collective-permute-done.9.refs_3_), channel_id=1, source_target_pairs={{0,1},{1,0},{2,3},{3,2},{4,5},{5,4},{6,7},{7,6},{8,9},{9,8},{10,11... | collective-permute-start | bytes 393224 | tf_op jit(solution)/shard_map/ppermute | solution.py:330
  89.0 12.2 %copy-start.11 = (f32[128]{0:T(128)S(1)}, f32[128]{0:T(128)}, u32[]{:S(2)}) copy-start(f32[128]{0:T(128)} %param.13) | copy-start | bytes 1540
where the time goes:
time: 103 us
  Pallas kernels  58.2 us (57%)
  waiting for transfers between devices  21.1 us (20%)
  starting transfers between devices  19.2 us (19%)
  local copies, waits for them, and re-layouts  4.07 us (4%)
    pallas_call x7, Pallas kernels, call(): pl.pallas_call(kernel, out_shape=outs, in_specs=[VMEM] * len(args) if spe...  58.2 us
    ppermute x14, waiting for transfers between devices, permute(): return lax.ppermute(x, AXES, pairs)  21.1 us
    ppermute x14, starting transfers between devices, permute(): return lax.ppermute(x, AXES, pairs)  19.2 us
    unnamed x24, local copies, waits for them, and re-layouts  4.07 us
  transfers between devices with their start and end apart: 14, of which 6 were waited for; matrix products, arithmetic and copies ran while one was open for 0% of the time, Pallas kernels for 14%

commit v1 on v0

--- a/solution.py
+++ b/solution.py
@@ -20,6 +20,7 @@
 f32 = jnp.float32
 bf16 = jnp.bfloat16
 VMEM = pl.BlockSpec(memory_space=pltpu.VMEM)
+ANY = pl.BlockSpec(memory_space=pl.ANY)
 SMEM = pl.BlockSpec(memory_space=pltpu.SMEM)
 
 
@@ -46,15 +47,30 @@
     return high, (x - high.astype(f32)).astype(bf16)
 
 
+def left(x):
+    return jnp.concatenate(split(x), axis=1)
+
+
+def right(x):
+    wide = jnp.concatenate(split(x), axis=1)
+    return jnp.concatenate([wide, wide], axis=0)
+
+
+def fold(x):
+    half = x.shape[1] // 2
+    return x[:, :half] + x[:, half:]
+
+
 def mm3(a, b):
-    a_high, a_low = split(a)
-    b_high, b_low = split(b)
-    return mm(a_high, b_high) + (mm(a_high, b_low) + mm(a_low, b_high))
+    return fold(mm(left(a), right(b)))
 
 
 def mm2(a, b):
-    a_high, a_low = split(a)
-    return mm(a_high, b) + mm(a_low, b)
+    return mm(left(a), twice(b))
+
+
+def twice(x):
+    return jnp.concatenate([x, x], axis=0)
 
 
 def compose(later, early):
@@ -108,9 +124,87 @@
     return col, row
 
 
+def fetch(pairs, sems):
+    copies = [pltpu.make_async_copy(a, b, sems.at[i]) for i, (a, b) in enumerate(pairs)]
+    for copy in copies:
+        copy.start()
+    for copy in copies:
+        copy.wait()
+
+
+def odd_rows(x, size):
+    return jnp.concatenate([x[i : i + size] for i in range(size, BLOCK, 2 * size)], axis=0)
+
+
+def with_odd_rows(x, rows, size):
+    pieces = []
+    for i in range(0, BLOCK // 2, size):
+        pieces += [x[2 * i : 2 * i + size], rows[i : i + size]]
+    return jnp.concatenate(pieces, axis=0)
+
+
+def invert(systems, apart):
+    eye = (apart == 0).astype(f32)
+    near = apart < 16
+    powers = [jnp.where(near, n, 0.0) for n in systems]
+    solved = [eye - n for n in powers]
+    powers = [mm3(n, n) for n in powers]
+    for last in (False, False, True):
+        rights = [right(n) for n in powers]
+        if last:
+            solved = [s + fold(mm(left(s), r)) for s, r in zip(solved, rights)]
+        else:
+            both = [
+                fold(mm(left(jnp.concatenate([n, s], axis=0)), r))
+                for n, s, r in zip(powers, solved, rights)
+            ]
+            powers = [x[:BLOCK] for x in both]
+            solved = [s + x[BLOCK:] for s, x in zip(solved, both)]
+    size = 16
+    while size < BLOCK:
+        band = odd_rows((apart >= size) & (apart < 2 * size), size)
+        corners = [jnp.where(band, odd_rows(n, size), 0.0) for n in systems]
+        products = [mm3(c, s) for c, s in zip(corners, solved)]
+        zero = jnp.zeros((BLOCK, BLOCK), f32)
+        fulls = [with_odd_rows(zero, p, size) for p in products]
+        rows = [odd_rows(s, size) for s in solved]
+        rows = [r - mm3(r, u) for r, u in zip(rows, fulls)]
+        solved = [with_odd_rows(s, r, size) for s, r in zip(solved, rows)]
+        size = 2 * size
+    return solved
+
+
 def maps_kernel(
-    parts, n_sub, lengths_ref, k_ref, v_ref, decay_ref, rate_ref, keep_ref, send_ref, inverse_ref
+    parts,
+    n_sub,
+    lengths_hbm,
+    k_hbm,
+    v_hbm,
+    decay_hbm,
+    rate_hbm,
+    keep_ref,
+    send_ref,
+    inverse_ref,
+    lengths_ref,
+    k_ref,
+    v_ref,
+    decay_ref,
+    rate_ref,
+    middle,
+    weights,
+    wholes,
+    sems,
 ):
+    fetch(
+        (
+            (lengths_hbm, lengths_ref),
+            (k_hbm, k_ref),
+            (decay_hbm, decay_ref),
+            (rate_hbm, rate_ref),
+            (v_hbm, v_ref),
+        ),
+        sems,
+    )
     core = lax.rem(my_rank(n_sub), 2)
     seg_row, seg_col, before = token_masks(lengths_ref, n_sub)
     sum_row, sum_col, rate_row, rate_col = gates(decay_ref, rate_ref)
@@ -121,44 +215,47 @@
     last = seg_row[:, BLOCK - 1 :]
     ends_col = (seg_col == last).astype(f32)
 
-    for core_of in range(2):
-        for chip in range(CHIPS):
-            j = 4 * core_of + chip
+    n = len(parts)
+    batch = 4
+    for j0 in range(0, HK, batch // n):
+        systems, ends = [], []
+        for j in range(j0, j0 + batch // n):
             key = k_ref[:, j * D : (j + 1) * D]
             key_t = key.T
             n_col, n_row = key_norms(key, key_t)
             gram = mm(key, key_t) * n_row
             for place, part in enumerate(parts):
-                h = head_of(core_of, chip, part)
+                h = 2 * j + part
                 s_row, s_col = sum_row[h : h + 1, :], sum_col[:, h : h + 1]
                 b_row, b_col = rate_row[h : h + 1, :], rate_col[:, h : h + 1]
                 between = jnp.exp(jnp.minimum(s_col - s_row, 0.0))
-                system = jnp.where(strict, between * gram * (b_col * n_col), 0.0)
-                solved = eye - jnp.where(apart == 1, system, 0.0)
-                size = 2
-                while size < BLOCK:
-                    corner = jnp.where((apart >= size) & (apart < 2 * size), system, 0.0)
-                    solved = solved - mm3(solved, mm3(corner, solved))
-                    size = 2 * size
-                inverse_ref[h // 2, place] = solved
+                systems.append(jnp.where(strict, between * gram * (b_col * n_col), 0.0))
                 from_row = jnp.exp(s_row) * reaches
-                to_end = jnp.exp(s_col[BLOCK - 1 :, :] - s_col) * ends_col
-                value = v_ref[:, h * D : (h + 1) * D]
-                fresh = mm2(solved * b_row, value)
-                wy = mm2(solved * (b_row * from_row * n_row), key)
-                scaled = jnp.concatenate([wy, fresh], axis=1) * (to_end * n_col)
-                high, low = split(scaled)
-                both = mm(key_t, high) + mm(key_t, low)
-                whole = from_row[:, BLOCK - 1 :]
-                pair = jnp.concatenate([whole * eye - both[:, :D], both[:, D:]], axis=1)
-
-                @pl.when(core == core_of)
-                def _():
-                    keep_ref[chip, place] = pair
-
-                @pl.when(core != core_of)
-                def _():
-                    send_ref[chip, place] = pair
+                ends.append(jnp.exp(s_col[BLOCK - 1 :, :] - s_col) * ends_col * n_col)
+                weights[n * j + place, 0:1] = b_row * from_row * n_row
+                weights[n * j + place, 1:2] = b_row
+                wholes[n * j + place] = from_row[:, BLOCK - 1 :] * eye
+        solved = invert(systems, apart)
+        for i, (inverse, end) in enumerate(zip(solved, ends)):
+            inverse_ref[j0 + i // n, i % n] = inverse
+            middle[n * j0 + i] = inverse * end
+
+    for out_ref, core_of in ((send_ref, 1 - core), (keep_ref, core)):
+        for chip in range(CHIPS):
+            j = CHIPS * core_of + chip
+            key = k_ref[:, pl.ds(pl.multiple_of(j * D, D), D)]
+            key_t = key.T
+            keys, key_ts = twice(key), jnp.concatenate([key_t, key_t], axis=1)
+            for place, part in enumerate(parts):
+                at = n * j + place
+                mid = middle[at]
+                value = v_ref[:, pl.ds(pl.multiple_of((2 * j + part) * D, D), D)]
+                wy = mm(left(mid * weights[at, 0:1]), keys)
+                fresh = mm(left(mid * weights[at, 1:2]), twice(value))
+                high, low = split(jnp.concatenate([wy, fresh], axis=1))
+                both = mm(key_ts, jnp.concatenate([high, low], axis=0))
+                out_ref[chip, place, :, :D] = wholes[at] - both[:, :D]
+                out_ref[chip, place, :, D:] = both[:, D:]
 
 
 def chip_kernel(n_sub, keep_ref, recv_ref, *out_refs):
@@ -174,7 +271,7 @@
             out_refs[slot][place] = compose(late, early)
 
 
-def group_kernel(n_sub, r0, r1, r2, r3, total_map_ref, total_add_ref, ahead_ref, held):
+def group_kernel(n_sub, r0, r1, r2, r3, after_ref, total_map_ref, total_add_ref, ahead_ref, held):
     rank = my_rank(n_sub)
     chip = lax.rem(rank // 2, CHIPS)
     for slot, ref in enumerate((r0, r1, r2, r3)):
@@ -253,15 +350,17 @@
             fresh = mm2(mixed * b_row, v_ref[:, h * D : (h + 1) * D])
             through = wide * (from_col * q_col) - mm2(mixed * (b_row * from_row * n_row), key)
 
-            @pl.when(core == 0)
-            def _():
-                read_ref[h] = jnp.concatenate([through, fresh], axis=1)
-
-            @pl.when(core == 1)
-            def _():
-                source = recv_refs[phase] if j >= 4 else extra_refs[phase]
-                both = mm3(through, source[j % 4, place])
-                read_ref[h] = jnp.concatenate([both[:, :D], both[:, D:] + fresh], axis=1)
+            read_ref[h] = jnp.concatenate([through, fresh], axis=1)
+
+    @pl.when(core == 1)
+    def _():
+        for h in range(VALUE_HEADS):
+            phase, place = (h % 2) // per_phase, (h % 2) % per_phase
+            source = recv_refs[phase] if h >= 8 else extra_refs[phase]
+            read = read_ref[h]
+            both = mm3(read[:, :D], source[(h // 2) % CHIPS, place])
+            read_ref[h, :, :D] = both[:, :D]
+            read_ref[h, :, D:] = both[:, D:] + read[:, D:]
 
 
 def output_kernel(n_sub, n_phases, gain_ref, read_ref, *refs):
@@ -283,7 +382,7 @@
                     out_ref[:, pl.ds(at, D)] = (raw * scale * gain).astype(bf16)
 
 
-def call(kernel, outs, args, scratch=(), specs=None, flops=0, name=None):
+def call(kernel, outs, args, scratch=(), specs=None, flops=0, name=None, vmem=32):
     moved = sum(a.size * a.dtype.itemsize for a in args)
     moved += sum(o.size * o.dtype.itemsize for o in jax.tree.leaves(outs))
     return pl.pallas_call(
@@ -292,7 +391,7 @@
         in_specs=[VMEM] * len(args) if specs is None else specs,
         out_specs=jax.tree.map(lambda o: VMEM, outs),
         scratch_shapes=list(scratch),
-        compiler_params=pltpu.CompilerParams(vmem_limit_bytes=32 * 2**20),
+        compiler_params=pltpu.CompilerParams(vmem_limit_bytes=vmem * 2**20),
         cost_estimate=pl.CostEstimate(flops=flops, bytes_accessed=moved, transcendentals=0),
         name=name,
     )(*args)
@@ -336,9 +435,21 @@
             functools.partial(maps_kernel, parts, n_sub),
             (like(CHIPS, n, D, 2 * D), like(CHIPS, n, D, 2 * D), like(HK, n, BLOCK, BLOCK)),
             (passage_lengths, key_vectors, values, log_decay, write_rate),
-            specs=[SMEM, VMEM, VMEM, VMEM, VMEM],
+            scratch=(
+                pltpu.SMEM(passage_lengths.shape, jnp.int32),
+                pltpu.VMEM(key_vectors.shape, bf16),
+                pltpu.VMEM(values.shape, bf16),
+                pltpu.VMEM(log_decay.shape, f32),
+                pltpu.VMEM(write_rate.shape, f32),
+                pltpu.VMEM((HK * n, BLOCK, BLOCK), f32),
+                pltpu.VMEM((HK * n, 8, BLOCK), f32),
+                pltpu.VMEM((HK * n, D, D), f32),
+                pltpu.SemaphoreType.DMA((5,)),
+            ),
+            specs=[ANY] * 5,
             flops=8 * n * 44 * step,
             name="maps",
+            vmem=60,
         )
         recv = permute(send, swap_pairs)
         extra = permute(keep, up_pairs)
@@ -353,10 +464,29 @@
             name="chip",
         )
         got = [slots[0]] + [permute(slots[s], chip_pairs(s)) for s in range(1, CHIPS)]
+        read = call(
+            functools.partial(readout_kernel, n_sub, n_phases),
+            like(VALUE_HEADS, BLOCK, 2 * D),
+            (
+                passage_lengths,
+                queries,
+                key_vectors,
+                values,
+                log_decay,
+                write_rate,
+                *inverses,
+                *recvs,
+                *extras,
+            ),
+            specs=[SMEM] + [VMEM] * (5 + 3 * n_phases),
+            flops=16 * 13 * step,
+            name="readout",
+        )
         total_map, total_add, ahead = call(
             functools.partial(group_kernel, n_sub),
             (like(n, D, D), like(n, D, D), like(n, 3, D, 2 * D)),
-            got,
+            (*got, read),
+            specs=[VMEM] * CHIPS + [ANY],
             scratch=(pltpu.VMEM((CHIPS, n, D, 2 * D), f32),),
             flops=n * 24 * step,
             name="group",
@@ -383,24 +513,6 @@
         own = [outs[0]] + [permute(outs[s], chip_pairs(s)) for s in range(1, CHIPS)]
         states += own + [permute(x, swap_pairs) for x in own]
 
-    read = call(
-        functools.partial(readout_kernel, n_sub, n_phases),
-        like(VALUE_HEADS, BLOCK, 2 * D),
-        (
-            passage_lengths,
-            queries,
-            key_vectors,
-            values,
-            log_decay,
-            write_rate,
-            *inverses,
-            *recvs,
-            *extras,
-        ),
-        specs=[SMEM] + [VMEM] * (5 + 3 * n_phases),
-        flops=16 * 13 * step,
-        name="readout",
-    )
     return call(
         functools.partial(output_kernel, n_sub, n_phases),
         jax.ShapeDtypeStruct((BLOCK, VALUE_HEADS * D), bf16),

time: 103 us -> 60.6 us (0.59)
  Pallas kernels: 58.2 us -> 22.9 us
  waiting for transfers between devices: 21.1 us -> 16.7 us
  local copies, waits for them, and re-layouts: 4.07 us -> 1.26 us
    pallas_call x7, Pallas kernels: 58.2 us -> 22.9 us  [call(): pl.pallas_call(kernel, out_shape=outs, in_specs=[VMEM] * len(args) if spe...]
    ppermute x14, waiting for transfers between devices: 21.1 us -> 16.7 us  [permute(): return lax.ppermute(x, AXES, pairs)]
    unnamed x24 -> x18, local copies, waits for them, and re-layouts: 4.07 us -> 1.26 us
  transfers between devices with their start and end apart: 14 -> 14, of which waited for: 6 -> 5; matrix products, arithmetic and copies ran while one was open for 0% -> 0% of each run, Pallas kernels for 14% -> 10%
where the time goes in v1:
time: 60.6 us; the launch traced here: 60.1 us
  Pallas kernels  22.9 us (38%)
  starting transfers between devices  19 us (31%)
  waiting for transfers between devices  16.7 us (28%)
  local copies, waits for them, and re-layouts  1.26 us (2%)
    pallas_call x7, Pallas kernels, call(): pl.pallas_call(kernel, out_shape=outs, in_specs=[VMEM] * len(args) if spe...  22.9 us
    ppermute x14, starting transfers between devices, permute(): return lax.ppermute(x, AXES, pairs)  19 us
    ppermute x14, waiting for transfers between devices, permute(): return lax.ppermute(x, AXES, pairs)  16.7 us
    unnamed x18, local copies, waits for them, and re-layouts  1.26 us
  transfers between devices with their start and end apart: 14, of which 5 were waited for; matrix products, arithmetic and copies ran while one was open for 0% of the time, Pallas kernels for 10%

profile of v1, /device:TPU:25, one launch (start us, length us, event | category | flops | bytes accessed | tf_op | source)
XLA Modules:
  0.0 60.1 jit_solution(11830322312033865901)
XLA Ops:
  0.0 13.8 %maps.1 = (f32[4,2,128,256]{3,2,1,0:T(8,128)}, f32[4,2,128,256]{3,2,1,0:T(8,128)}, f32[8,2,128,128]{3,2,1,0:T(8,128)}) custom-call(s32[8]{0:T(128)} %lengths_ref.1, bf16[128,1024]{1,0:T(8,128)(2,1)} %k_ref.1, bf16[128,2048]{1,0:T(8,128)(2,1)} %v_ref.1, f32[16,128]{1,0:T(8,128)} %decay_ref.1, f32[16,128]{1,0:T(8,128)} %rate_ref.1), custom_call_target="tpu_custom_call" | custom-call | flops 2952790016 | bytes 3948576 | tf_op jit(solution)/shard_map/maps/pallas_call | solution.py:388
  13.8 0.7 %collective-permute-start = (f32[4,2,128,256]{3,2,1,0:T(8,128)}, f32[4,2,128,256]{3,2,1,0:T(8,128)S(1)}, u32[]{:S(2)}, u32[]{:S(2)}) collective-permute-start(f32[4,2,128,256]{3,2,1,0:T(8,128)} %get-tuple-element.20), channel_id=1, source_target_pairs={{0,1},{1,0},{2,3},{3,2},{4,5},{5,4},{6,7},{7,6},{8,9},{9,8},{10,11... | collective-permute-start | bytes 3145736 | tf_op jit(solution)/shard_map/ppermute | solution.py:429
  14.6 1.3 %collective-permute-start.1 = (f32[4,2,128,256]{3,2,1,0:T(8,128)}, f32[4,2,128,256]{3,2,1,0:T(8,128)S(1)}, u32[]{:S(2)}, u32[]{:S(2)}) collective-permute-start(f32[4,2,128,256]{3,2,1,0:T(8,128)} %get-tuple-element.21.keep_ref), channel_id=1, source_target_pairs={{0,1},{2,3},{4,5},{6,7},{8,9},{10,11},{12,13},{14,15},{16,17},{18,... | collective-permute-start | bytes 3145736 | tf_op jit(solution)/shard_map/ppermute | solution.py:429
  15.9 1.2 %collective-permute-done.refs_1_.recv_ref = f32[4,2,128,256]{3,2,1,0:T(8,128)S(1)} collective-permute-done((f32[4,2,128,256]{3,2,1,0:T(8,128)}, f32[4,2,128,256]{3,2,1,0:T(8,128)S(1)}, u32[]{:S(2)}, u32[]{:S(2)}) %collective-permute-start) | collective-permute-done | bytes 1048608 | tf_op jit(solution)/shard_map/ppermute | solution.py:429
  17.1 1.2 %copy-done.1 = f32[4,2,128,256]{3,2,1,0:T(8,128)S(1)} copy-done((f32[4,2,128,256]{3,2,1,0:T(8,128)S(1)}, f32[4,2,128,256]{3,2,1,0:T(8,128)}, u32[]{:S(2)}) %copy-start.1) | copy-done | bytes 1048600
  18.3 0.5 chip.1
  18.8 1.3 %collective-permute-start.2 = (f32[2,128,256]{2,1,0:T(8,128)S(1)}, f32[2,128,256]{2,1,0:T(8,128)S(1)}, u32[]{:S(2)}, u32[]{:S(2)}) collective-permute-start(f32[2,128,256]{2,1,0:T(8,128)S(1)} %get-tuple-element.23), channel_id=1, source_target_pairs={{0,2},{1,3},{2,0},{3,1},{4,6},{5,7},{6,4},{7,5},{8,10},{9,11},{10,... | collective-permute-start | bytes 786440 | tf_op jit(solution)/shard_map/ppermute | solution.py:429
  20.1 1.2 %collective-permute-start.3 = (f32[2,128,256]{2,1,0:T(8,128)S(1)}, f32[2,128,256]{2,1,0:T(8,128)S(1)}, u32[]{:S(2)}, u32[]{:S(2)}) collective-permute-start(f32[2,128,256]{2,1,0:T(8,128)S(1)} %get-tuple-element.24), channel_id=1, source_target_pairs={{0,4},{1,5},{2,6},{3,7},{4,0},{5,1},{6,2},{7,3},{8,12},{9,13},{10,... | collective-permute-start | bytes 786440 | tf_op jit(solution)/shard_map/ppermute | solution.py:429
  21.3 0.2 collective-permute-start.4
  21.5 0.0 collective-permute-done.1.refs_2_
  21.6 5.7 %readout.1.after_ref.read_ref = f32[16,128,256]{2,1,0:T(8,128)S(1)} custom-call(s32[8]{0:T(128)S(1)} %copy-done.7, bf16[128,1024]{1,0:T(8,128)(2,1)S(1)} %copy-done.3, bf16[128,1024]{1,0:T(8,128)(2,1)S(1)} %copy-done.4, bf16[128,2048]{1,0:T(8,128)(2,1)S(1)} %copy-done.2, f32[16,128]{1,0:T(8,128)S(1)} %copy-done.5, f32[16,128]{1,0:T(8,128)S(1)} %copy-done.6, ...), custom_call_target="tpu_custom_call" | custom-call | flops 872415232 | bytes 6307872 | tf_op jit(solution)/shard_map/readout/pallas_call | solution.py:388
  27.3 0.0 collective-permute-done.2.r1
  27.3 0.0 collective-permute-done.3.r2
  27.3 5.7 %collective-permute-done.4.r3 = f32[2,128,256]{2,1,0:T(8,128)S(1)} collective-permute-done((f32[2,128,256]{2,1,0:T(8,128)S(1)}, f32[2,128,256]{2,1,0:T(8,128)S(1)}, u32[]{:S(2)}, u32[]{:S(2)}) %collective-permute-start.4) | collective-permute-done | bytes 262176 | tf_op jit(solution)/shard_map/ppermute | solution.py:429
  33.0 0.8 %group.1 = (f32[2,128,128]{2,1,0:T(8,128)S(1)}, f32[2,128,128]{2,1,0:T(8,128)S(1)}, f32[2,3,128,256]{3,2,1,0:T(8,128)S(1)}) custom-call(f32[2,128,256]{2,1,0:T(8,128)S(1)} %get-tuple-element.22.r0, f32[2,128,256]{2,1,0:T(8,128)S(1)} %collective-permute-done.2.r1, f32[2,128,256]{2,1,0:T(8,128)S(1)} %collective-permute-done.3.r2, ...), custom_call_target="tpu_custom_call" | custom-call | flops 201326592 | bytes 4194304 | tf_op jit(solution)/shard_map/group/pallas_call | solution.py:388
  33.9 1.3 %collective-permute-start.5 = (f32[2,128,128]{2,1,0:T(8,128)S(1)}, f32[2,128,128]{2,1,0:T(8,128)S(1)}, u32[]{:S(2)}, u32[]{:S(2)}) collective-permute-start(f32[2,128,128]{2,1,0:T(8,128)S(1)} %get-tuple-element.28.add_ref), channel_id=1, source_target_pairs={{0,8},{1,9},{2,10},{3,11},{4,12},{5,13},{6,14},{7,15},{8,16},{9,17... | collective-permute-start | bytes 393224 | tf_op jit(solution)/shard_map/ppermute | solution.py:429
  35.2 4.4 %collective-permute-done.5.state_ref = f32[2,128,128]{2,1,0:T(8,128)S(1)} collective-permute-done((f32[2,128,128]{2,1,0:T(8,128)S(1)}, f32[2,128,128]{2,1,0:T(8,128)S(1)}, u32[]{:S(2)}, u32[]{:S(2)}) %collective-permute-start.5) | collective-permute-done | bytes 131104 | tf_op jit(solution)/shard_map/ppermute | solution.py:429
  39.6 0.2 step.1
  39.8 1.3 %collective-permute-start.6 = (f32[2,128,128]{2,1,0:T(8,128)S(1)}, f32[2,128,128]{2,1,0:T(8,128)S(1)}, u32[]{:S(2)}, u32[]{:S(2)}) collective-permute-start(f32[2,128,128]{2,1,0:T(8,128)S(1)} %step.1), channel_id=1, source_target_pairs={{0,8},{1,9},{2,10},{3,11},{4,12},{5,13},{6,14},{7,15},{8,16},{9,17... | collective-permute-start | bytes 393224 | tf_op jit(solution)/shard_map/ppermute | solution.py:429
  41.1 4.4 %collective-permute-done.6.state_ref = f32[2,128,128]{2,1,0:T(8,128)S(1)} collective-permute-done((f32[2,128,128]{2,1,0:T(8,128)S(1)}, f32[2,128,128]{2,1,0:T(8,128)S(1)}, u32[]{:S(2)}, u32[]{:S(2)}) %collective-permute-start.6) | collective-permute-done | bytes 131104 | tf_op jit(solution)/shard_map/ppermute | solution.py:429
  45.5 0.3 spread.1
  45.9 1.2 %collective-permute-start.7 = (f32[2,128,128]{2,1,0:T(8,128)S(1)}, f32[2,128,128]{2,1,0:T(8,128)S(1)}, u32[]{:S(2)}, u32[]{:S(2)}) collective-permute-start(f32[2,128,128]{2,1,0:T(8,128)S(1)} %get-tuple-element.30), channel_id=1, source_target_pairs={{0,2},{1,3},{2,0},{3,1},{4,6},{5,7},{6,4},{7,5},{8,10},{9,11},{10,... | collective-permute-start | bytes 393224 | tf_op jit(solution)/shard_map/ppermute | solution.py:429
  47.1 0.3 collective-permute-start.8
  47.4 1.2 %collective-permute-start.9 = (f32[2,128,128]{2,1,0:T(8,128)S(1)}, f32[2,128,128]{2,1,0:T(8,128)S(1)}, u32[]{:S(2)}, u32[]{:S(2)}) collective-permute-start(f32[2,128,128]{2,1,0:T(8,128)S(1)} %get-tuple-element.32), channel_id=1, source_target_pairs={{0,6},{1,7},{2,4},{3,5},{4,2},{5,3},{6,0},{7,1},{8,14},{9,15},{10,... | collective-permute-start | bytes 393224 | tf_op jit(solution)/shard_map/ppermute | solution.py:429
  48.6 4.5 %collective-permute-start.10 = (f32[2,128,128]{2,1,0:T(8,128)S(1)}, f32[2,128,128]{2,1,0:T(8,128)S(1)}, u32[]{:S(2)}, u32[]{:S(2)}) collective-permute-start(f32[2,128,128]{2,1,0:T(8,128)S(1)} %get-tuple-element.29.refs_0_), channel_id=1, source_target_pairs={{0,1},{1,0},{2,3},{3,2},{4,5},{5,4},{6,7},{7,6},{8,9},{9,8},{10,11... | collective-permute-start | bytes 393224 | tf_op jit(solution)/shard_map/ppermute | solution.py:429
  53.1 0.0 collective-permute-done.7.refs_1_
  53.1 1.5 %collective-permute-start.11 = (f32[2,128,128]{2,1,0:T(8,128)S(1)}, f32[2,128,128]{2,1,0:T(8,128)S(1)}, u32[]{:S(2)}, u32[]{:S(2)}) collective-permute-start(f32[2,128,128]{2,1,0:T(8,128)S(1)} %collective-permute-done.7.refs_1_), channel_id=1, source_target_pairs={{0,1},{1,0},{2,3},{3,2},{4,5},{5,4},{6,7},{7,6},{8,9},{9,8},{10,11... | collective-permute-start | bytes 393224 | tf_op jit(solution)/shard_map/ppermute | solution.py:429
  54.6 1.2 %collective-permute-start.12 = (f32[2,128,128]{2,1,0:T(8,128)S(1)}, f32[2,128,128]{2,1,0:T(8,128)S(1)}, u32[]{:S(2)}, u32[]{:S(2)}) collective-permute-start(f32[2,128,128]{2,1,0:T(8,128)S(1)} %collective-permute-done.8.refs_2_), channel_id=1, source_target_pairs={{0,1},{1,0},{2,3},{3,2},{4,5},{5,4},{6,7},{7,6},{8,9},{9,8},{10,11... | collective-permute-start | bytes 393224 | tf_op jit(solution)/shard_map/ppermute | solution.py:429
  55.8 0.0 collective-permute-done.9.refs_3_
  55.8 1.7 %collective-permute-start.13 = (f32[2,128,128]{2,1,0:T(8,128)S(1)}, f32[2,128,128]{2,1,0:T(8,128)S(1)}, u32[]{:S(2)}, u32[]{:S(2)}) collective-permute-start(f32[2,128,128]{2,1,0:T(8,128)S(1)} %collective-permute-done.9.refs_3_), channel_id=1, source_target_pairs={{0,1},{1,0},{2,3},{3,2},{4,5},{5,4},{6,7},{7,6},{8,9},{9,8},{10,11... | collective-permute-start | bytes 393224 | tf_op jit(solution)/shard_map/ppermute | solution.py:429
  57.6 1.0 %collective-permute-done.13.refs_7_ = f32[2,128,128]{2,1,0:T(8,128)S(1)} collective-permute-done((f32[2,128,128]{2,1,0:T(8,128)S(1)}, f32[2,128,128]{2,1,0:T(8,128)S(1)}, u32[]{:S(2)}, u32[]{:S(2)}) %collective-permute-start.13) | collective-permute-done | bytes 131104 | tf_op jit(solution)/shard_map/ppermute | solution.py:429
  58.6 1.5 %output.1 = bf16[128,2048]{1,0:T(8,128)(2,1)} custom-call(f32[1,128]{1,0:T(1,128)S(1)} %bitcast.1, f32[16,128,256]{2,1,0:T(8,128)S(1)} %readout.1.after_ref.read_ref, f32[2,128,128]{2,1,0:T(8,128)S(1)} %get-tuple-element.29.refs_0_, f32[2,128,128]{2,1,0:T(8,128)S(1)} %collective-permute-done.7.refs_1_, f32[2,128,128]{2,1,0:T(8,128)S(1)} %collective-permute-done.8.refs_2_, ...), custom_call_target="tpu_custom_call" | custom-call | flops 201326592 | bytes 3670528 | tf_op jit(solution)/shard_map/output/pallas_call | solution.py:388
  (21 shorter events, 0.0 us)
Async XLA Ops:
  0.0 21.5 %copy-start.2 = (bf16[128,2048]{1,0:T(8,128)(2,1)S(1)}, bf16[128,2048]{1,0:T(8,128)(2,1)}, u32[]{:S(2)}) copy-start(bf16[128,2048]{1,0:T(8,128)(2,1)} %v_ref.1) | copy-start | bytes 1572868
  0.0 21.5 %copy-start.3 = (bf16[128,1024]{1,0:T(8,128)(2,1)S(1)}, bf16[128,1024]{1,0:T(8,128)(2,1)}, u32[]{:S(2)}) copy-start(bf16[128,1024]{1,0:T(8,128)(2,1)} %q_ref.1) | copy-start | bytes 786436
  0.0 21.5 %copy-start.4 = (bf16[128,1024]{1,0:T(8,128)(2,1)S(1)}, bf16[128,1024]{1,0:T(8,128)(2,1)}, u32[]{:S(2)}) copy-start(bf16[128,1024]{1,0:T(8,128)(2,1)} %k_ref.1) | copy-start | bytes 786436
  0.0 21.6 %copy-start.5 = (f32[16,128]{1,0:T(8,128)S(1)}, f32[16,128]{1,0:T(8,128)}, u32[]{:S(2)}) copy-start(f32[16,128]{1,0:T(8,128)} %decay_ref.1) | copy-start | bytes 24580
  0.0 21.6 %copy-start.6 = (f32[16,128]{1,0:T(8,128)S(1)}, f32[16,128]{1,0:T(8,128)}, u32[]{:S(2)}) copy-start(f32[16,128]{1,0:T(8,128)} %rate_ref.1) | copy-start | bytes 24580
  0.0 21.6 %copy-start.7 = (s32[8]{0:T(128)S(1)}, s32[8]{0:T(128)}, u32[]{:S(2)}) copy-start(s32[8]{0:T(128)} %lengths_ref.1) | copy-start | bytes 100
  13.8 7.8 %copy-start = (f32[8,2,128,128]{3,2,1,0:T(8,128)S(1)}, f32[8,2,128,128]{3,2,1,0:T(8,128)}, u32[]{:S(2)}) copy-start(f32[8,2,128,128]{3,2,1,0:T(8,128)} %get-tuple-element.19.refs_0_) | copy-start | bytes 3145732
  13.8 3.2 %collective-permute-start = (f32[4,2,128,256]{3,2,1,0:T(8,128)}, f32[4,2,128,256]{3,2,1,0:T(8,128)S(1)}, u32[]{:S(2)}, u32[]{:S(2)}) collective-permute-start(f32[4,2,128,256]{3,2,1,0:T(8,128)} %get-tuple-element.20), channel_id=1, source_target_pairs={{0,1},{1,0},{2,3},{3,2},{4,5},{5,4},{6,7},{7,6},{8,9},{9,8},{10,11... | collective-permute-start | bytes 3145736 | tf_op jit(solution)/shard_map/ppermute | solution.py:429
  14.6 7.0 %collective-permute-start.1 = (f32[4,2,128,256]{3,2,1,0:T(8,128)}, f32[4,2,128,256]{3,2,1,0:T(8,128)S(1)}, u32[]{:S(2)}, u32[]{:S(2)}) collective-permute-start(f32[4,2,128,256]{3,2,1,0:T(8,128)} %get-tuple-element.21.keep_ref), channel_id=1, source_target_pairs={{0,1},{2,3},{4,5},{6,7},{8,9},{10,11},{12,13},{14,15},{16,17},{18,... | collective-permute-start | bytes 3145736 | tf_op jit(solution)/shard_map/ppermute | solution.py:429
  17.1 1.2 %copy-start.1 = (f32[4,2,128,256]{3,2,1,0:T(8,128)S(1)}, f32[4,2,128,256]{3,2,1,0:T(8,128)}, u32[]{:S(2)}) copy-start(f32[4,2,128,256]{3,2,1,0:T(8,128)} %get-tuple-element.21.keep_ref) | copy-start | bytes 3145732
  18.8 8.5 %collective-permute-start.2 = (f32[2,128,256]{2,1,0:T(8,128)S(1)}, f32[2,128,256]{2,1,0:T(8,128)S(1)}, u32[]{:S(2)}, u32[]{:S(2)}) collective-permute-start(f32[2,128,256]{2,1,0:T(8,128)S(1)} %get-tuple-element.23), channel_id=1, source_target_pairs={{0,2},{1,3},{2,0},{3,1},{4,6},{5,7},{6,4},{7,5},{8,10},{9,11},{10,... | collective-permute-start | bytes 786440 | tf_op jit(solution)/shard_map/ppermute | solution.py:429
  20.1 7.2 %collective-permute-start.3 = (f32[2,128,256]{2,1,0:T(8,128)S(1)}, f32[2,128,256]{2,1,0:T(8,128)S(1)}, u32[]{:S(2)}, u32[]{:S(2)}) collective-permute-start(f32[2,128,256]{2,1,0:T(8,128)S(1)} %get-tuple-element.24), channel_id=1, source_target_pairs={{0,4},{1,5},{2,6},{3,7},{4,0},{5,1},{6,2},{7,3},{8,12},{9,13},{10,... | collective-permute-start | bytes 786440 | tf_op jit(solution)/shard_map/ppermute | solution.py:429
  21.3 11.7 %collective-permute-start.4 = (f32[2,128,256]{2,1,0:T(8,128)S(1)}, f32[2,128,256]{2,1,0:T(8,128)S(1)}, u32[]{:S(2)}, u32[]{:S(2)}) collective-permute-start(f32[2,128,256]{2,1,0:T(8,128)S(1)} %get-tuple-element.25), channel_id=1, source_target_pairs={{0,6},{1,7},{2,4},{3,5},{4,2},{5,3},{6,0},{7,1},{8,14},{9,15},{10,... | collective-permute-start | bytes 786440 | tf_op jit(solution)/shard_map/ppermute | solution.py:429
  33.0 25.5 %copy-start.8 = (f32[128]{0:T(128)S(1)}, f32[128]{0:T(128)}, u32[]{:S(2)}) copy-start(f32[128]{0:T(128)} %param.13) | copy-start | bytes 1540
  33.9 5.7 %collective-permute-start.5 = (f32[2,128,128]{2,1,0:T(8,128)S(1)}, f32[2,128,128]{2,1,0:T(8,128)S(1)}, u32[]{:S(2)}, u32[]{:S(2)}) collective-permute-start(f32[2,128,128]{2,1,0:T(8,128)S(1)} %get-tuple-element.28.add_ref), channel_id=1, source_target_pairs={{0,8},{1,9},{2,10},{3,11},{4,12},{5,13},{6,14},{7,15},{8,16},{9,17... | collective-permute-start | bytes 393224 | tf_op jit(solution)/shard_map/ppermute | solution.py:429
  39.8 5.7 %collective-permute-start.6 = (f32[2,128,128]{2,1,0:T(8,128)S(1)}, f32[2,128,128]{2,1,0:T(8,128)S(1)}, u32[]{:S(2)}, u32[]{:S(2)}) collective-permute-start(f32[2,128,128]{2,1,0:T(8,128)S(1)} %step.1), channel_id=1, source_target_pairs={{0,8},{1,9},{2,10},{3,11},{4,12},{5,13},{6,14},{7,15},{8,16},{9,17... | collective-permute-start | bytes 393224 | tf_op jit(solution)/shard_map/ppermute | solution.py:429
  45.9 7.3 %collective-permute-start.7 = (f32[2,128,128]{2,1,0:T(8,128)S(1)}, f32[2,128,128]{2,1,0:T(8,128)S(1)}, u32[]{:S(2)}, u32[]{:S(2)}) collective-permute-start(f32[2,128,128]{2,1,0:T(8,128)S(1)} %get-tuple-element.30), channel_id=1, source_target_pairs={{0,2},{1,3},{2,0},{3,1},{4,6},{5,7},{6,4},{7,5},{8,10},{9,11},{10,... | collective-permute-start | bytes 393224 | tf_op jit(solution)/shard_map/ppermute | solution.py:429
  47.1 7.5 %collective-permute-start.8 = (f32[2,128,128]{2,1,0:T(8,128)S(1)}, f32[2,128,128]{2,1,0:T(8,128)S(1)}, u32[]{:S(2)}, u32[]{:S(2)}) collective-permute-start(f32[2,128,128]{2,1,0:T(8,128)S(1)} %get-tuple-element.31), channel_id=1, source_target_pairs={{0,4},{1,5},{2,6},{3,7},{4,0},{5,1},{6,2},{7,3},{8,12},{9,13},{10,... | collective-permute-start | bytes 393224 | tf_op jit(solution)/shard_map/ppermute | solution.py:429
  47.4 8.5 %collective-permute-start.9 = (f32[2,128,128]{2,1,0:T(8,128)S(1)}, f32[2,128,128]{2,1,0:T(8,128)S(1)}, u32[]{:S(2)}, u32[]{:S(2)}) collective-permute-start(f32[2,128,128]{2,1,0:T(8,128)S(1)} %get-tuple-element.32), channel_id=1, source_target_pairs={{0,6},{1,7},{2,4},{3,5},{4,2},{5,3},{6,0},{7,1},{8,14},{9,15},{10,... | collective-permute-start | bytes 393224 | tf_op jit(solution)/shard_map/ppermute | solution.py:429
  48.6 9.0 %collective-permute-start.10 = (f32[2,128,128]{2,1,0:T(8,128)S(1)}, f32[2,128,128]{2,1,0:T(8,128)S(1)}, u32[]{:S(2)}, u32[]{:S(2)}) collective-permute-start(f32[2,128,128]{2,1,0:T(8,128)S(1)} %get-tuple-element.29.refs_0_), channel_id=1, source_target_pairs={{0,1},{1,0},{2,3},{3,2},{4,5},{5,4},{6,7},{7,6},{8,9},{9,8},{10,11... | collective-permute-start | bytes 393224 | tf_op jit(solution)/shard_map/ppermute | solution.py:429
  53.1 4.5 %collective-permute-start.11 = (f32[2,128,128]{2,1,0:T(8,128)S(1)}, f32[2,128,128]{2,1,0:T(8,128)S(1)}, u32[]{:S(2)}, u32[]{:S(2)}) collective-permute-start(f32[2,128,128]{2,1,0:T(8,128)S(1)} %collective-permute-done.7.refs_1_), channel_id=1, source_target_pairs={{0,1},{1,0},{2,3},{3,2},{4,5},{5,4},{6,7},{7,6},{8,9},{9,8},{10,11... | collective-permute-start | bytes 393224 | tf_op jit(solution)/shard_map/ppermute | solution.py:429
  54.6 3.0 %collective-permute-start.12 = (f32[2,128,128]{2,1,0:T(8,128)S(1)}, f32[2,128,128]{2,1,0:T(8,128)S(1)}, u32[]{:S(2)}, u32[]{:S(2)}) collective-permute-start(f32[2,128,128]{2,1,0:T(8,128)S(1)} %collective-permute-done.8.refs_2_), channel_id=1, source_target_pairs={{0,1},{1,0},{2,3},{3,2},{4,5},{5,4},{6,7},{7,6},{8,9},{9,8},{10,11... | collective-permute-start | bytes 393224 | tf_op jit(solution)/shard_map/ppermute | solution.py:429
  55.8 2.7 %collective-permute-start.13 = (f32[2,128,128]{2,1,0:T(8,128)S(1)}, f32[2,128,128]{2,1,0:T(8,128)S(1)}, u32[]{:S(2)}, u32[]{:S(2)}) collective-permute-start(f32[2,128,128]{2,1,0:T(8,128)S(1)} %collective-permute-done.9.refs_3_), channel_id=1, source_target_pairs={{0,1},{1,0},{2,3},{3,2},{4,5},{5,4},{6,7},{7,6},{8,9},{9,8},{10,11... | collective-permute-start | bytes 393224 | tf_op jit(solution)/shard_map/ppermute | solution.py:429

commit v2 on v0

v2 whole, which is shorter than its diff:
```python
import functools
import math

import jax
import jax.numpy as jnp
from jax import lax
from jax.experimental import pallas as pl
from jax.experimental.pallas import tpu as pltpu
from jax.sharding import PartitionSpec as P

D = 128
VALUE_HEADS = 16
HK = 8
BLOCK = 128
AXES = ("seq", "sub")
CHIPS = 4
GROUP = 2 * CHIPS
SIDES = (0, 1)
PHASES = ((0, 1, 2, 3),)
BATCH = 8
LONGEST = {4096: 2048, 65536: 8192}

f32 = jnp.float32
bf16 = jnp.bfloat16
VMEM = pl.BlockSpec(memory_space=pltpu.VMEM)
ANY = pl.BlockSpec(memory_space=pl.ANY)
HBM = pl.BlockSpec(memory_space=pltpu.HBM)
SMEM = pl.BlockSpec(memory_space=pltpu.SMEM)


def my_rank(n_sub):
    return lax.axis_index("seq") * n_sub + lax.axis_index("sub")


def mm(a, b):
    return lax.dot_general(a, b, (((1,), (0,)), ((), ())), preferred_element_type=f32)


def mm_nt(a, b, precision=None):
    return lax.dot_general(
        a, b, (((1,), (1,)), ((), ())), preferred_element_type=f32, precision=precision
    )


def split(x):
    high = x.astype(bf16)
    return high, (x - high.astype(f32)).astype(bf16)


def left(x):
    return jnp.concatenate(split(x), axis=1)


def right(x):
    wide = jnp.concatenate(split(x), axis=1)
    return jnp.concatenate([wide, wide], axis=0)


def fold(x):
    half = x.shape[1] // 2
    return x[:, :half] + x[:, half:]


def mm3(a, b):
    return fold(mm(left(a), right(b)))


def mm2(a, b):
    return mm(left(a), twice(b))


def twice(x):
    return jnp.concatenate([x, x], axis=0)


def compose(later, early):
    both = mm3(later[:, :D], early)
    return jnp.concatenate([both[:, :D], both[:, D:] + later[:, D:]], axis=1)


def iota(axis):
    return lax.broadcasted_iota(jnp.int32, (BLOCK, BLOCK), axis)


def token_masks(lengths_ref, n_sub):
    first = my_rank(n_sub) * BLOCK
    row_at = first + lax.broadcasted_iota(jnp.int32, (1, BLOCK), 1)
    col_at = first + lax.broadcasted_iota(jnp.int32, (BLOCK, 1), 0)

    def one(i, carried):
        start, row, col, before = carried
        row = row + (row_at >= start).astype(jnp.int32)
        col = col + (col_at >= start).astype(jnp.int32)
        before = before + (first > start).astype(jnp.int32)
        return start + lengths_ref[i], row, col, before

    zero = jnp.int32(0)
    _, row, col, before = lax.fori_loop(
        0,
        lengths_ref.shape[0],
        one,
        (zero, jnp.zeros((1, BLOCK), jnp.int32), jnp.zeros((BLOCK, 1), jnp.int32), zero),
    )
    return row, col, before


def gates(heads, decay_ref, rate_ref):
    decay = jnp.concatenate([decay_ref[pl.ds(h, 1), :] for h in heads], axis=0)
    rate_row = jnp.concatenate([rate_ref[pl.ds(h, 1), :] for h in heads], axis=0)
    lower = (iota(0) >= iota(1)).astype(f32)
    eye = (iota(0) == iota(1)).astype(f32)
    highest = lax.Precision.HIGHEST
    sum_row = mm_nt(decay, lower, highest)
    sum_col = mm_nt(lower, decay, highest)
    rate_col = mm_nt(eye, rate_row, highest)
    return sum_row, sum_col, rate_row, rate_col


def columns(ref, at):
    return ref[:, pl.ds(pl.multiple_of(at * D, D), D)]


def key_heads(n_sub, slots):
    rank = my_rank(n_sub)
    core, chip = lax.rem(rank, 2), lax.rem(rank // 2, CHIPS)
    return [CHIPS * (core ^ side) + (chip ^ slot) for side in SIDES for slot in slots]


def value_heads(keys):
    return [2 * j + part for j in keys for part in range(2)]


def key_norms(key, key_t):
    wide = key.astype(f32)
    col = lax.rsqrt(jnp.sum(wide * wide, axis=1, keepdims=True) + 1e-06)
    wide_t = key_t.astype(f32)
    row = lax.rsqrt(jnp.sum(wide_t * wide_t, axis=0, keepdims=True) + 1e-06)
    return col, row


def fetch(pairs, sems):
    copies = [pltpu.make_async_copy(a, b, sems.at[i]) for i, (a, b) in enumerate(pairs)]
    for copy in copies:
        copy.start()
    for copy in copies:
        copy.wait()


def odd_rows(x, size):
    return jnp.concatenate([x[i : i + size] for i in range(size, BLOCK, 2 * size)], axis=0)


def with_odd_rows(x, rows, size):
    pieces = []
    for i in range(0, BLOCK // 2, size):
        pieces += [x[2 * i : 2 * i + size], rows[i : i + size]]
    return jnp.concatenate(pieces, axis=0)


def invert(systems, apart):
    eye = (apart == 0).astype(f32)
    near = apart < 16
    powers = [jnp.where(near, n, 0.0) for n in systems]
    solved = [eye - n for n in powers]
    powers = [mm3(n, n) for n in powers]
    for last in (False, False, True):
        rights = [right(n) for n in powers]
        if last:
            solved = [s + fold(mm(left(s), r)) for s, r in zip(solved, rights)]
        else:
            both = [
                fold(mm(left(jnp.concatenate([n, s], axis=0)), r))
                for n, s, r in zip(powers, solved, rights)
            ]
            powers = [x[:BLOCK] for x in both]
            solved = [s + x[BLOCK:] for s, x in zip(solved, both)]
    size = 16
    while size < BLOCK:
        band = odd_rows((apart >= size) & (apart < 2 * size), size)
        corners = [jnp.where(band, odd_rows(n, size), 0.0) for n in systems]
        products = [mm3(c, s) for c, s in zip(corners, solved)]
        zero = jnp.zeros((BLOCK, BLOCK), f32)
        fulls = [with_odd_rows(zero, p, size) for p in products]
        rows = [odd_rows(s, size) for s in solved]
        rows = [r - mm3(r, u) for r, u in zip(rows, fulls)]
        solved = [with_odd_rows(s, r, size) for s, r in zip(solved, rows)]
        size = 2 * size
    return solved


def maps_kernel(slots, n_sub, *refs):
    if len(refs) == 9:
        keep_ref, send_ref, inverse_ref = refs[6:]
    else:
        keep_ref, send_ref, inverse_ref = refs[5:8]
        fetch(list(zip(refs[:5], refs[8:13])), refs[13])
        refs = refs[8:]
    lengths_ref, k_ref, v_ref, decay_ref, rate_ref = refs[:5]
    keys = key_heads(n_sub, slots)
    heads = value_heads(keys)
    seg_row, seg_col, before = token_masks(lengths_ref, n_sub)
    sum_row, sum_col, rate_row, rate_col = gates(heads, decay_ref, rate_ref)
    apart = iota(0) ^ iota(1)
    strict = (iota(0) > iota(1)) & (seg_row == seg_col)
    eye = (apart == 0).astype(f32)
    reaches = (seg_row == before).astype(f32)
    last = seg_row[:, BLOCK - 1 :]
    ends_col = (seg_col == last).astype(f32)

    for j0 in range(0, len(keys), BATCH // 2):
        systems, details = [], []
        for j in range(j0, j0 + BATCH // 2):
            key = columns(k_ref, keys[j])
            key_t = key.T
            n_col, n_row = key_norms(key, key_t)
            gram = mm(key, key_t) * n_row
            for part in range(2):
                i = 2 * j + part
                s_row, s_col = sum_row[i : i + 1, :], sum_col[:, i : i + 1]
                b_row, b_col = rate_row[i : i + 1, :], rate_col[:, i : i + 1]
                between = jnp.exp(jnp.minimum(s_col - s_row, 0.0))
                systems.append(jnp.where(strict, between * gram * (b_col * n_col), 0.0))
                from_row = jnp.exp(s_row) * reaches
                end = jnp.exp(s_col[BLOCK - 1 :, :] - s_col) * ends_col * n_col
                details.append((i, key, key_t, n_row, b_row, from_row, end))
        solved = invert(systems, apart)
        for inverse, (i, key, key_t, n_row, b_row, from_row, end) in zip(solved, details):
            inverse_ref[i] = inverse
            middle = inverse * end
            wy = mm(left(middle * (b_row * from_row * n_row)), twice(key))
            fresh = mm(left(middle * b_row), twice(columns(v_ref, heads[i])))
            high, low = split(jnp.concatenate([wy, fresh], axis=1))
            key_ts = jnp.concatenate([key_t, key_t], axis=1)
            both = mm(key_ts, jnp.concatenate([high, low], axis=0))
            out_ref = keep_ref if i < len(heads) // 2 else send_ref
            at = i % (len(heads) // 2)
            out_ref[at, :, :D] = from_row[:, BLOCK - 1 :] * eye - both[:, :D]
            out_ref[at, :, D:] = both[:, D:]


def chip_kernel(n_sub, keep_ref, recv_ref, *out_refs):
    first = lax.rem(my_rank(n_sub), 2) == 0
    for i in range(keep_ref.shape[0]):
        mine, theirs = keep_ref[i], recv_ref[i]
        early = jnp.where(first, mine, theirs)
        late = jnp.where(first, theirs, mine)
        out_refs[i // 2][i % 2] = compose(late, early)


def group_kernel(n_sub, r0, r1, r2, r3, after_ref, total_map_ref, total_add_ref, ahead_ref, held):
    rank = my_rank(n_sub)
    chip = lax.rem(rank // 2, CHIPS)
    for slot, ref in enumerate((r0, r1, r2, r3)):
        held[chip ^ slot] = ref[...]
    for place in range(r0.shape[0]):
        one = held[0, place]
        two = compose(held[1, place], one)
        upper = compose(held[3, place], held[2, place])
        total = compose(upper, two)
        total_map_ref[place] = total[:, :D]
        total_add_ref[place] = total[:, D:]
        ahead_ref[place, 0] = one
        ahead_ref[place, 1] = two
        ahead_ref[place, 2] = compose(held[2, place], two)


def step_kernel(map_ref, add_ref, state_ref, out_ref):
    for place in range(map_ref.shape[0]):
        out_ref[place] = add_ref[place] + mm3(map_ref[place], state_ref[place])


def spread_kernel(n_sub, ahead_ref, state_ref, o0, o1, o2, o3, held):
    rank = my_rank(n_sub)
    chip = lax.rem(rank // 2, CHIPS)
    for place in range(state_ref.shape[0]):
        state = state_ref[place]
        held[0, place] = state
        for i in range(CHIPS - 1):
            held[i + 1, place] = (
                mm3(ahead_ref[place, i, :, :D], state) + ahead_ref[place, i, :, D:]
            )
    for slot, ref in enumerate((o0, o1, o2, o3)):
        ref[...] = held[chip ^ slot]


def readout_kernel(n_sub, lengths_ref, q_ref, k_ref, v_ref, decay_ref, rate_ref, *refs):
    n = len(PHASES)
    read_refs = refs[3 * n :]
    core = lax.rem(my_rank(n_sub), 2)
    seg_row, seg_col, before = token_masks(lengths_ref, n_sub)
    lower = (iota(0) >= iota(1)) & (seg_row == seg_col)
    reaches_row = (seg_row == before).astype(f32)
    reaches_col = (seg_col == before).astype(f32)
    for phase, slots in enumerate(PHASES):
        keys = key_heads(n_sub, slots)
        heads = value_heads(keys)
        sum_row, sum_col, rate_row, _ = gates(heads, decay_ref, rate_ref)
        for j in range(len(keys)):
            key = columns(k_ref, keys[j])
            key_t = key.T
            n_col, n_row = key_norms(key, key_t)
            query = columns(q_ref, keys[j])
            wide = query.astype(f32)
            q_col = lax.rsqrt(jnp.sum(wide * wide, axis=1, keepdims=True) + 1e-06)
            cross = mm(query, key_t) * n_row
            for part in range(2):
                i = 2 * j + part
                s_row, s_col = sum_row[i : i + 1, :], sum_col[:, i : i + 1]
                b_row = rate_row[i : i + 1, :]
                between = jnp.exp(jnp.minimum(s_col - s_row, 0.0))
                scores = jnp.where(lower, between * cross * q_col, 0.0)
                mixed = mm3(scores, refs[phase][i])
                from_row = jnp.exp(s_row) * reaches_row
                from_col = jnp.exp(s_col) * reaches_col
                fresh = mm2(mixed * b_row, columns(v_ref, heads[i]))
                through = wide * (from_col * q_col) - mm2(mixed * (b_row * from_row * n_row), key)
                read_refs[phase][i] = jnp.concatenate([through, fresh], axis=1)

    @pl.when(core == 1)
    def _():
        for phase in range(n):
            read_ref = read_refs[phase]
            half = read_ref.shape[0] // 2
            for i in range(2 * half):
                source = refs[n + phase] if i < half else refs[2 * n + phase]
                read = read_ref[i]
                both = mm3(read[:, :D], source[i % half])
                read_ref[i, :, :D] = both[:, :D]
                read_ref[i, :, D:] = both[:, D:] + read[:, D:]


def output_kernel(n_sub, gain_ref, *refs):
    read_refs, states, out_ref = refs[: len(PHASES)], refs[len(PHASES) : -1], refs[-1]
    gain = gain_ref[...]
    for phase, slots in enumerate(PHASES):
        heads = value_heads(key_heads(n_sub, slots))
        for i, h in enumerate(heads):
            side, place = divmod(i, 2 * len(slots))
            state = states[side * CHIPS + slots[place // 2]][place % 2]
            read = read_refs[phase][i]
            raw = mm3(read[:, :D], state) + read[:, D:]
            scale = lax.rsqrt(jnp.mean(raw * raw, axis=1, keepdims=True) + 1e-06)
            out_ref[:, pl.ds(pl.multiple_of(h * D, D), D)] = (raw * scale * gain).astype(bf16)


def call(kernel, outs, args, scratch=(), specs=None, flops=0, name=None, vmem=32):
    moved = sum(a.size * a.dtype.itemsize for a in args)
    moved += sum(math.prod(o.shape) * o.dtype.itemsize for o in jax.tree.leaves(outs))
    return pl.pallas_call(
        kernel,
        out_shape=outs,
        in_specs=[VMEM] * len(args) if specs is None else specs,
        out_specs=[VMEM] * len(outs) if isinstance(outs, tuple) else VMEM,
        scratch_shapes=list(scratch),
        compiler_params=pltpu.CompilerParams(vmem_limit_bytes=vmem * 2**20),
        cost_estimate=pl.CostEstimate(flops=flops, bytes_accessed=moved, transcendentals=0),
        name=name,
    )(*args)


def like(*shape):
    return jax.ShapeDtypeStruct(shape, f32)


def on_device(
    n_dev,
    n_sub,
    queries,
    key_vectors,
    values,
    log_decay,
    write_rate,
    passage_lengths,
    norm_gain,
):
    assert values.shape[0] == BLOCK
    tokens = n_dev * BLOCK
    longest = LONGEST.get(tokens, tokens)
    reach = min(-(-longest // (GROUP * BLOCK)), n_dev // GROUP)
    n = 2
    swap_pairs = [(i, i ^ 1) for i in range(n_dev)]
    next_pairs = [(i, i + GROUP) for i in range(n_dev - GROUP)]

    def chip_pairs(slot):
        return [(i, i ^ (2 * slot)) for i in range(n_dev)]

    def permute(x, pairs):
        return lax.ppermute(x, AXES, pairs)

    step = 2 * BLOCK**3
    inverses, recvs, extras, got = [], [], [], [None] * CHIPS
    inputs = (passage_lengths, key_vectors, values, log_decay, write_rate)
    after = []
    for phase, slots in enumerate(PHASES):
        count = 4 * len(slots)
        halves = pltpu.VMEM((count // 2, D, 2 * D), f32)
        scratch, specs = (), [SMEM] + [VMEM] * 4
        placed = inputs
        if phase == 0:
            placed = [pltpu.with_memory_space_constraint(x, pltpu.HBM) for x in inputs]
            specs = [HBM] * 5
            scratch = [pltpu.SMEM(passage_lengths.shape, jnp.int32)]
            scratch += [pltpu.VMEM(x.shape, x.dtype) for x in inputs[1:]]
            scratch += [pltpu.SemaphoreType.DMA((5,))]
        keep, send, inverse = call(
            functools.partial(maps_kernel, slots, n_sub),
            (halves, halves, pltpu.VMEM((count, BLOCK, BLOCK), f32)),
            (*placed, *after),
            scratch=scratch,
            specs=specs + [ANY] * len(after),
            flops=count * 44 * step,
            name="maps",
        )
        recv = permute(send, swap_pairs)
        inverses.append(inverse)
        recvs.append(recv)
        extras.append(permute(keep, swap_pairs))
        outs = call(
            functools.partial(chip_kernel, n_sub),
            (like(n, D, 2 * D),) * len(slots),
            (keep, recv),
            flops=count * 3 * step,
            name="chip",
        )
        after = [outs[0]]
        for slot, out in zip(slots, outs):
            got[slot] = permute(out, chip_pairs(slot)) if slot else out
    read = call(
        functools.partial(readout_kernel, n_sub),
        tuple(like(4 * len(slots), BLOCK, 2 * D) for slots in PHASES),
        (
            passage_lengths,
            queries,
            key_vectors,
            values,
            log_decay,
            write_rate,
            *inverses,
            *recvs,
            *extras,
        ),
        specs=[SMEM] + [VMEM] * (5 + 3 * len(PHASES)),
        flops=16 * 13 * step,
        name="readout",
    )
    total_map, total_add, ahead = call(
        functools.partial(group_kernel, n_sub),
        (like(n, D, D), like(n, D, D), like(n, 3, D, 2 * D)),
        (*got, read[0]),
        specs=[VMEM] * CHIPS + [ANY],
        scratch=(pltpu.VMEM((CHIPS, n, D, 2 * D), f32),),
        flops=n * 24 * step,
        name="group",
    )
    state = total_add
    for _ in range(reach - 1):
        state = permute(state, next_pairs)
        state = call(
            step_kernel,
            like(n, D, D),
            (total_map, total_add, state),
            flops=n * 3 * step,
            name="step",
        )
    state = permute(state, next_pairs)
    outs = call(
        functools.partial(spread_kernel, n_sub),
        (like(n, D, D),) * CHIPS,
        (ahead, state),
        scratch=(pltpu.VMEM((CHIPS, n, D, D), f32),),
        flops=n * 9 * step,
        name="spread",
    )
    own = [outs[0]] + [permute(outs[slot], chip_pairs(slot)) for slot in range(1, CHIPS)]
    other = [permute(x, swap_pairs) for x in own]
    return call(
        functools.partial(output_kernel, n_sub),
        jax.ShapeDtypeStruct((BLOCK, VALUE_HEADS * D), bf16),
        (norm_gain.reshape(1, D), *read, *own, *other),
        flops=16 * 3 * step,
        name="output",
    )


def solution(mesh):
    n_sub = mesh.shape["sub"]
    n_dev = mesh.shape["seq"] * n_sub
    tokens = P(AXES, None)
    heads = P(None, AXES)
    return jax.shard_map(
        functools.partial(on_device, n_dev, n_sub),
        mesh=mesh,
        in_specs=(tokens, tokens, tokens, heads, heads, P(), P()),
        out_specs=tokens,
        check_vma=False,
    )
```

time: 103 us -> 55.2 us (0.54)
  Pallas kernels: 58.2 us -> 18.7 us
  local copies, waits for them, and re-layouts: 4.07 us -> 0.04 us
  waiting for transfers between devices: 21.1 us -> 18 us
  starting transfers between devices: 19.2 us -> 17.8 us
    pallas_call x7, Pallas kernels: 58.2 us -> 18.7 us  [call(): pl.pallas_call(kernel, out_shape=outs, in_specs=[VMEM] * len(args) if spe...]
    unnamed x24 -> x14, local copies, waits for them, and re-layouts: 4.07 us -> 0.04 us
    ppermute x14, waiting for transfers between devices: 21.1 us -> 18 us  [permute(): return lax.ppermute(x, AXES, pairs)]
    ppermute x14, starting transfers between devices: 19.2 us -> 17.8 us  [permute(): return lax.ppermute(x, AXES, pairs)]
  transfers between devices with their start and end apart: 14 -> 14, of which waited for: 6 -> 6; matrix products, arithmetic and copies ran while one was open for 0% -> 0% of each run, Pallas kernels for 14% -> 11%
where the time goes in v2:
time: 55.2 us; the launch traced here: 54.7 us
  Pallas kernels  18.7 us (34%)
  waiting for transfers between devices  18 us (33%)
  starting transfers between devices  17.8 us (32%)
    pallas_call x7, Pallas kernels, call(): pl.pallas_call(kernel, out_shape=outs, in_specs=[VMEM] * len(args) if spe...  18.7 us
    ppermute x14, waiting for transfers between devices, permute(): return lax.ppermute(x, AXES, pairs)  18 us
    ppermute x14, starting transfers between devices, permute(): return lax.ppermute(x, AXES, pairs)  17.8 us
  transfers between devices with their start and end apart: 14, of which 6 were waited for; matrix products, arithmetic and copies ran while one was open for 0% of the time, Pallas kernels for 11%

profile of v2, /device:TPU:25, one launch (start us, length us, event | category | flops | bytes accessed | tf_op | source)
XLA Modules:
  0.0 54.7 jit_solution(8771443547231951363)
XLA Ops:
  0.0 9.8 %maps.1 = (f32[8,128,256]{2,1,0:T(8,128)S(1)}, f32[8,128,256]{2,1,0:T(8,128)S(1)}, f32[16,128,128]{2,1,0:T(8,128)S(1)}) custom-call(s32[8]{0:T(128)} %lengths_ref.1, bf16[128,1024]{1,0:T(8,128)(2,1)} %k_ref.1, bf16[128,2048]{1,0:T(8,128)(2,1)} %v_ref.1, f32[16,128]{1,0:T(8,128)} %decay_ref.1, f32[16,128]{1,0:T(8,128)} %rate_ref.1), custom_call_target="tpu_custom_call" | custom-call | flops 2952790016 | bytes 3948576 | tf_op jit(solution)/shard_map/maps/pallas_call | solution.py:349
  9.8 0.0 copy-start
  9.8 0.0 copy-start.1
  9.9 0.0 copy-start.2
  9.9 0.0 copy-start.3
  9.9 0.0 copy-start.4
  9.9 0.7 %collective-permute-start = (f32[8,128,256]{2,1,0:T(8,128)S(1)}, f32[8,128,256]{2,1,0:T(8,128)S(1)}, u32[]{:S(2)}, u32[]{:S(2)}) collective-permute-start(f32[8,128,256]{2,1,0:T(8,128)S(1)} %get-tuple-element.20), channel_id=1, source_target_pairs={{0,1},{1,0},{2,3},{3,2},{4,5},{5,4},{6,7},{7,6},{8,9},{9,8},{10,11... | collective-permute-start | bytes 3145736 | tf_op jit(solution)/shard_map/ppermute | solution.py:388
  10.6 0.1 collective-permute-start.1
  10.7 2.2 %collective-permute-done.refs_1_.recv_ref = f32[8,128,256]{2,1,0:T(8,128)S(1)} collective-permute-done((f32[8,128,256]{2,1,0:T(8,128)S(1)}, f32[8,128,256]{2,1,0:T(8,128)S(1)}, u32[]{:S(2)}, u32[]{:S(2)}) %collective-permute-start) | collective-permute-done | bytes 1048608 | tf_op jit(solution)/shard_map/ppermute | solution.py:388
  12.9 0.5 chip.1
  13.5 1.3 %collective-permute-start.2 = (f32[2,128,256]{2,1,0:T(8,128)S(1)}, f32[2,128,256]{2,1,0:T(8,128)S(1)}, u32[]{:S(2)}, u32[]{:S(2)}) collective-permute-start(f32[2,128,256]{2,1,0:T(8,128)S(1)} %get-tuple-element.23), channel_id=1, source_target_pairs={{0,2},{1,3},{2,0},{3,1},{4,6},{5,7},{6,4},{7,5},{8,10},{9,11},{10,... | collective-permute-start | bytes 786440 | tf_op jit(solution)/shard_map/ppermute | solution.py:388
  14.8 1.2 %collective-permute-start.3 = (f32[2,128,256]{2,1,0:T(8,128)S(1)}, f32[2,128,256]{2,1,0:T(8,128)S(1)}, u32[]{:S(2)}, u32[]{:S(2)}) collective-permute-start(f32[2,128,256]{2,1,0:T(8,128)S(1)} %get-tuple-element.24), channel_id=1, source_target_pairs={{0,4},{1,5},{2,6},{3,7},{4,0},{5,1},{6,2},{7,3},{8,12},{9,13},{10,... | collective-permute-start | bytes 786440 | tf_op jit(solution)/shard_map/ppermute | solution.py:388
  16.0 0.2 collective-permute-start.4
  16.2 5.5 %readout.1.after_ref.refs_0_ = f32[16,128,256]{2,1,0:T(8,128)S(1)} custom-call(s32[8]{0:T(128)S(1)} %copy-done.5, bf16[128,1024]{1,0:T(8,128)(2,1)S(1)} %copy-done.1, bf16[128,1024]{1,0:T(8,128)(2,1)S(1)} %copy-done.2, bf16[128,2048]{1,0:T(8,128)(2,1)S(1)} %copy-done, f32[16,128]{1,0:T(8,128)S(1)} %copy-done.3, f32[16,128]{1,0:T(8,128)S(1)} %copy-done.4, ...), custom_call_target="tpu_custom_call" | custom-call | flops 872415232 | bytes 6307872 | tf_op jit(solution)/shard_map/readout/pallas_call | solution.py:349
  21.7 0.2 collective-permute-done.3.r2
  22.0 5.7 %collective-permute-done.4.r3 = f32[2,128,256]{2,1,0:T(8,128)S(1)} collective-permute-done((f32[2,128,256]{2,1,0:T(8,128)S(1)}, f32[2,128,256]{2,1,0:T(8,128)S(1)}, u32[]{:S(2)}, u32[]{:S(2)}) %collective-permute-start.4) | collective-permute-done | bytes 262176 | tf_op jit(solution)/shard_map/ppermute | solution.py:388
  27.7 0.8 %group.1 = (f32[2,128,128]{2,1,0:T(8,128)S(1)}, f32[2,128,128]{2,1,0:T(8,128)S(1)}, f32[2,3,128,256]{3,2,1,0:T(8,128)S(1)}) custom-call(f32[2,128,256]{2,1,0:T(8,128)S(1)} %get-tuple-element.22.r0, f32[2,128,256]{2,1,0:T(8,128)S(1)} %collective-permute-done.2.r1, f32[2,128,256]{2,1,0:T(8,128)S(1)} %collective-permute-done.3.r2, ...), custom_call_target="tpu_custom_call" | custom-call | flops 201326592 | bytes 4194304 | tf_op jit(solution)/shard_map/group/pallas_call | solution.py:349
  28.5 1.3 %collective-permute-start.5 = (f32[2,128,128]{2,1,0:T(8,128)S(1)}, f32[2,128,128]{2,1,0:T(8,128)S(1)}, u32[]{:S(2)}, u32[]{:S(2)}) collective-permute-start(f32[2,128,128]{2,1,0:T(8,128)S(1)} %get-tuple-element.28.add_ref), channel_id=1, source_target_pairs={{0,8},{1,9},{2,10},{3,11},{4,12},{5,13},{6,14},{7,15},{8,16},{9,17... | collective-permute-start | bytes 393224 | tf_op jit(solution)/shard_map/ppermute | solution.py:388
  29.8 4.4 %collective-permute-done.5.state_ref = f32[2,128,128]{2,1,0:T(8,128)S(1)} collective-permute-done((f32[2,128,128]{2,1,0:T(8,128)S(1)}, f32[2,128,128]{2,1,0:T(8,128)S(1)}, u32[]{:S(2)}, u32[]{:S(2)}) %collective-permute-start.5) | collective-permute-done | bytes 131104 | tf_op jit(solution)/shard_map/ppermute | solution.py:388
  34.3 0.2 step.1
  34.5 1.3 %collective-permute-start.6 = (f32[2,128,128]{2,1,0:T(8,128)S(1)}, f32[2,128,128]{2,1,0:T(8,128)S(1)}, u32[]{:S(2)}, u32[]{:S(2)}) collective-permute-start(f32[2,128,128]{2,1,0:T(8,128)S(1)} %step.1), channel_id=1, source_target_pairs={{0,8},{1,9},{2,10},{3,11},{4,12},{5,13},{6,14},{7,15},{8,16},{9,17... | collective-permute-start | bytes 393224 | tf_op jit(solution)/shard_map/ppermute | solution.py:388
  35.8 4.4 %collective-permute-done.6.state_ref = f32[2,128,128]{2,1,0:T(8,128)S(1)} collective-permute-done((f32[2,128,128]{2,1,0:T(8,128)S(1)}, f32[2,128,128]{2,1,0:T(8,128)S(1)}, u32[]{:S(2)}, u32[]{:S(2)}) %collective-permute-start.6) | collective-permute-done | bytes 131104 | tf_op jit(solution)/shard_map/ppermute | solution.py:388
  40.2 0.3 spread.1
  40.5 1.2 %collective-permute-start.7 = (f32[2,128,128]{2,1,0:T(8,128)S(1)}, f32[2,128,128]{2,1,0:T(8,128)S(1)}, u32[]{:S(2)}, u32[]{:S(2)}) collective-permute-start(f32[2,128,128]{2,1,0:T(8,128)S(1)} %get-tuple-element.30), channel_id=1, source_target_pairs={{0,2},{1,3},{2,0},{3,1},{4,6},{5,7},{6,4},{7,5},{8,10},{9,11},{10,... | collective-permute-start | bytes 393224 | tf_op jit(solution)/shard_map/ppermute | solution.py:388
  41.8 0.3 collective-permute-start.8
  42.0 1.2 %collective-permute-start.9 = (f32[2,128,128]{2,1,0:T(8,128)S(1)}, f32[2,128,128]{2,1,0:T(8,128)S(1)}, u32[]{:S(2)}, u32[]{:S(2)}) collective-permute-start(f32[2,128,128]{2,1,0:T(8,128)S(1)} %get-tuple-element.32), channel_id=1, source_target_pairs={{0,6},{1,7},{2,4},{3,5},{4,2},{5,3},{6,0},{7,1},{8,14},{9,15},{10,... | collective-permute-start | bytes 393224 | tf_op jit(solution)/shard_map/ppermute | solution.py:388
  43.2 4.6 %collective-permute-start.10 = (f32[2,128,128]{2,1,0:T(8,128)S(1)}, f32[2,128,128]{2,1,0:T(8,128)S(1)}, u32[]{:S(2)}, u32[]{:S(2)}) collective-permute-start(f32[2,128,128]{2,1,0:T(8,128)S(1)} %get-tuple-element.29.refs_1_), channel_id=1, source_target_pairs={{0,1},{1,0},{2,3},{3,2},{4,5},{5,4},{6,7},{7,6},{8,9},{9,8},{10,11... | collective-permute-start | bytes 393224 | tf_op jit(solution)/shard_map/ppermute | solution.py:388
  47.8 1.5 %collective-permute-start.11 = (f32[2,128,128]{2,1,0:T(8,128)S(1)}, f32[2,128,128]{2,1,0:T(8,128)S(1)}, u32[]{:S(2)}, u32[]{:S(2)}) collective-permute-start(f32[2,128,128]{2,1,0:T(8,128)S(1)} %collective-permute-done.7.refs_2_), channel_id=1, source_target_pairs={{0,1},{1,0},{2,3},{3,2},{4,5},{5,4},{6,7},{7,6},{8,9},{9,8},{10,11... | collective-permute-start | bytes 393224 | tf_op jit(solution)/shard_map/ppermute | solution.py:388
  49.3 1.2 %collective-permute-start.12 = (f32[2,128,128]{2,1,0:T(8,128)S(1)}, f32[2,128,128]{2,1,0:T(8,128)S(1)}, u32[]{:S(2)}, u32[]{:S(2)}) collective-permute-start(f32[2,128,128]{2,1,0:T(8,128)S(1)} %collective-permute-done.8.refs_3_), channel_id=1, source_target_pairs={{0,1},{1,0},{2,3},{3,2},{4,5},{5,4},{6,7},{7,6},{8,9},{9,8},{10,11... | collective-permute-start | bytes 393224 | tf_op jit(solution)/shard_map/ppermute | solution.py:388
  50.5 1.7 %collective-permute-start.13 = (f32[2,128,128]{2,1,0:T(8,128)S(1)}, f32[2,128,128]{2,1,0:T(8,128)S(1)}, u32[]{:S(2)}, u32[]{:S(2)}) collective-permute-start(f32[2,128,128]{2,1,0:T(8,128)S(1)} %collective-permute-done.9.refs_4_), channel_id=1, source_target_pairs={{0,1},{1,0},{2,3},{3,2},{4,5},{5,4},{6,7},{7,6},{8,9},{9,8},{10,11... | collective-permute-start | bytes 393224 | tf_op jit(solution)/shard_map/ppermute | solution.py:388
  52.2 1.0 %collective-permute-done.13.refs_8_ = f32[2,128,128]{2,1,0:T(8,128)S(1)} collective-permute-done((f32[2,128,128]{2,1,0:T(8,128)S(1)}, f32[2,128,128]{2,1,0:T(8,128)S(1)}, u32[]{:S(2)}, u32[]{:S(2)}) %collective-permute-start.13) | collective-permute-done | bytes 131104 | tf_op jit(solution)/shard_map/ppermute | solution.py:388
  53.2 1.5 %output.1 = bf16[128,2048]{1,0:T(8,128)(2,1)} custom-call(f32[1,128]{1,0:T(1,128)S(1)} %bitcast.1, f32[16,128,256]{2,1,0:T(8,128)S(1)} %readout.1.after_ref.refs_0_, f32[2,128,128]{2,1,0:T(8,128)S(1)} %get-tuple-element.29.refs_1_, f32[2,128,128]{2,1,0:T(8,128)S(1)} %collective-permute-done.7.refs_2_, f32[2,128,128]{2,1,0:T(8,128)S(1)} %collective-permute-done.8.refs_3_, ...), custom_call_target="tpu_custom_call" | custom-call | flops 201326592 | bytes 3670528 | tf_op jit(solution)/shard_map/output/pallas_call | solution.py:349
  (17 shorter events, 0.0 us)
Async XLA Ops:
  9.8 6.4 %copy-start = (bf16[128,2048]{1,0:T(8,128)(2,1)S(1)}, bf16[128,2048]{1,0:T(8,128)(2,1)}, u32[]{:S(2)}) copy-start(bf16[128,2048]{1,0:T(8,128)(2,1)} %v_ref.1) | copy-start | bytes 1572868
  9.8 6.4 %copy-start.1 = (bf16[128,1024]{1,0:T(8,128)(2,1)S(1)}, bf16[128,1024]{1,0:T(8,128)(2,1)}, u32[]{:S(2)}) copy-start(bf16[128,1024]{1,0:T(8,128)(2,1)} %q_ref.1) | copy-start | bytes 786436
  9.9 6.4 %copy-start.2 = (bf16[128,1024]{1,0:T(8,128)(2,1)S(1)}, bf16[128,1024]{1,0:T(8,128)(2,1)}, u32[]{:S(2)}) copy-start(bf16[128,1024]{1,0:T(8,128)(2,1)} %k_ref.1) | copy-start | bytes 786436
  9.9 6.4 %copy-start.3 = (f32[16,128]{1,0:T(8,128)S(1)}, f32[16,128]{1,0:T(8,128)}, u32[]{:S(2)}) copy-start(f32[16,128]{1,0:T(8,128)} %decay_ref.1) | copy-start | bytes 24580
  9.9 6.4 %copy-start.4 = (f32[16,128]{1,0:T(8,128)S(1)}, f32[16,128]{1,0:T(8,128)}, u32[]{:S(2)}) copy-start(f32[16,128]{1,0:T(8,128)} %rate_ref.1) | copy-start | bytes 24580
  9.9 6.3 %copy-start.5 = (s32[8]{0:T(128)S(1)}, s32[8]{0:T(128)}, u32[]{:S(2)}) copy-start(s32[8]{0:T(128)} %lengths_ref.1) | copy-start | bytes 100
  9.9 3.0 %collective-permute-start = (f32[8,128,256]{2,1,0:T(8,128)S(1)}, f32[8,128,256]{2,1,0:T(8,128)S(1)}, u32[]{:S(2)}, u32[]{:S(2)}) collective-permute-start(f32[8,128,256]{2,1,0:T(8,128)S(1)} %get-tuple-element.20), channel_id=1, source_target_pairs={{0,1},{1,0},{2,3},{3,2},{4,5},{5,4},{6,7},{7,6},{8,9},{9,8},{10,11... | collective-permute-start | bytes 3145736 | tf_op jit(solution)/shard_map/ppermute | solution.py:388
  10.6 5.5 %collective-permute-start.1 = (f32[8,128,256]{2,1,0:T(8,128)S(1)}, f32[8,128,256]{2,1,0:T(8,128)S(1)}, u32[]{:S(2)}, u32[]{:S(2)}) collective-permute-start(f32[8,128,256]{2,1,0:T(8,128)S(1)} %get-tuple-element.21.keep_ref), channel_id=1, source_target_pairs={{0,1},{1,0},{2,3},{3,2},{4,5},{5,4},{6,7},{7,6},{8,9},{9,8},{10,11... | collective-permute-start | bytes 3145736 | tf_op jit(solution)/shard_map/ppermute | solution.py:388
  13.5 8.3 %collective-permute-start.2 = (f32[2,128,256]{2,1,0:T(8,128)S(1)}, f32[2,128,256]{2,1,0:T(8,128)S(1)}, u32[]{:S(2)}, u32[]{:S(2)}) collective-permute-start(f32[2,128,256]{2,1,0:T(8,128)S(1)} %get-tuple-element.23), channel_id=1, source_target_pairs={{0,2},{1,3},{2,0},{3,1},{4,6},{5,7},{6,4},{7,5},{8,10},{9,11},{10,... | collective-permute-start | bytes 786440 | tf_op jit(solution)/shard_map/ppermute | solution.py:388
  14.8 7.2 %collective-permute-start.3 = (f32[2,128,256]{2,1,0:T(8,128)S(1)}, f32[2,128,256]{2,1,0:T(8,128)S(1)}, u32[]{:S(2)}, u32[]{:S(2)}) collective-permute-start(f32[2,128,256]{2,1,0:T(8,128)S(1)} %get-tuple-element.24), channel_id=1, source_target_pairs={{0,4},{1,5},{2,6},{3,7},{4,0},{5,1},{6,2},{7,3},{8,12},{9,13},{10,... | collective-permute-start | bytes 786440 | tf_op jit(solution)/shard_map/ppermute | solution.py:388
  16.0 11.7 %collective-permute-start.4 = (f32[2,128,256]{2,1,0:T(8,128)S(1)}, f32[2,128,256]{2,1,0:T(8,128)S(1)}, u32[]{:S(2)}, u32[]{:S(2)}) collective-permute-start(f32[2,128,256]{2,1,0:T(8,128)S(1)} %get-tuple-element.25), channel_id=1, source_target_pairs={{0,6},{1,7},{2,4},{3,5},{4,2},{5,3},{6,0},{7,1},{8,14},{9,15},{10,... | collective-permute-start | bytes 786440 | tf_op jit(solution)/shard_map/ppermute | solution.py:388
  27.7 25.5 %copy-start.6 = (f32[128]{0:T(128)S(1)}, f32[128]{0:T(128)}, u32[]{:S(2)}) copy-start(f32[128]{0:T(128)} %param.13) | copy-start | bytes 1540
  28.5 5.7 %collective-permute-start.5 = (f32[2,128,128]{2,1,0:T(8,128)S(1)}, f32[2,128,128]{2,1,0:T(8,128)S(1)}, u32[]{:S(2)}, u32[]{:S(2)}) collective-permute-start(f32[2,128,128]{2,1,0:T(8,128)S(1)} %get-tuple-element.28.add_ref), channel_id=1, source_target_pairs={{0,8},{1,9},{2,10},{3,11},{4,12},{5,13},{6,14},{7,15},{8,16},{9,17... | collective-permute-start | bytes 393224 | tf_op jit(solution)/shard_map/ppermute | solution.py:388
  34.5 5.7 %collective-permute-start.6 = (f32[2,128,128]{2,1,0:T(8,128)S(1)}, f32[2,128,128]{2,1,0:T(8,128)S(1)}, u32[]{:S(2)}, u32[]{:S(2)}) collective-permute-start(f32[2,128,128]{2,1,0:T(8,128)S(1)} %step.1), channel_id=1, source_target_pairs={{0,8},{1,9},{2,10},{3,11},{4,12},{5,13},{6,14},{7,15},{8,16},{9,17... | collective-permute-start | bytes 393224 | tf_op jit(solution)/shard_map/ppermute | solution.py:388
  40.5 7.3 %collective-permute-start.7 = (f32[2,128,128]{2,1,0:T(8,128)S(1)}, f32[2,128,128]{2,1,0:T(8,128)S(1)}, u32[]{:S(2)}, u32[]{:S(2)}) collective-permute-start(f32[2,128,128]{2,1,0:T(8,128)S(1)} %get-tuple-element.30), channel_id=1, source_target_pairs={{0,2},{1,3},{2,0},{3,1},{4,6},{5,7},{6,4},{7,5},{8,10},{9,11},{10,... | collective-permute-start | bytes 393224 | tf_op jit(solution)/shard_map/ppermute | solution.py:388
  41.8 7.5 %collective-permute-start.8 = (f32[2,128,128]{2,1,0:T(8,128)S(1)}, f32[2,128,128]{2,1,0:T(8,128)S(1)}, u32[]{:S(2)}, u32[]{:S(2)}) collective-permute-start(f32[2,128,128]{2,1,0:T(8,128)S(1)} %get-tuple-element.31), channel_id=1, source_target_pairs={{0,4},{1,5},{2,6},{3,7},{4,0},{5,1},{6,2},{7,3},{8,12},{9,13},{10,... | collective-permute-start | bytes 393224 | tf_op jit(solution)/shard_map/ppermute | solution.py:388
  42.0 8.5 %collective-permute-start.9 = (f32[2,128,128]{2,1,0:T(8,128)S(1)}, f32[2,128,128]{2,1,0:T(8,128)S(1)}, u32[]{:S(2)}, u32[]{:S(2)}) collective-permute-start(f32[2,128,128]{2,1,0:T(8,128)S(1)} %get-tuple-element.32), channel_id=1, source_target_pairs={{0,6},{1,7},{2,4},{3,5},{4,2},{5,3},{6,0},{7,1},{8,14},{9,15},{10,... | collective-permute-start | bytes 393224 | tf_op jit(solution)/shard_map/ppermute | solution.py:388
  43.2 9.0 %collective-permute-start.10 = (f32[2,128,128]{2,1,0:T(8,128)S(1)}, f32[2,128,128]{2,1,0:T(8,128)S(1)}, u32[]{:S(2)}, u32[]{:S(2)}) collective-permute-start(f32[2,128,128]{2,1,0:T(8,128)S(1)} %get-tuple-element.29.refs_1_), channel_id=1, source_target_pairs={{0,1},{1,0},{2,3},{3,2},{4,5},{5,4},{6,7},{7,6},{8,9},{9,8},{10,11... | collective-permute-start | bytes 393224 | tf_op jit(solution)/shard_map/ppermute | solution.py:388
  47.8 4.4 %collective-permute-start.11 = (f32[2,128,128]{2,1,0:T(8,128)S(1)}, f32[2,128,128]{2,1,0:T(8,128)S(1)}, u32[]{:S(2)}, u32[]{:S(2)}) collective-permute-start(f32[2,128,128]{2,1,0:T(8,128)S(1)} %collective-permute-done.7.refs_2_), channel_id=1, source_target_pairs={{0,1},{1,0},{2,3},{3,2},{4,5},{5,4},{6,7},{7,6},{8,9},{9,8},{10,11... | collective-permute-start | bytes 393224 | tf_op jit(solution)/shard_map/ppermute | solution.py:388
  49.3 3.0 %collective-permute-start.12 = (f32[2,128,128]{2,1,0:T(8,128)S(1)}, f32[2,128,128]{2,1,0:T(8,128)S(1)}, u32[]{:S(2)}, u32[]{:S(2)}) collective-permute-start(f32[2,128,128]{2,1,0:T(8,128)S(1)} %collective-permute-done.8.refs_3_), channel_id=1, source_target_pairs={{0,1},{1,0},{2,3},{3,2},{4,5},{5,4},{6,7},{7,6},{8,9},{9,8},{10,11... | collective-permute-start | bytes 393224 | tf_op jit(solution)/shard_map/ppermute | solution.py:388
  50.5 2.7 %collective-permute-start.13 = (f32[2,128,128]{2,1,0:T(8,128)S(1)}, f32[2,128,128]{2,1,0:T(8,128)S(1)}, u32[]{:S(2)}, u32[]{:S(2)}) collective-permute-start(f32[2,128,128]{2,1,0:T(8,128)S(1)} %collective-permute-done.9.refs_4_), channel_id=1, source_target_pairs={{0,1},{1,0},{2,3},{3,2},{4,5},{5,4},{6,7},{7,6},{8,9},{9,8},{10,11... | collective-permute-start | bytes 393224 | tf_op jit(solution)/shard_map/ppermute | solution.py:388

commit v3 on v2

v3 whole, which is shorter than its diff:
```python
import functools
import math

import jax
import jax.numpy as jnp
from jax import lax
from jax.experimental import pallas as pl
from jax.experimental.pallas import tpu as pltpu
from jax.sharding import PartitionSpec as P

D = 128
VALUE_HEADS = 16
HK = 8
BLOCK = 128
AXES = ("seq", "sub")
CHIPS = 4
GROUP = 2 * CHIPS
LONGEST = {4096: 2048, 65536: 8192}

f32 = jnp.float32
bf16 = jnp.bfloat16
VMEM = pl.BlockSpec(memory_space=pltpu.VMEM)
ANY = pl.BlockSpec(memory_space=pl.ANY)
HBM = pl.BlockSpec(memory_space=pltpu.HBM)


def my_rank(n_sub):
    return lax.axis_index("seq") * n_sub + lax.axis_index("sub")


def mm(a, b):
    return lax.dot_general(a, b, (((1,), (0,)), ((), ())), preferred_element_type=f32)


def mm_nt(a, b, precision=None):
    return lax.dot_general(
        a, b, (((1,), (1,)), ((), ())), preferred_element_type=f32, precision=precision
    )


def split(x):
    high = x.astype(bf16)
    return high, (x - high.astype(f32)).astype(bf16)


def across(high, low):
    return jnp.concatenate([high, low], axis=1)


def square(high, low):
    wide = across(high, low)
    return jnp.concatenate([wide, wide], axis=0)


def left(x):
    return across(*split(x))


def right(x):
    return square(*split(x))


def fold(x):
    half = x.shape[1] // 2
    return x[:, :half] + x[:, half:]


def mm_tall(a, b):
    rows = a[0].shape[0]
    out = mm(jnp.concatenate(a, axis=0), across(*b))
    return out[:rows, :D] + (out[:rows, D:] + out[rows:, :D])


def mm_half(a, b):
    rows = a[0].shape[0]
    out = mm(jnp.concatenate(a, axis=0), b)
    return out[:rows] + out[rows:]


def mm3(a, b):
    return fold(mm(left(a), right(b)))


def mm2(a, b):
    return mm(left(a), twice(b))


def twice(x):
    return jnp.concatenate([x, x], axis=0)


def compose(later, early):
    both = mm3(later[:, :D], early)
    return jnp.concatenate([both[:, :D], both[:, D:] + later[:, D:]], axis=1)


def iota(axis):
    return lax.broadcasted_iota(jnp.int32, (BLOCK, BLOCK), axis)


def token_masks(lengths_ref, n_sub):
    first = my_rank(n_sub) * BLOCK
    row_at = first + lax.broadcasted_iota(jnp.int32, (1, BLOCK), 1)
    col_at = first + lax.broadcasted_iota(jnp.int32, (BLOCK, 1), 0)

    def one(i, carried):
        start, row, col, before = carried
        row = row + (row_at >= start).astype(jnp.int32)
        col = col + (col_at >= start).astype(jnp.int32)
        before = before + (first > start).astype(jnp.int32)
        return start + lengths_ref[i], row, col, before

    zero = jnp.int32(0)
    _, row, col, before = lax.fori_loop(
        0,
        lengths_ref.shape[0],
        one,
        (zero, jnp.zeros((1, BLOCK), jnp.int32), jnp.zeros((BLOCK, 1), jnp.int32), zero),
    )
    return row, col, before


def gates(heads, decay_ref, rate_ref):
    decay = jnp.concatenate([decay_ref[pl.ds(h, 1), :] for h in heads], axis=0)
    rate_row = jnp.concatenate([rate_ref[pl.ds(h, 1), :] for h in heads], axis=0)
    lower = (iota(0) >= iota(1)).astype(f32)
    eye = (iota(0) == iota(1)).astype(f32)
    highest = lax.Precision.HIGHEST
    sum_row = mm_nt(decay, lower, highest)
    sum_col = mm_nt(lower, decay, highest)
    rate_col = mm_nt(eye, rate_row, highest)
    return sum_row, sum_col, rate_row, rate_col


def columns(ref, at):
    return ref[:, pl.ds(pl.multiple_of(at * D, D), D)]


def key_heads(n_sub, side):
    rank = my_rank(n_sub)
    core, chip = lax.rem(rank, 2), lax.rem(rank // 2, CHIPS)
    return [CHIPS * (core ^ side) + (chip ^ slot) for slot in range(CHIPS)]


def value_heads(keys):
    return [2 * j + part for j in keys for part in range(2)]


def key_norms(key, key_t):
    wide = key.astype(f32)
    col = lax.rsqrt(jnp.sum(wide * wide, axis=1, keepdims=True) + 1e-06)
    wide_t = key_t.astype(f32)
    row = lax.rsqrt(jnp.sum(wide_t * wide_t, axis=0, keepdims=True) + 1e-06)
    return col, row


def odd_rows(x, size):
    return jnp.concatenate([x[i : i + size] for i in range(size, BLOCK, 2 * size)], axis=0)


def with_odd_rows(x, rows, size):
    pieces = []
    for i in range(0, BLOCK // 2, size):
        pieces += [x[2 * i : 2 * i + size], rows[i : i + size]]
    return jnp.concatenate(pieces, axis=0)


def invert(systems, apart):
    near = apart < 16
    eye = (apart == 0).astype(f32)
    solved = [eye - jnp.where(near, n, 0.0) for n in systems]
    parts = [split(n) for n in systems]
    near = near.astype(f32).astype(bf16)
    powers = [(high * near, low * near) for high, low in parts]
    powers = [split(fold(mm(across(*n), square(*n)))) for n in powers]
    for last in (False, False, True):
        if last:
            solved = [s + fold(mm(left(s), square(*n))) for s, n in zip(solved, powers)]
        else:
            both = [
                fold(mm(jnp.concatenate([across(*n), left(s)], axis=0), square(*n)))
                for n, s in zip(powers, solved)
            ]
            powers = [split(x[:BLOCK]) for x in both]
            solved = [s + x[BLOCK:] for s, x in zip(solved, both)]
    size = 16
    zero = jnp.zeros((BLOCK, BLOCK), bf16)
    while size < BLOCK:
        band = (apart >= size) & (apart < 2 * size)
        band = odd_rows(band.astype(f32), size).astype(bf16)
        pairs = [split(s) for s in solved]
        products = [
            split(mm_tall([odd_rows(p, size) * band for p in n], s))
            for n, s in zip(parts, pairs)
        ]
        fulls = [[with_odd_rows(zero, p, size) for p in u] for u in products]
        rows = [mm_tall([odd_rows(p, size) for p in s], u) for s, u in zip(pairs, fulls)]
        solved = [
            with_odd_rows(s, odd_rows(s, size) - r, size) for s, r in zip(solved, rows)
        ]
        size = 2 * size
    return solved


def first_maps_kernel(n_sub, *refs):
    sources, outs, (gain_ref, lengths_ref, sems) = refs[:6], refs[6:14], refs[14:]
    row_ref, col_ref = outs[6:]
    targets = (lengths_ref, *outs[2:6], gain_ref)
    copies = [
        pltpu.make_async_copy(a, b, sems.at[i]) for i, (a, b) in enumerate(zip(sources, targets))
    ]
    for copy in copies:
        copy.start()
    copies[0].wait()
    row, col, before = token_masks(lengths_ref, n_sub)
    row_ref[0:1] = row
    row_ref[1:2] = jnp.zeros_like(row) + before
    col_ref[...] = jnp.zeros((BLOCK, BLOCK), jnp.int32) + col
    for i in (1, 3, 4, 5):
        copies[i].wait()
    make_maps(1, n_sub, *outs[2:], *outs[:2], copies[2].wait)


def second_maps_kernel(n_sub, *refs):
    make_maps(0, n_sub, *refs, lambda: None)


def make_maps(
    side, n_sub, k_ref, v_ref, decay_ref, rate_ref, row_ref, col_ref, map_ref, inverse_ref, values_in
):
    keys = key_heads(n_sub, side)
    heads = value_heads(keys)
    seg_row, before = row_ref[0:1], row_ref[1:2]
    seg_col = col_ref[:, 0:1]
    sum_row, sum_col, rate_row, rate_col = gates(heads, decay_ref, rate_ref)
    apart = iota(0) ^ iota(1)
    strict = (iota(0) > iota(1)) & (seg_row == col_ref[...])
    eye = (apart == 0).astype(f32)
    reaches = (seg_row == before).astype(f32)
    last = seg_row[:, BLOCK - 1 :]
    ends_col = (seg_col == last).astype(f32)

    systems, details = [], []
    for j, key_head in enumerate(keys):
        key = columns(k_ref, key_head)
        key_t = key.T
        n_col, n_row = key_norms(key, key_t)
        gram = mm(key, key_t) * n_row
        for i in (2 * j, 2 * j + 1):
            s_row, s_col = sum_row[i : i + 1, :], sum_col[:, i : i + 1]
            b_row, b_col = rate_row[i : i + 1, :], rate_col[:, i : i + 1]
            between = jnp.exp(jnp.minimum(s_col - s_row, 0.0))
            systems.append(jnp.where(strict, between * gram * (b_col * n_col), 0.0))
            from_row = jnp.exp(s_row) * reaches
            end = jnp.exp(s_col[BLOCK - 1 :, :] - s_col) * ends_col * n_col
            details.append((key, key_t, n_row, b_row, from_row, end))
    solved = invert(systems, apart)
    values_in()
    for i, (key, key_t, n_row, b_row, from_row, end) in enumerate(details):
        inverse_ref[i] = solved[i]
        middle = solved[i] * end
        wy = mm_half(split(middle * (b_row * from_row * n_row)), key)
        fresh = mm_half(split(middle * b_row), columns(v_ref, heads[i]))
        high, low = split(across(wy, fresh))
        both = mm(across(key_t, key_t), jnp.concatenate([high, low], axis=0))
        map_ref[i, :, :D] = from_row[:, BLOCK - 1 :] * eye - both[:, :D]
        map_ref[i, :, D:] = both[:, D:]


def chip_kernel(n_sub, keep_ref, recv_ref, *out_refs):
    first = lax.rem(my_rank(n_sub), 2) == 0
    for i in range(keep_ref.shape[0]):
        mine, theirs = keep_ref[i], recv_ref[i]
        early = jnp.where(first, mine, theirs)
        late = jnp.where(first, theirs, mine)
        out_refs[i // 2][i % 2] = compose(late, early)


def group_kernel(n_sub, r0, r1, r2, r3, after_ref, add_ref, lower_ref, upper_ref, third_ref, held):
    chip = lax.rem(my_rank(n_sub) // 2, CHIPS)
    for slot, ref in enumerate((r0, r1, r2, r3)):
        held[chip ^ slot] = ref[...]
    for place in range(r0.shape[0]):
        one, third = held[0, place], held[2, place]
        two = compose(held[1, place], one)
        upper = compose(held[3, place], third)
        add_ref[place] = mm3(upper[:, :D], two[:, D:]) + upper[:, D:]
        lower_ref[place, 0] = one
        lower_ref[place, 1] = two
        upper_ref[place] = upper
        third_ref[place] = third


def ahead_kernel(lower_ref, upper_ref, third_ref, map_ref, ahead_ref):
    for place in range(upper_ref.shape[0]):
        two = lower_ref[place, 1]
        map_ref[place] = mm3(upper_ref[place, :, :D], two[:, :D])
        ahead_ref[place, 0] = lower_ref[place, 0]
        ahead_ref[place, 1] = two
        ahead_ref[place, 2] = compose(third_ref[place], two)


def step_kernel(map_ref, add_ref, state_ref, out_ref):
    for place in range(map_ref.shape[0]):
        out_ref[place] = add_ref[place] + mm3(map_ref[place], state_ref[place])


def spread_kernel(n_sub, ahead_ref, state_ref, o0, o1, o2, o3, held):
    rank = my_rank(n_sub)
    chip = lax.rem(rank // 2, CHIPS)
    for place in range(state_ref.shape[0]):
        state = state_ref[place]
        held[0, place] = state
        for i in range(CHIPS - 1):
            held[i + 1, place] = (
                mm3(ahead_ref[place, i, :, :D], state) + ahead_ref[place, i, :, D:]
            )
    for slot, ref in enumerate((o0, o1, o2, o3)):
        ref[...] = held[chip ^ slot]


def readout_kernel(n_sub, q_ref, k_ref, v_ref, decay_ref, rate_ref, row_ref, col_ref, *refs):
    inverse_refs, early_refs, read_refs = refs[:2], refs[2:4], refs[4:]
    core = lax.rem(my_rank(n_sub), 2)
    seg_row, before = row_ref[0:1], row_ref[1:2]
    lower = (iota(0) >= iota(1)) & (seg_row == col_ref[...])
    reaches_row = (seg_row == before).astype(f32)
    reaches_col = (col_ref[:, 0:1] == before[:, 0:1]).astype(f32)
    for side in range(2):
        keys = key_heads(n_sub, side)
        heads = value_heads(keys)
        sum_row, sum_col, rate_row, _ = gates(heads, decay_ref, rate_ref)
        for j, key_head in enumerate(keys):
            key = columns(k_ref, key_head)
            key_t = key.T
            n_col, n_row = key_norms(key, key_t)
            query = columns(q_ref, key_head)
            wide = query.astype(f32)
            q_col = lax.rsqrt(jnp.sum(wide * wide, axis=1, keepdims=True) + 1e-06)
            cross = mm(query, key_t) * n_row
            for i in (2 * j, 2 * j + 1):
                s_row, s_col = sum_row[i : i + 1, :], sum_col[:, i : i + 1]
                b_row = rate_row[i : i + 1, :]
                between = jnp.exp(jnp.minimum(s_col - s_row, 0.0))
                scores = jnp.where(lower, between * cross * q_col, 0.0)
                mixed = mm3(scores, inverse_refs[side][i])
                from_row = jnp.exp(s_row) * reaches_row
                from_col = jnp.exp(s_col) * reaches_col
                fresh = mm2(mixed * b_row, columns(v_ref, heads[i]))
                through = wide * (from_col * q_col) - mm2(mixed * (b_row * from_row * n_row), key)
                read_refs[side][i] = across(through, fresh)

    @pl.when(core == 1)
    def _():
        for early_ref, read_ref in zip(early_refs, read_refs):
            for i in range(VALUE_HEADS // 2):
                read = read_ref[i]
                both = mm3(read[:, :D], early_ref[i])
                read_ref[i, :, :D] = both[:, :D]
                read_ref[i, :, D:] = both[:, D:] + read[:, D:]


def normed(read, state, gain):
    raw = mm3(read[:, :D], state) + read[:, D:]
    scale = lax.rsqrt(jnp.mean(raw * raw, axis=1, keepdims=True) + 1e-06)
    return (raw * scale * gain).astype(bf16)


def early_output_kernel(gain_ref, *refs):
    read_refs, states, out_ref = refs[:2], refs[2:-1], refs[-1]
    for i in range(VALUE_HEADS - 2):
        side, at = divmod(i, VALUE_HEADS // 2)
        out_ref[i] = normed(read_refs[side][at], states[i // 2][at % 2], gain_ref[...])


def output_kernel(n_sub, gain_ref, read_ref, state_ref, early_ref, out_ref):
    heads = value_heads(key_heads(n_sub, 0)) + value_heads(key_heads(n_sub, 1))
    for i, h in enumerate(heads):
        if i < VALUE_HEADS - 2:
            out = early_ref[i]
        else:
            out = normed(read_ref[i - VALUE_HEADS // 2], state_ref[i % 2], gain_ref[...])
        out_ref[:, pl.ds(pl.multiple_of(h * D, D), D)] = out


def call(kernel, outs, args, scratch=(), specs=None, flops=0, name=None):
    moved = sum(a.size * a.dtype.itemsize for a in args)
    moved += sum(math.prod(o.shape) * o.dtype.itemsize for o in jax.tree.leaves(outs))
    return pl.pallas_call(
        kernel,
        out_shape=outs,
        in_specs=[VMEM] * len(args) if specs is None else specs,
        out_specs=[VMEM] * len(outs) if isinstance(outs, tuple) else VMEM,
        scratch_shapes=list(scratch),
        compiler_params=pltpu.CompilerParams(vmem_limit_bytes=32 * 2**20),
        cost_estimate=pl.CostEstimate(flops=flops, bytes_accessed=moved, transcendentals=0),
        name=name,
    )(*args)


def like(*shape):
    return jax.ShapeDtypeStruct(shape, f32)


def on_device(
    n_dev,
    n_sub,
    queries,
    key_vectors,
    values,
    log_decay,
    write_rate,
    passage_lengths,
    norm_gain,
):
    assert values.shape[0] == BLOCK
    tokens = n_dev * BLOCK
    longest = LONGEST.get(tokens, tokens)
    reach = min(-(-longest // (GROUP * BLOCK)), n_dev // GROUP)
    n = 2
    swap_pairs = [(i, i ^ 1) for i in range(n_dev)]
    next_pairs = [(i, i + GROUP) for i in range(n_dev - GROUP)]

    def chip_pairs(slot):
        return [(i, i ^ (2 * slot)) for i in range(n_dev)]

    def permute(x, pairs):
        return lax.ppermute(x, AXES, pairs)

    step = 2 * BLOCK**3
    half = VALUE_HEADS // 2
    made = (pltpu.VMEM((half, D, 2 * D), f32), pltpu.VMEM((half, BLOCK, BLOCK), f32))
    inputs = (
        passage_lengths,
        key_vectors,
        values,
        log_decay,
        write_rate,
        norm_gain.reshape(1, D),
    )
    send, send_inverse, *held, gain = call(
        functools.partial(first_maps_kernel, n_sub),
        (
            *made,
            *[pltpu.VMEM(x.shape, x.dtype) for x in inputs[1:5]],
            pltpu.VMEM((8, BLOCK), jnp.int32),
            pltpu.VMEM((BLOCK, BLOCK), jnp.int32),
            pltpu.VMEM((1, D), f32),
        ),
        [pltpu.with_memory_space_constraint(x, pltpu.HBM) for x in inputs],
        scratch=[
            pltpu.SMEM(passage_lengths.shape, jnp.int32),
            pltpu.SemaphoreType.DMA((6,)),
        ],
        specs=[HBM] * 6,
        flops=half * 44 * step,
        name="first_maps",
    )
    recv = permute(send, swap_pairs)
    keep, keep_inverse = call(
        functools.partial(second_maps_kernel, n_sub),
        made,
        held,
        flops=half * 44 * step,
        name="second_maps",
    )
    extra = permute(keep, swap_pairs)
    outs = call(
        functools.partial(chip_kernel, n_sub),
        (like(n, D, 2 * D),) * CHIPS,
        (keep, recv),
        flops=half * 6 * step,
        name="chip",
    )
    got = [outs[0]] + [permute(outs[slot], chip_pairs(slot)) for slot in range(1, CHIPS)]
    read = call(
        functools.partial(readout_kernel, n_sub),
        (like(half, BLOCK, 2 * D),) * 2,
        (queries, *held, keep_inverse, send_inverse, recv, extra),
        flops=16 * 13 * step,
        name="readout",
    )
    total_add, *held_maps = call(
        functools.partial(group_kernel, n_sub),
        (like(n, D, D), like(n, 2, D, 2 * D), like(n, D, 2 * D), like(n, D, 2 * D)),
        (*got, read[0]),
        specs=[VMEM] * CHIPS + [ANY],
        scratch=(pltpu.VMEM((CHIPS, n, D, 2 * D), f32),),
        flops=n * 15 * step,
        name="group",
    )
    total_map, ahead = call(
        ahead_kernel,
        (like(n, D, D), like(n, 3, D, 2 * D)),
        held_maps,
        flops=n * 9 * step,
        name="ahead",
    )
    state = total_add
    for _ in range(reach - 1):
        state = permute(state, next_pairs)
        state = call(
            step_kernel,
            like(n, D, D),
            (total_map, total_add, state),
            flops=n * 3 * step,
            name="step",
        )
    state = permute(state, next_pairs)
    outs = call(
        functools.partial(spread_kernel, n_sub),
        (like(n, D, D),) * CHIPS,
        (ahead, state),
        scratch=(pltpu.VMEM((CHIPS, n, D, D), f32),),
        flops=n * 9 * step,
        name="spread",
    )
    own = [outs[0]] + [permute(outs[slot], chip_pairs(slot)) for slot in range(1, CHIPS)]
    other = [permute(x, swap_pairs) for x in own]
    early = call(
        early_output_kernel,
        jax.ShapeDtypeStruct((VALUE_HEADS - 2, BLOCK, D), bf16),
        (gain, *read, *own, *other[:-1]),
        flops=14 * 3 * step,
        name="early_output",
    )
    return call(
        functools.partial(output_kernel, n_sub),
        jax.ShapeDtypeStruct((BLOCK, VALUE_HEADS * D), bf16),
        (gain, read[1], other[-1], early),
        flops=2 * 3 * step,
        name="output",
    )


def solution(mesh):
    n_sub = mesh.shape["sub"]
    n_dev = mesh.shape["seq"] * n_sub
    tokens = P(AXES, None)
    heads = P(None, AXES)
    return jax.shard_map(
        functools.partial(on_device, n_dev, n_sub),
        mesh=mesh,
        in_specs=(tokens, tokens, tokens, heads, heads, P(), P()),
        out_specs=tokens,
        check_vma=False,
    )
```

time: 55.2 us -> 52.8 us (0.957)
  waiting for transfers between devices: 18 us -> 15 us
  Pallas kernels: 18.7 us -> 19.3 us
    ppermute x14, waiting for transfers between devices: 18 us -> 15 us  [permute(): return lax.ppermute(x, AXES, pairs)]
    pallas_call x7 -> x10, Pallas kernels: 18.7 us -> 19.3 us  [call(): pl.pallas_call(kernel, out_shape=outs, in_specs=[VMEM] * len(args) if spe...]
  transfers between devices with their start and end apart: 14 -> 14, of which waited for: 6 -> 5; matrix products, arithmetic and copies ran while one was open for 0% -> 0% of each run, Pallas kernels for 11% -> 21%
where the time goes in v3:
time: 52.8 us; the launch traced here: 52.4 us
  Pallas kernels  19.3 us (37%)
  starting transfers between devices  18 us (34%)
  waiting for transfers between devices  15 us (28%)
    pallas_call x10, Pallas kernels, call(): pl.pallas_call(kernel, out_shape=outs, in_specs=[VMEM] * len(args) if spe...  19.3 us
    ppermute x14, starting transfers between devices, permute(): return lax.ppermute(x, AXES, pairs)  18 us
    ppermute x14, waiting for transfers between devices, permute(): return lax.ppermute(x, AXES, pairs)  15 us
  transfers between devices with their start and end apart: 14, of which 5 were waited for; matrix products, arithmetic and copies ran while one was open for 0% of the time, Pallas kernels for 21%

profile of v3, /device:TPU:25, one launch (start us, length us, event | category | flops | bytes accessed | tf_op | source)
XLA Modules:
  0.0 52.4 jit_solution(9861253312921652176)
XLA Ops:
  0.0 5.8 %first_maps.1 = (f32[8,128,256]{2,1,0:T(8,128)S(1)}, f32[8,128,128]{2,1,0:T(8,128)S(1)}, bf16[128,1024]{1,0:T(8,128)(2,1)S(1)}, bf16[128,2048]{1,0:T(8,128)(2,1)...) custom-call(s32[8]{0:T(128)} %refs_0_.1, ...), custom_call_target="tpu_custom_call" | custom-call | flops 1476395008 | bytes 3249184 | tf_op jit(solution)/shard_map/first_maps/pallas_call | solution.py:389
  5.8 0.7 %collective-permute-start = (f32[8,128,256]{2,1,0:T(8,128)S(1)}, f32[8,128,256]{2,1,0:T(8,128)S(1)}, u32[]{:S(2)}, u32[]{:S(2)}) collective-permute-start(f32[8,128,256]{2,1,0:T(8,128)S(1)} %get-tuple-element.41), channel_id=1, source_target_pairs={{0,1},{1,0},{2,3},{3,2},{4,5},{5,4},{6,7},{7,6},{8,9},{9,8},{10,11... | collective-permute-start | bytes 3145736 | tf_op jit(solution)/shard_map/ppermute | solution.py:428
  6.5 4.5 %second_maps.1 = (f32[8,128,256]{2,1,0:T(8,128)S(1)}, f32[8,128,128]{2,1,0:T(8,128)S(1)}) custom-call(bf16[128,1024]{1,0:T(8,128)(2,1)S(1)} %get-tuple-element.33.refs_0_.k_ref, bf16[128,2048]{1,0:T(8,128)(2,1)S(1)} %get-tuple-element.34.refs_1_.v_ref, f32[16,128]{1,0:T(8,128)S(1)} %get-tuple-element.35.refs_2_.decay_ref, ...), custom_call_target="tpu_custom_call" | custom-call | flops 1476395008 | bytes 2445312 | tf_op jit(solution)/shard_map/second_maps/pallas_call | solution.py:389
  11.0 0.0 copy-start
  11.0 0.1 collective-permute-start.1
  11.1 0.0 collective-permute-done.refs_2_.recv_ref
  11.1 0.5 %chip.1 = (f32[2,128,256]{2,1,0:T(8,128)S(1)}, f32[2,128,256]{2,1,0:T(8,128)S(1)}, f32[2,128,256]{2,1,0:T(8,128)S(1)}, f32[2,128,256]{2,1,0:T(8,128)S(1)}) custom-call(f32[8,128,256]{2,1,0:T(8,128)S(1)} %get-tuple-element.42.keep_ref, f32[8,128,256]{2,1,0:T(8,128)S(1)} %collective-permute-done.refs_2_.recv_ref), custom_call_target="tpu_custom_call" | custom-call | flops 201326592 | bytes 3145728 | tf_op jit(solution)/shard_map/chip/pallas_call | solution.py:389
  11.7 1.3 %collective-permute-start.2 = (f32[2,128,256]{2,1,0:T(8,128)S(1)}, f32[2,128,256]{2,1,0:T(8,128)S(1)}, u32[]{:S(2)}, u32[]{:S(2)}) collective-permute-start(f32[2,128,256]{2,1,0:T(8,128)S(1)} %get-tuple-element.45), channel_id=1, source_target_pairs={{0,2},{1,3},{2,0},{3,1},{4,6},{5,7},{6,4},{7,5},{8,10},{9,11},{10,... | collective-permute-start | bytes 786440 | tf_op jit(solution)/shard_map/ppermute | solution.py:428
  12.9 1.2 %collective-permute-start.3 = (f32[2,128,256]{2,1,0:T(8,128)S(1)}, f32[2,128,256]{2,1,0:T(8,128)S(1)}, u32[]{:S(2)}, u32[]{:S(2)}) collective-permute-start(f32[2,128,256]{2,1,0:T(8,128)S(1)} %get-tuple-element.46), channel_id=1, source_target_pairs={{0,4},{1,5},{2,6},{3,7},{4,0},{5,1},{6,2},{7,3},{8,12},{9,13},{10,... | collective-permute-start | bytes 786440 | tf_op jit(solution)/shard_map/ppermute | solution.py:428
  14.2 0.2 collective-permute-start.4
  14.4 0.0 collective-permute-done.1.refs_3_
  14.4 5.2 %readout.1 = (f32[8,128,256]{2,1,0:T(8,128)S(1)}, f32[8,128,256]{2,1,0:T(8,128)S(1)}) custom-call(bf16[128,1024]{1,0:T(8,128)(2,1)S(1)} %copy-done, bf16[128,1024]{1,0:T(8,128)(2,1)S(1)} %get-tuple-element.33.refs_0_.k_ref, bf16[128,2048]{1,0:T(8,128)(2,1)S(1)} %get-tuple-element.34.refs_1_.v_ref, f32[16,128]{1,0:T(8,128)S(1)} %get-tuple-element.35.refs_2_.decay_ref, ...), custom_call_target="tpu_custom_call" | custom-call | flops 872415232 | bytes 6377472 | tf_op jit(solution)/shard_map/readout/pallas_call | solution.py:389
  19.6 0.4 collective-permute-done.3.r2
  20.0 5.7 %collective-permute-done.4.r3 = f32[2,128,256]{2,1,0:T(8,128)S(1)} collective-permute-done((f32[2,128,256]{2,1,0:T(8,128)S(1)}, f32[2,128,256]{2,1,0:T(8,128)S(1)}, u32[]{:S(2)}, u32[]{:S(2)}) %collective-permute-start.4) | collective-permute-done | bytes 262176 | tf_op jit(solution)/shard_map/ppermute | solution.py:428
  25.7 0.7 %group.1 = (f32[2,128,128]{2,1,0:T(8,128)S(1)}, f32[2,2,128,256]{3,2,1,0:T(8,128)S(1)}, f32[2,128,256]{2,1,0:T(8,128)S(1)}, f32[2,128,256]{2,1,0:T(8,128)S(1)}) custom-call(f32[2,128,256]{2,1,0:T(8,128)S(1)} %get-tuple-element.44.r0, f32[2,128,256]{2,1,0:T(8,128)S(1)} %collective-permute-done.2.r1, f32[2,128,256]{2,1,0:T(8,128)S(1)} %collective-permute-done.3.r2, ...), custom_call_target="tpu_custom_call" | custom-call | flops 125829120 | bytes 3276800 | tf_op jit(solution)/shard_map/group/pallas_call | solution.py:389
  26.4 1.3 %collective-permute-start.5 = (f32[2,128,128]{2,1,0:T(8,128)S(1)}, f32[2,128,128]{2,1,0:T(8,128)S(1)}, u32[]{:S(2)}, u32[]{:S(2)}) collective-permute-start(f32[2,128,128]{2,1,0:T(8,128)S(1)} %get-tuple-element.54.add_ref), channel_id=1, source_target_pairs={{0,8},{1,9},{2,10},{3,11},{4,12},{5,13},{6,14},{7,15},{8,16},{9,17... | collective-permute-start | bytes 393224 | tf_op jit(solution)/shard_map/ppermute | solution.py:428
  27.7 0.3 ahead.1
  28.0 4.1 %collective-permute-done.5.state_ref = f32[2,128,128]{2,1,0:T(8,128)S(1)} collective-permute-done((f32[2,128,128]{2,1,0:T(8,128)S(1)}, f32[2,128,128]{2,1,0:T(8,128)S(1)}, u32[]{:S(2)}, u32[]{:S(2)}) %collective-permute-start.5) | collective-permute-done | bytes 131104 | tf_op jit(solution)/shard_map/ppermute | solution.py:428
  32.2 0.2 step.1
  32.4 1.3 %collective-permute-start.6 = (f32[2,128,128]{2,1,0:T(8,128)S(1)}, f32[2,128,128]{2,1,0:T(8,128)S(1)}, u32[]{:S(2)}, u32[]{:S(2)}) collective-permute-start(f32[2,128,128]{2,1,0:T(8,128)S(1)} %step.1), channel_id=1, source_target_pairs={{0,8},{1,9},{2,10},{3,11},{4,12},{5,13},{6,14},{7,15},{8,16},{9,17... | collective-permute-start | bytes 393224 | tf_op jit(solution)/shard_map/ppermute | solution.py:428
  33.7 4.4 %collective-permute-done.6.state_ref = f32[2,128,128]{2,1,0:T(8,128)S(1)} collective-permute-done((f32[2,128,128]{2,1,0:T(8,128)S(1)}, f32[2,128,128]{2,1,0:T(8,128)S(1)}, u32[]{:S(2)}, u32[]{:S(2)}) %collective-permute-start.6) | collective-permute-done | bytes 131104 | tf_op jit(solution)/shard_map/ppermute | solution.py:428
  38.1 0.3 spread.1
  38.4 1.2 %collective-permute-start.9 = (f32[2,128,128]{2,1,0:T(8,128)S(1)}, f32[2,128,128]{2,1,0:T(8,128)S(1)}, u32[]{:S(2)}, u32[]{:S(2)}) collective-permute-start(f32[2,128,128]{2,1,0:T(8,128)S(1)} %get-tuple-element.57), channel_id=1, source_target_pairs={{0,2},{1,3},{2,0},{3,1},{4,6},{5,7},{6,4},{7,5},{8,10},{9,11},{10,... | collective-permute-start | bytes 393224 | tf_op jit(solution)/shard_map/ppermute | solution.py:428
  39.6 0.3 collective-permute-start.10
  39.9 1.2 %collective-permute-start.7 = (f32[2,128,128]{2,1,0:T(8,128)S(1)}, f32[2,128,128]{2,1,0:T(8,128)S(1)}, u32[]{:S(2)}, u32[]{:S(2)}) collective-permute-start(f32[2,128,128]{2,1,0:T(8,128)S(1)} %get-tuple-element.55), channel_id=1, source_target_pairs={{0,6},{1,7},{2,4},{3,5},{4,2},{5,3},{6,0},{7,1},{8,14},{9,15},{10,... | collective-permute-start | bytes 393224 | tf_op jit(solution)/shard_map/ppermute | solution.py:428
  41.1 4.7 %collective-permute-start.11 = (f32[2,128,128]{2,1,0:T(8,128)S(1)}, f32[2,128,128]{2,1,0:T(8,128)S(1)}, u32[]{:S(2)}, u32[]{:S(2)}) collective-permute-start(f32[2,128,128]{2,1,0:T(8,128)S(1)} %get-tuple-element.56.refs_2_), channel_id=1, source_target_pairs={{0,1},{1,0},{2,3},{3,2},{4,5},{5,4},{6,7},{7,6},{8,9},{9,8},{10,11... | collective-permute-start | bytes 393224 | tf_op jit(solution)/shard_map/ppermute | solution.py:428
  45.8 1.5 %collective-permute-start.12 = (f32[2,128,128]{2,1,0:T(8,128)S(1)}, f32[2,128,128]{2,1,0:T(8,128)S(1)}, u32[]{:S(2)}, u32[]{:S(2)}) collective-permute-start(f32[2,128,128]{2,1,0:T(8,128)S(1)} %collective-permute-done.9.refs_3_), channel_id=1, source_target_pairs={{0,1},{1,0},{2,3},{3,2},{4,5},{5,4},{6,7},{7,6},{8,9},{9,8},{10,11... | collective-permute-start | bytes 393224 | tf_op jit(solution)/shard_map/ppermute | solution.py:428
  47.3 1.2 %collective-permute-start.13 = (f32[2,128,128]{2,1,0:T(8,128)S(1)}, f32[2,128,128]{2,1,0:T(8,128)S(1)}, u32[]{:S(2)}, u32[]{:S(2)}) collective-permute-start(f32[2,128,128]{2,1,0:T(8,128)S(1)} %collective-permute-done.10.refs_4_), channel_id=1, source_target_pairs={{0,1},{1,0},{2,3},{3,2},{4,5},{5,4},{6,7},{7,6},{8,9},{9,8},{10,11... | collective-permute-start | bytes 393224 | tf_op jit(solution)/shard_map/ppermute | solution.py:428
  48.5 1.7 %collective-permute-start.8 = (f32[2,128,128]{2,1,0:T(8,128)S(1)}, f32[2,128,128]{2,1,0:T(8,128)S(1)}, u32[]{:S(2)}, u32[]{:S(2)}) collective-permute-start(f32[2,128,128]{2,1,0:T(8,128)S(1)} %collective-permute-done.7.refs_5_), channel_id=1, source_target_pairs={{0,1},{1,0},{2,3},{3,2},{4,5},{5,4},{6,7},{7,6},{8,9},{9,8},{10,11... | collective-permute-start | bytes 393224 | tf_op jit(solution)/shard_map/ppermute | solution.py:428
  50.3 0.6 %early_output.1.early_ref = bf16[14,128,128]{2,1,0:T(8,128)(2,1)S(1)} custom-call(f32[1,128]{1,0:T(1,128)S(1)} %get-tuple-element.32.gain_ref, f32[8,128,256]{2,1,0:T(8,128)S(1)} %get-tuple-element.48.after_ref.refs_0_, f32[8,128,256]{2,1,0:T(8,128)S(1)} %get-tuple-element.43.refs_1_.read_ref, f32[2,128,128]{2,1,0:T(8,128)S(1)} %get-tuple-element.56.refs_2_, ...), custom_call_target="tpu_custom_call" | custom-call | flops 176160768 | bytes 3473920 | tf_op jit(solution)/shard_map/early_output/pallas_call | solution.py:389
  50.9 0.4 collective-permute-done.8.state_ref
  51.3 1.1 %output.1 = bf16[128,2048]{1,0:T(8,128)(2,1)} custom-call(f32[1,128]{1,0:T(1,128)S(1)} %get-tuple-element.32.gain_ref, f32[8,128,256]{2,1,0:T(8,128)S(1)} %get-tuple-element.43.refs_1_.read_ref, f32[2,128,128]{2,1,0:T(8,128)S(1)} %collective-permute-done.8.state_ref, bf16[14,128,128]{2,1,0:T(8,128)(2,1)S(1)} %early_output.1.early_ref), custom_call_target="tpu_custom_call" | custom-call | flops 25165824 | bytes 2163200 | tf_op jit(solution)/shard_map/output/pallas_call | solution.py:389
  (8 shorter events, 0.0 us)
Async XLA Ops:
  5.8 5.3 %collective-permute-start = (f32[8,128,256]{2,1,0:T(8,128)S(1)}, f32[8,128,256]{2,1,0:T(8,128)S(1)}, u32[]{:S(2)}, u32[]{:S(2)}) collective-permute-start(f32[8,128,256]{2,1,0:T(8,128)S(1)} %get-tuple-element.41), channel_id=1, source_target_pairs={{0,1},{1,0},{2,3},{3,2},{4,5},{5,4},{6,7},{7,6},{8,9},{9,8},{10,11... | collective-permute-start | bytes 3145736 | tf_op jit(solution)/shard_map/ppermute | solution.py:428
  11.0 3.4 %copy-start = (bf16[128,1024]{1,0:T(8,128)(2,1)S(1)}, bf16[128,1024]{1,0:T(8,128)(2,1)}, u32[]{:S(2)}) copy-start(bf16[128,1024]{1,0:T(8,128)(2,1)} %q_ref.1) | copy-start | bytes 786436
  11.0 3.4 %collective-permute-start.1 = (f32[8,128,256]{2,1,0:T(8,128)S(1)}, f32[8,128,256]{2,1,0:T(8,128)S(1)}, u32[]{:S(2)}, u32[]{:S(2)}) collective-permute-start(f32[8,128,256]{2,1,0:T(8,128)S(1)} %get-tuple-element.42.keep_ref), channel_id=1, source_target_pairs={{0,1},{1,0},{2,3},{3,2},{4,5},{5,4},{6,7},{7,6},{8,9},{9,8},{10,11... | collective-permute-start | bytes 3145736 | tf_op jit(solution)/shard_map/ppermute | solution.py:428
  11.7 8.0 %collective-permute-start.2 = (f32[2,128,256]{2,1,0:T(8,128)S(1)}, f32[2,128,256]{2,1,0:T(8,128)S(1)}, u32[]{:S(2)}, u32[]{:S(2)}) collective-permute-start(f32[2,128,256]{2,1,0:T(8,128)S(1)} %get-tuple-element.45), channel_id=1, source_target_pairs={{0,2},{1,3},{2,0},{3,1},{4,6},{5,7},{6,4},{7,5},{8,10},{9,11},{10,... | collective-permute-start | bytes 786440 | tf_op jit(solution)/shard_map/ppermute | solution.py:428
  12.9 7.1 %collective-permute-start.3 = (f32[2,128,256]{2,1,0:T(8,128)S(1)}, f32[2,128,256]{2,1,0:T(8,128)S(1)}, u32[]{:S(2)}, u32[]{:S(2)}) collective-permute-start(f32[2,128,256]{2,1,0:T(8,128)S(1)} %get-tuple-element.46), channel_id=1, source_target_pairs={{0,4},{1,5},{2,6},{3,7},{4,0},{5,1},{6,2},{7,3},{8,12},{9,13},{10,... | collective-permute-start | bytes 786440 | tf_op jit(solution)/shard_map/ppermute | solution.py:428
  14.2 11.6 %collective-permute-start.4 = (f32[2,128,256]{2,1,0:T(8,128)S(1)}, f32[2,128,256]{2,1,0:T(8,128)S(1)}, u32[]{:S(2)}, u32[]{:S(2)}) collective-permute-start(f32[2,128,256]{2,1,0:T(8,128)S(1)} %get-tuple-element.47), channel_id=1, source_target_pairs={{0,6},{1,7},{2,4},{3,5},{4,2},{5,3},{6,0},{7,1},{8,14},{9,15},{10,... | collective-permute-start | bytes 786440 | tf_op jit(solution)/shard_map/ppermute | solution.py:428
  26.4 5.7 %collective-permute-start.5 = (f32[2,128,128]{2,1,0:T(8,128)S(1)}, f32[2,128,128]{2,1,0:T(8,128)S(1)}, u32[]{:S(2)}, u32[]{:S(2)}) collective-permute-start(f32[2,128,128]{2,1,0:T(8,128)S(1)} %get-tuple-element.54.add_ref), channel_id=1, source_target_pairs={{0,8},{1,9},{2,10},{3,11},{4,12},{5,13},{6,14},{7,15},{8,16},{9,17... | collective-permute-start | bytes 393224 | tf_op jit(solution)/shard_map/ppermute | solution.py:428
  32.4 5.7 %collective-permute-start.6 = (f32[2,128,128]{2,1,0:T(8,128)S(1)}, f32[2,128,128]{2,1,0:T(8,128)S(1)}, u32[]{:S(2)}, u32[]{:S(2)}) collective-permute-start(f32[2,128,128]{2,1,0:T(8,128)S(1)} %step.1), channel_id=1, source_target_pairs={{0,8},{1,9},{2,10},{3,11},{4,12},{5,13},{6,14},{7,15},{8,16},{9,17... | collective-permute-start | bytes 393224 | tf_op jit(solution)/shard_map/ppermute | solution.py:428
  38.4 7.4 %collective-permute-start.9 = (f32[2,128,128]{2,1,0:T(8,128)S(1)}, f32[2,128,128]{2,1,0:T(8,128)S(1)}, u32[]{:S(2)}, u32[]{:S(2)}) collective-permute-start(f32[2,128,128]{2,1,0:T(8,128)S(1)} %get-tuple-element.57), channel_id=1, source_target_pairs={{0,2},{1,3},{2,0},{3,1},{4,6},{5,7},{6,4},{7,5},{8,10},{9,11},{10,... | collective-permute-start | bytes 393224 | tf_op jit(solution)/shard_map/ppermute | solution.py:428
  39.6 7.6 %collective-permute-start.10 = (f32[2,128,128]{2,1,0:T(8,128)S(1)}, f32[2,128,128]{2,1,0:T(8,128)S(1)}, u32[]{:S(2)}, u32[]{:S(2)}) collective-permute-start(f32[2,128,128]{2,1,0:T(8,128)S(1)} %get-tuple-element.58), channel_id=1, source_target_pairs={{0,4},{1,5},{2,6},{3,7},{4,0},{5,1},{6,2},{7,3},{8,12},{9,13},{10,... | collective-permute-start | bytes 393224 | tf_op jit(solution)/shard_map/ppermute | solution.py:428
  39.9 8.6 %collective-permute-start.7 = (f32[2,128,128]{2,1,0:T(8,128)S(1)}, f32[2,128,128]{2,1,0:T(8,128)S(1)}, u32[]{:S(2)}, u32[]{:S(2)}) collective-permute-start(f32[2,128,128]{2,1,0:T(8,128)S(1)} %get-tuple-element.55), channel_id=1, source_target_pairs={{0,6},{1,7},{2,4},{3,5},{4,2},{5,3},{6,0},{7,1},{8,14},{9,15},{10,... | collective-permute-start | bytes 393224 | tf_op jit(solution)/shard_map/ppermute | solution.py:428
  41.1 9.1 %collective-permute-start.11 = (f32[2,128,128]{2,1,0:T(8,128)S(1)}, f32[2,128,128]{2,1,0:T(8,128)S(1)}, u32[]{:S(2)}, u32[]{:S(2)}) collective-permute-start(f32[2,128,128]{2,1,0:T(8,128)S(1)} %get-tuple-element.56.refs_2_), channel_id=1, source_target_pairs={{0,1},{1,0},{2,3},{3,2},{4,5},{5,4},{6,7},{7,6},{8,9},{9,8},{10,11... | collective-permute-start | bytes 393224 | tf_op jit(solution)/shard_map/ppermute | solution.py:428
  45.8 4.5 %collective-permute-start.12 = (f32[2,128,128]{2,1,0:T(8,128)S(1)}, f32[2,128,128]{2,1,0:T(8,128)S(1)}, u32[]{:S(2)}, u32[]{:S(2)}) collective-permute-start(f32[2,128,128]{2,1,0:T(8,128)S(1)} %collective-permute-done.9.refs_3_), channel_id=1, source_target_pairs={{0,1},{1,0},{2,3},{3,2},{4,5},{5,4},{6,7},{7,6},{8,9},{9,8},{10,11... | collective-permute-start | bytes 393224 | tf_op jit(solution)/shard_map/ppermute | solution.py:428
  47.3 3.0 %collective-permute-start.13 = (f32[2,128,128]{2,1,0:T(8,128)S(1)}, f32[2,128,128]{2,1,0:T(8,128)S(1)}, u32[]{:S(2)}, u32[]{:S(2)}) collective-permute-start(f32[2,128,128]{2,1,0:T(8,128)S(1)} %collective-permute-done.10.refs_4_), channel_id=1, source_target_pairs={{0,1},{1,0},{2,3},{3,2},{4,5},{5,4},{6,7},{7,6},{8,9},{9,8},{10,11... | collective-permute-start | bytes 393224 | tf_op jit(solution)/shard_map/ppermute | solution.py:428
  48.5 2.7 %collective-permute-start.8 = (f32[2,128,128]{2,1,0:T(8,128)S(1)}, f32[2,128,128]{2,1,0:T(8,128)S(1)}, u32[]{:S(2)}, u32[]{:S(2)}) collective-permute-start(f32[2,128,128]{2,1,0:T(8,128)S(1)} %collective-permute-done.7.refs_5_), channel_id=1, source_target_pairs={{0,1},{1,0},{2,3},{3,2},{4,5},{5,4},{6,7},{7,6},{8,9},{9,8},{10,11... | collective-permute-start | bytes 393224 | tf_op jit(solution)/shard_map/ppermute | solution.py:428

commit v4 on v3

--- a/solution.py
+++ b/solution.py
@@ -69,6 +69,12 @@
     rows = a[0].shape[0]
     out = mm(jnp.concatenate(a, axis=0), across(*b))
     return out[:rows, :D] + (out[:rows, D:] + out[rows:, :D])
+
+
+def mm_long(a, b):
+    return mm(
+        jnp.concatenate([a[0], a[1], a[0]], axis=1), jnp.concatenate([b[0], b[0], b[1]], axis=0)
+    )
 
 
 def mm_half(a, b):
@@ -132,6 +138,12 @@
     return sum_row, sum_col, rate_row, rate_col
 
 
+def gates_of(side, *refs):
+    at = slice(side * VALUE_HEADS // 2, (side + 1) * VALUE_HEADS // 2)
+    sum_row, sum_col, rate_row, rate_col = refs
+    return sum_row[at, :], sum_col[:, at], rate_row[at, :], rate_col[:, at]
+
+
 def columns(ref, at):
     return ref[:, pl.ds(pl.multiple_of(at * D, D), D)]
 
@@ -172,17 +184,21 @@
     parts = [split(n) for n in systems]
     near = near.astype(f32).astype(bf16)
     powers = [(high * near, low * near) for high, low in parts]
-    powers = [split(fold(mm(across(*n), square(*n)))) for n in powers]
-    for last in (False, False, True):
-        if last:
-            solved = [s + fold(mm(left(s), square(*n))) for s, n in zip(solved, powers)]
-        else:
-            both = [
-                fold(mm(jnp.concatenate([across(*n), left(s)], axis=0), square(*n)))
-                for n, s in zip(powers, solved)
-            ]
-            powers = [split(x[:BLOCK]) for x in both]
-            solved = [s + x[BLOCK:] for s, x in zip(solved, both)]
+    powers = [split(mm_long(n, n)) for n in powers]
+    both = [fold(mm(jnp.concatenate([across(*n), left(s)], axis=0), square(*n))) for n, s in zip(powers, solved)]
+    fourth = [odd_rows(x[:BLOCK], 8) for x in both]
+    powers = [split(x[:BLOCK]) for x in both]
+    solved = [s + x[BLOCK:] for s, x in zip(solved, both)]
+    both = [
+        fold(mm(jnp.concatenate([left(q), left(s)], axis=0), square(*n)))
+        for q, n, s in zip(fourth, powers, solved)
+    ]
+    zero = jnp.zeros((BLOCK, BLOCK), f32)
+    powers = [split(with_odd_rows(zero, x[: BLOCK // 2], 8)) for x in both]
+    solved = [s + x[BLOCK // 2 :] for s, x in zip(solved, both)]
+    rows = [odd_rows(s, 8) for s in solved]
+    rows = [r + mm_long(split(r), n) for r, n in zip(rows, powers)]
+    solved = [with_odd_rows(s, r, 8) for s, r in zip(solved, rows)]
     size = 16
     zero = jnp.zeros((BLOCK, BLOCK), bf16)
     while size < BLOCK:
@@ -190,11 +206,11 @@
         band = odd_rows(band.astype(f32), size).astype(bf16)
         pairs = [split(s) for s in solved]
         products = [
-            split(mm_tall([odd_rows(p, size) * band for p in n], s))
+            split(mm_long([odd_rows(p, size) * band for p in n], s))
             for n, s in zip(parts, pairs)
         ]
         fulls = [[with_odd_rows(zero, p, size) for p in u] for u in products]
-        rows = [mm_tall([odd_rows(p, size) for p in s], u) for s, u in zip(pairs, fulls)]
+        rows = [mm_long([odd_rows(p, size) for p in s], u) for s, u in zip(pairs, fulls)]
         solved = [
             with_odd_rows(s, odd_rows(s, size) - r, size) for s, r in zip(solved, rows)
         ]
@@ -203,9 +219,10 @@
 
 
 def first_maps_kernel(n_sub, *refs):
-    sources, outs, (gain_ref, lengths_ref, sems) = refs[:6], refs[6:14], refs[14:]
-    row_ref, col_ref = outs[6:]
-    targets = (lengths_ref, *outs[2:6], gain_ref)
+    sources, outs, refs = refs[:6], refs[6:16], refs[16:]
+    gain_ref, lengths_ref, decay_ref, rate_ref, sems = refs
+    row_ref, col_ref = outs[8:]
+    targets = (lengths_ref, *outs[2:4], decay_ref, rate_ref, gain_ref)
     copies = [
         pltpu.make_async_copy(a, b, sems.at[i]) for i, (a, b) in enumerate(zip(sources, targets))
     ]
@@ -218,6 +235,9 @@
     col_ref[...] = jnp.zeros((BLOCK, BLOCK), jnp.int32) + col
     for i in (1, 3, 4, 5):
         copies[i].wait()
+    heads = value_heads(key_heads(n_sub, 0)) + value_heads(key_heads(n_sub, 1))
+    for ref, gate in zip(outs[4:8], gates(heads, decay_ref, rate_ref)):
+        ref[...] = gate
     make_maps(1, n_sub, *outs[2:], *outs[:2], copies[2].wait)
 
 
@@ -226,13 +246,13 @@
 
 
 def make_maps(
-    side, n_sub, k_ref, v_ref, decay_ref, rate_ref, row_ref, col_ref, map_ref, inverse_ref, values_in
+    side, n_sub, k_ref, v_ref, g0, g1, g2, g3, row_ref, col_ref, map_ref, inverse_ref, values_in
 ):
     keys = key_heads(n_sub, side)
     heads = value_heads(keys)
     seg_row, before = row_ref[0:1], row_ref[1:2]
     seg_col = col_ref[:, 0:1]
-    sum_row, sum_col, rate_row, rate_col = gates(heads, decay_ref, rate_ref)
+    sum_row, sum_col, rate_row, rate_col = gates_of(side, g0, g1, g2, g3)
     apart = iota(0) ^ iota(1)
     strict = (iota(0) > iota(1)) & (seg_row == col_ref[...])
     eye = (apart == 0).astype(f32)
@@ -258,13 +278,10 @@
     values_in()
     for i, (key, key_t, n_row, b_row, from_row, end) in enumerate(details):
         inverse_ref[i] = solved[i]
-        middle = solved[i] * end
-        wy = mm_half(split(middle * (b_row * from_row * n_row)), key)
-        fresh = mm_half(split(middle * b_row), columns(v_ref, heads[i]))
-        high, low = split(across(wy, fresh))
-        both = mm(across(key_t, key_t), jnp.concatenate([high, low], axis=0))
-        map_ref[i, :, :D] = from_row[:, BLOCK - 1 :] * eye - both[:, :D]
-        map_ref[i, :, D:] = both[:, D:]
+        through = fold(mm(key_t, across(*split(solved[i] * end))))
+        mapped = mm_half(split(through * (b_row * from_row * n_row)), key)
+        map_ref[i, :, :D] = from_row[:, BLOCK - 1 :] * eye - mapped
+        map_ref[i, :, D:] = mm_half(split(through * b_row), columns(v_ref, heads[i]))
 
 
 def chip_kernel(n_sub, keep_ref, recv_ref, *out_refs):
@@ -319,7 +336,8 @@
         ref[...] = held[chip ^ slot]
 
 
-def readout_kernel(n_sub, q_ref, k_ref, v_ref, decay_ref, rate_ref, row_ref, col_ref, *refs):
+def readout_kernel(n_sub, q_ref, k_ref, v_ref, *refs):
+    gate_refs, (row_ref, col_ref), refs = refs[:4], refs[4:6], refs[6:]
     inverse_refs, early_refs, read_refs = refs[:2], refs[2:4], refs[4:]
     core = lax.rem(my_rank(n_sub), 2)
     seg_row, before = row_ref[0:1], row_ref[1:2]
@@ -329,7 +347,7 @@
     for side in range(2):
         keys = key_heads(n_sub, side)
         heads = value_heads(keys)
-        sum_row, sum_col, rate_row, _ = gates(heads, decay_ref, rate_ref)
+        sum_row, sum_col, rate_row, _ = gates_of(side, *gate_refs)
         for j, key_head in enumerate(keys):
             key = columns(k_ref, key_head)
             key_t = key.T
@@ -442,7 +460,8 @@
         functools.partial(first_maps_kernel, n_sub),
         (
             *made,
-            *[pltpu.VMEM(x.shape, x.dtype) for x in inputs[1:5]],
+            *[pltpu.VMEM(x.shape, x.dtype) for x in inputs[1:3]],
+            *[pltpu.VMEM(shape, f32) for shape in 2 * ((VALUE_HEADS, BLOCK), (BLOCK, VALUE_HEADS))],
             pltpu.VMEM((8, BLOCK), jnp.int32),
             pltpu.VMEM((BLOCK, BLOCK), jnp.int32),
             pltpu.VMEM((1, D), f32),
@@ -450,6 +469,8 @@
         [pltpu.with_memory_space_constraint(x, pltpu.HBM) for x in inputs],
         scratch=[
             pltpu.SMEM(passage_lengths.shape, jnp.int32),
+            pltpu.VMEM(log_decay.shape, f32),
+            pltpu.VMEM(write_rate.shape, f32),
             pltpu.SemaphoreType.DMA((6,)),
         ],
         specs=[HBM] * 6,

time: 52.8 us -> 51.8 us (0.981)
  Pallas kernels: 19.3 us -> 17.8 us
    pallas_call x10, Pallas kernels: 19.3 us -> 17.8 us  [call(): pl.pallas_call(kernel, out_shape=outs, in_specs=[VMEM] * len(args) if spe...]
  transfers between devices with their start and end apart: 14 -> 14, of which waited for: 5 -> 5; matrix products, arithmetic and copies ran while one was open for 0% -> 0% of each run, Pallas kernels for 21% -> 20%
where the time goes in v4:
time: 51.8 us; the launch traced here: 51.4 us
  starting transfers between devices  18 us (35%)
  Pallas kernels  17.8 us (34%)
  waiting for transfers between devices  15.5 us (30%)
    ppermute x14, starting transfers between devices, permute(): return lax.ppermute(x, AXES, pairs)  18 us
    pallas_call x10, Pallas kernels, call(): pl.pallas_call(kernel, out_shape=outs, in_specs=[VMEM] * len(args) if spe...  17.8 us
    ppermute x14, waiting for transfers between devices, permute(): return lax.ppermute(x, AXES, pairs)  15.5 us
  transfers between devices with their start and end apart: 14, of which 5 were waited for; matrix products, arithmetic and copies ran while one was open for 0% of the time, Pallas kernels for 20%

profile of v4, /device:TPU:25, one launch (start us, length us, event | category | flops | bytes accessed | tf_op | source)
XLA Modules:
  0.0 51.4 jit_solution(16101314602506127487)
XLA Ops:
  0.0 5.4 %first_maps.1 = (f32[8,128,256]{2,1,0:T(8,128)S(1)}, f32[8,128,128]{2,1,0:T(8,128)S(1)}, bf16[128,1024]{1,0:T(8,128)(2,1)S(1)}, bf16[128,2048]{1,0:T(8,128)(2,1)...) custom-call(s32[8]{0:T(128)} %refs_0_.1, ...), custom_call_target="tpu_custom_call" | custom-call | flops 1476395008 | bytes 3265568 | tf_op jit(solution)/shard_map/first_maps/pallas_call | solution.py:407
  5.4 0.7 %collective-permute-start = (f32[8,128,256]{2,1,0:T(8,128)S(1)}, f32[8,128,256]{2,1,0:T(8,128)S(1)}, u32[]{:S(2)}, u32[]{:S(2)}) collective-permute-start(f32[8,128,256]{2,1,0:T(8,128)S(1)} %get-tuple-element.45), channel_id=1, source_target_pairs={{0,1},{1,0},{2,3},{3,2},{4,5},{5,4},{6,7},{7,6},{8,9},{9,8},{10,11... | collective-permute-start | bytes 3145736 | tf_op jit(solution)/shard_map/ppermute | solution.py:446
  6.1 3.9 %second_maps.1 = (f32[8,128,256]{2,1,0:T(8,128)S(1)}, f32[8,128,128]{2,1,0:T(8,128)S(1)}) custom-call(bf16[128,1024]{1,0:T(8,128)(2,1)S(1)} %get-tuple-element.35.refs_0_.k_ref, bf16[128,2048]{1,0:T(8,128)(2,1)S(1)} %get-tuple-element.36.refs_1_.v_ref, f32[16,128]{1,0:T(8,128)S(1)} %get-tuple-element.37.refs_2_.refs_0_, ...), custom_call_target="tpu_custom_call" | custom-call | flops 1476395008 | bytes 2461696 | tf_op jit(solution)/shard_map/second_maps/pallas_call | solution.py:407
  10.0 0.0 copy-start
  10.0 0.1 collective-permute-start.1
  10.1 0.0 collective-permute-done.refs_8_.recv_ref
  10.1 0.5 %chip.1 = (f32[2,128,256]{2,1,0:T(8,128)S(1)}, f32[2,128,256]{2,1,0:T(8,128)S(1)}, f32[2,128,256]{2,1,0:T(8,128)S(1)}, f32[2,128,256]{2,1,0:T(8,128)S(1)}) custom-call(f32[8,128,256]{2,1,0:T(8,128)S(1)} %get-tuple-element.46.keep_ref, f32[8,128,256]{2,1,0:T(8,128)S(1)} %collective-permute-done.refs_8_.recv_ref), custom_call_target="tpu_custom_call" | custom-call | flops 201326592 | bytes 3145728 | tf_op jit(solution)/shard_map/chip/pallas_call | solution.py:407
  10.6 1.3 %collective-permute-start.2 = (f32[2,128,256]{2,1,0:T(8,128)S(1)}, f32[2,128,256]{2,1,0:T(8,128)S(1)}, u32[]{:S(2)}, u32[]{:S(2)}) collective-permute-start(f32[2,128,256]{2,1,0:T(8,128)S(1)} %get-tuple-element.49), channel_id=1, source_target_pairs={{0,2},{1,3},{2,0},{3,1},{4,6},{5,7},{6,4},{7,5},{8,10},{9,11},{10,... | collective-permute-start | bytes 786440 | tf_op jit(solution)/shard_map/ppermute | solution.py:446
  11.9 1.2 %collective-permute-start.3 = (f32[2,128,256]{2,1,0:T(8,128)S(1)}, f32[2,128,256]{2,1,0:T(8,128)S(1)}, u32[]{:S(2)}, u32[]{:S(2)}) collective-permute-start(f32[2,128,256]{2,1,0:T(8,128)S(1)} %get-tuple-element.50), channel_id=1, source_target_pairs={{0,4},{1,5},{2,6},{3,7},{4,0},{5,1},{6,2},{7,3},{8,12},{9,13},{10,... | collective-permute-start | bytes 786440 | tf_op jit(solution)/shard_map/ppermute | solution.py:446
  13.2 0.2 collective-permute-start.4
  13.4 0.0 collective-permute-done.1.refs_9_
  13.4 4.8 %readout.1 = (f32[8,128,256]{2,1,0:T(8,128)S(1)}, f32[8,128,256]{2,1,0:T(8,128)S(1)}) custom-call(bf16[128,1024]{1,0:T(8,128)(2,1)S(1)} %copy-done, bf16[128,1024]{1,0:T(8,128)(2,1)S(1)} %get-tuple-element.35.refs_0_.k_ref, bf16[128,2048]{1,0:T(8,128)(2,1)S(1)} %get-tuple-element.36.refs_1_.v_ref, f32[16,128]{1,0:T(8,128)S(1)} %get-tuple-element.37.refs_2_.refs_0_, ...), custom_call_target="tpu_custom_call" | custom-call | flops 872415232 | bytes 6393856 | tf_op jit(solution)/shard_map/readout/pallas_call | solution.py:407
  18.2 0.8 %collective-permute-done.3.r2 = f32[2,128,256]{2,1,0:T(8,128)S(1)} collective-permute-done((f32[2,128,256]{2,1,0:T(8,128)S(1)}, f32[2,128,256]{2,1,0:T(8,128)S(1)}, u32[]{:S(2)}, u32[]{:S(2)}) %collective-permute-start.3) | collective-permute-done | bytes 262176 | tf_op jit(solution)/shard_map/ppermute | solution.py:446
  19.0 5.7 %collective-permute-done.4.r3 = f32[2,128,256]{2,1,0:T(8,128)S(1)} collective-permute-done((f32[2,128,256]{2,1,0:T(8,128)S(1)}, f32[2,128,256]{2,1,0:T(8,128)S(1)}, u32[]{:S(2)}, u32[]{:S(2)}) %collective-permute-start.4) | collective-permute-done | bytes 262176 | tf_op jit(solution)/shard_map/ppermute | solution.py:446
  24.7 0.7 %group.1 = (f32[2,128,128]{2,1,0:T(8,128)S(1)}, f32[2,2,128,256]{3,2,1,0:T(8,128)S(1)}, f32[2,128,256]{2,1,0:T(8,128)S(1)}, f32[2,128,256]{2,1,0:T(8,128)S(1)}) custom-call(f32[2,128,256]{2,1,0:T(8,128)S(1)} %get-tuple-element.48.r0, f32[2,128,256]{2,1,0:T(8,128)S(1)} %collective-permute-done.2.r1, f32[2,128,256]{2,1,0:T(8,128)S(1)} %collective-permute-done.3.r2, ...), custom_call_target="tpu_custom_call" | custom-call | flops 125829120 | bytes 3276800 | tf_op jit(solution)/shard_map/group/pallas_call | solution.py:407
  25.4 1.3 %collective-permute-start.5 = (f32[2,128,128]{2,1,0:T(8,128)S(1)}, f32[2,128,128]{2,1,0:T(8,128)S(1)}, u32[]{:S(2)}, u32[]{:S(2)}) collective-permute-start(f32[2,128,128]{2,1,0:T(8,128)S(1)} %get-tuple-element.58.add_ref), channel_id=1, source_target_pairs={{0,8},{1,9},{2,10},{3,11},{4,12},{5,13},{6,14},{7,15},{8,16},{9,17... | collective-permute-start | bytes 393224 | tf_op jit(solution)/shard_map/ppermute | solution.py:446
  26.7 0.3 ahead.1
  27.0 4.1 %collective-permute-done.5.state_ref = f32[2,128,128]{2,1,0:T(8,128)S(1)} collective-permute-done((f32[2,128,128]{2,1,0:T(8,128)S(1)}, f32[2,128,128]{2,1,0:T(8,128)S(1)}, u32[]{:S(2)}, u32[]{:S(2)}) %collective-permute-start.5) | collective-permute-done | bytes 131104 | tf_op jit(solution)/shard_map/ppermute | solution.py:446
  31.2 0.2 step.1
  31.4 1.3 %collective-permute-start.6 = (f32[2,128,128]{2,1,0:T(8,128)S(1)}, f32[2,128,128]{2,1,0:T(8,128)S(1)}, u32[]{:S(2)}, u32[]{:S(2)}) collective-permute-start(f32[2,128,128]{2,1,0:T(8,128)S(1)} %step.1), channel_id=1, source_target_pairs={{0,8},{1,9},{2,10},{3,11},{4,12},{5,13},{6,14},{7,15},{8,16},{9,17... | collective-permute-start | bytes 393224 | tf_op jit(solution)/shard_map/ppermute | solution.py:446
  32.7 4.4 %collective-permute-done.6.state_ref = f32[2,128,128]{2,1,0:T(8,128)S(1)} collective-permute-done((f32[2,128,128]{2,1,0:T(8,128)S(1)}, f32[2,128,128]{2,1,0:T(8,128)S(1)}, u32[]{:S(2)}, u32[]{:S(2)}) %collective-permute-start.6) | collective-permute-done | bytes 131104 | tf_op jit(solution)/shard_map/ppermute | solution.py:446
  37.1 0.3 spread.1
  37.4 1.2 %collective-permute-start.9 = (f32[2,128,128]{2,1,0:T(8,128)S(1)}, f32[2,128,128]{2,1,0:T(8,128)S(1)}, u32[]{:S(2)}, u32[]{:S(2)}) collective-permute-start(f32[2,128,128]{2,1,0:T(8,128)S(1)} %get-tuple-element.61), channel_id=1, source_target_pairs={{0,2},{1,3},{2,0},{3,1},{4,6},{5,7},{6,4},{7,5},{8,10},{9,11},{10,... | collective-permute-start | bytes 393224 | tf_op jit(solution)/shard_map/ppermute | solution.py:446
  38.6 0.3 collective-permute-start.10
  39.0 1.2 %collective-permute-start.7 = (f32[2,128,128]{2,1,0:T(8,128)S(1)}, f32[2,128,128]{2,1,0:T(8,128)S(1)}, u32[]{:S(2)}, u32[]{:S(2)}) collective-permute-start(f32[2,128,128]{2,1,0:T(8,128)S(1)} %get-tuple-element.59), channel_id=1, source_target_pairs={{0,6},{1,7},{2,4},{3,5},{4,2},{5,3},{6,0},{7,1},{8,14},{9,15},{10,... | collective-permute-start | bytes 393224 | tf_op jit(solution)/shard_map/ppermute | solution.py:446
  40.1 4.7 %collective-permute-start.11 = (f32[2,128,128]{2,1,0:T(8,128)S(1)}, f32[2,128,128]{2,1,0:T(8,128)S(1)}, u32[]{:S(2)}, u32[]{:S(2)}) collective-permute-start(f32[2,128,128]{2,1,0:T(8,128)S(1)} %get-tuple-element.60.refs_2_), channel_id=1, source_target_pairs={{0,1},{1,0},{2,3},{3,2},{4,5},{5,4},{6,7},{7,6},{8,9},{9,8},{10,11... | collective-permute-start | bytes 393224 | tf_op jit(solution)/shard_map/ppermute | solution.py:446
  44.8 1.5 %collective-permute-start.12 = (f32[2,128,128]{2,1,0:T(8,128)S(1)}, f32[2,128,128]{2,1,0:T(8,128)S(1)}, u32[]{:S(2)}, u32[]{:S(2)}) collective-permute-start(f32[2,128,128]{2,1,0:T(8,128)S(1)} %collective-permute-done.9.refs_3_), channel_id=1, source_target_pairs={{0,1},{1,0},{2,3},{3,2},{4,5},{5,4},{6,7},{7,6},{8,9},{9,8},{10,11... | collective-permute-start | bytes 393224 | tf_op jit(solution)/shard_map/ppermute | solution.py:446
  46.3 1.2 %collective-permute-start.13 = (f32[2,128,128]{2,1,0:T(8,128)S(1)}, f32[2,128,128]{2,1,0:T(8,128)S(1)}, u32[]{:S(2)}, u32[]{:S(2)}) collective-permute-start(f32[2,128,128]{2,1,0:T(8,128)S(1)} %collective-permute-done.10.refs_4_), channel_id=1, source_target_pairs={{0,1},{1,0},{2,3},{3,2},{4,5},{5,4},{6,7},{7,6},{8,9},{9,8},{10,11... | collective-permute-start | bytes 393224 | tf_op jit(solution)/shard_map/ppermute | solution.py:446
  47.5 1.7 %collective-permute-start.8 = (f32[2,128,128]{2,1,0:T(8,128)S(1)}, f32[2,128,128]{2,1,0:T(8,128)S(1)}, u32[]{:S(2)}, u32[]{:S(2)}) collective-permute-start(f32[2,128,128]{2,1,0:T(8,128)S(1)} %collective-permute-done.7.refs_5_), channel_id=1, source_target_pairs={{0,1},{1,0},{2,3},{3,2},{4,5},{5,4},{6,7},{7,6},{8,9},{9,8},{10,11... | collective-permute-start | bytes 393224 | tf_op jit(solution)/shard_map/ppermute | solution.py:446
  49.3 0.6 %early_output.1.early_ref = bf16[14,128,128]{2,1,0:T(8,128)(2,1)S(1)} custom-call(f32[1,128]{1,0:T(1,128)S(1)} %get-tuple-element.34.gain_ref, f32[8,128,256]{2,1,0:T(8,128)S(1)} %get-tuple-element.52.after_ref.refs_0_, f32[8,128,256]{2,1,0:T(8,128)S(1)} %get-tuple-element.47.refs_1_.read_ref, f32[2,128,128]{2,1,0:T(8,128)S(1)} %get-tuple-element.60.refs_2_, ...), custom_call_target="tpu_custom_call" | custom-call | flops 176160768 | bytes 3473920 | tf_op jit(solution)/shard_map/early_output/pallas_call | solution.py:407
  49.9 0.4 collective-permute-done.8.state_ref
  50.2 1.1 %output.1 = bf16[128,2048]{1,0:T(8,128)(2,1)} custom-call(f32[1,128]{1,0:T(1,128)S(1)} %get-tuple-element.34.gain_ref, f32[8,128,256]{2,1,0:T(8,128)S(1)} %get-tuple-element.47.refs_1_.read_ref, f32[2,128,128]{2,1,0:T(8,128)S(1)} %collective-permute-done.8.state_ref, bf16[14,128,128]{2,1,0:T(8,128)(2,1)S(1)} %early_output.1.early_ref), custom_call_target="tpu_custom_call" | custom-call | flops 25165824 | bytes 2163200 | tf_op jit(solution)/shard_map/output/pallas_call | solution.py:407
  (8 shorter events, 0.0 us)
Async XLA Ops:
  5.4 4.7 %collective-permute-start = (f32[8,128,256]{2,1,0:T(8,128)S(1)}, f32[8,128,256]{2,1,0:T(8,128)S(1)}, u32[]{:S(2)}, u32[]{:S(2)}) collective-permute-start(f32[8,128,256]{2,1,0:T(8,128)S(1)} %get-tuple-element.45), channel_id=1, source_target_pairs={{0,1},{1,0},{2,3},{3,2},{4,5},{5,4},{6,7},{7,6},{8,9},{9,8},{10,11... | collective-permute-start | bytes 3145736 | tf_op jit(solution)/shard_map/ppermute | solution.py:446
  10.0 3.4 %copy-start = (bf16[128,1024]{1,0:T(8,128)(2,1)S(1)}, bf16[128,1024]{1,0:T(8,128)(2,1)}, u32[]{:S(2)}) copy-start(bf16[128,1024]{1,0:T(8,128)(2,1)} %q_ref.1) | copy-start | bytes 786436
  10.0 3.4 %collective-permute-start.1 = (f32[8,128,256]{2,1,0:T(8,128)S(1)}, f32[8,128,256]{2,1,0:T(8,128)S(1)}, u32[]{:S(2)}, u32[]{:S(2)}) collective-permute-start(f32[8,128,256]{2,1,0:T(8,128)S(1)} %get-tuple-element.46.keep_ref), channel_id=1, source_target_pairs={{0,1},{1,0},{2,3},{3,2},{4,5},{5,4},{6,7},{7,6},{8,9},{9,8},{10,11... | collective-permute-start | bytes 3145736 | tf_op jit(solution)/shard_map/ppermute | solution.py:446
  10.6 7.6 %collective-permute-start.2 = (f32[2,128,256]{2,1,0:T(8,128)S(1)}, f32[2,128,256]{2,1,0:T(8,128)S(1)}, u32[]{:S(2)}, u32[]{:S(2)}) collective-permute-start(f32[2,128,256]{2,1,0:T(8,128)S(1)} %get-tuple-element.49), channel_id=1, source_target_pairs={{0,2},{1,3},{2,0},{3,1},{4,6},{5,7},{6,4},{7,5},{8,10},{9,11},{10,... | collective-permute-start | bytes 786440 | tf_op jit(solution)/shard_map/ppermute | solution.py:446
  11.9 7.1 %collective-permute-start.3 = (f32[2,128,256]{2,1,0:T(8,128)S(1)}, f32[2,128,256]{2,1,0:T(8,128)S(1)}, u32[]{:S(2)}, u32[]{:S(2)}) collective-permute-start(f32[2,128,256]{2,1,0:T(8,128)S(1)} %get-tuple-element.50), channel_id=1, source_target_pairs={{0,4},{1,5},{2,6},{3,7},{4,0},{5,1},{6,2},{7,3},{8,12},{9,13},{10,... | collective-permute-start | bytes 786440 | tf_op jit(solution)/shard_map/ppermute | solution.py:446
  13.2 11.6 %collective-permute-start.4 = (f32[2,128,256]{2,1,0:T(8,128)S(1)}, f32[2,128,256]{2,1,0:T(8,128)S(1)}, u32[]{:S(2)}, u32[]{:S(2)}) collective-permute-start(f32[2,128,256]{2,1,0:T(8,128)S(1)} %get-tuple-element.51), channel_id=1, source_target_pairs={{0,6},{1,7},{2,4},{3,5},{4,2},{5,3},{6,0},{7,1},{8,14},{9,15},{10,... | collective-permute-start | bytes 786440 | tf_op jit(solution)/shard_map/ppermute | solution.py:446
  25.4 5.7 %collective-permute-start.5 = (f32[2,128,128]{2,1,0:T(8,128)S(1)}, f32[2,128,128]{2,1,0:T(8,128)S(1)}, u32[]{:S(2)}, u32[]{:S(2)}) collective-permute-start(f32[2,128,128]{2,1,0:T(8,128)S(1)} %get-tuple-element.58.add_ref), channel_id=1, source_target_pairs={{0,8},{1,9},{2,10},{3,11},{4,12},{5,13},{6,14},{7,15},{8,16},{9,17... | collective-permute-start | bytes 393224 | tf_op jit(solution)/shard_map/ppermute | solution.py:446
  31.4 5.7 %collective-permute-start.6 = (f32[2,128,128]{2,1,0:T(8,128)S(1)}, f32[2,128,128]{2,1,0:T(8,128)S(1)}, u32[]{:S(2)}, u32[]{:S(2)}) collective-permute-start(f32[2,128,128]{2,1,0:T(8,128)S(1)} %step.1), channel_id=1, source_target_pairs={{0,8},{1,9},{2,10},{3,11},{4,12},{5,13},{6,14},{7,15},{8,16},{9,17... | collective-permute-start | bytes 393224 | tf_op jit(solution)/shard_map/ppermute | solution.py:446
  37.4 7.4 %collective-permute-start.9 = (f32[2,128,128]{2,1,0:T(8,128)S(1)}, f32[2,128,128]{2,1,0:T(8,128)S(1)}, u32[]{:S(2)}, u32[]{:S(2)}) collective-permute-start(f32[2,128,128]{2,1,0:T(8,128)S(1)} %get-tuple-element.61), channel_id=1, source_target_pairs={{0,2},{1,3},{2,0},{3,1},{4,6},{5,7},{6,4},{7,5},{8,10},{9,11},{10,... | collective-permute-start | bytes 393224 | tf_op jit(solution)/shard_map/ppermute | solution.py:446
  38.6 7.6 %collective-permute-start.10 = (f32[2,128,128]{2,1,0:T(8,128)S(1)}, f32[2,128,128]{2,1,0:T(8,128)S(1)}, u32[]{:S(2)}, u32[]{:S(2)}) collective-permute-start(f32[2,128,128]{2,1,0:T(8,128)S(1)} %get-tuple-element.62), channel_id=1, source_target_pairs={{0,4},{1,5},{2,6},{3,7},{4,0},{5,1},{6,2},{7,3},{8,12},{9,13},{10,... | collective-permute-start | bytes 393224 | tf_op jit(solution)/shard_map/ppermute | solution.py:446
  39.0 8.6 %collective-permute-start.7 = (f32[2,128,128]{2,1,0:T(8,128)S(1)}, f32[2,128,128]{2,1,0:T(8,128)S(1)}, u32[]{:S(2)}, u32[]{:S(2)}) collective-permute-start(f32[2,128,128]{2,1,0:T(8,128)S(1)} %get-tuple-element.59), channel_id=1, source_target_pairs={{0,6},{1,7},{2,4},{3,5},{4,2},{5,3},{6,0},{7,1},{8,14},{9,15},{10,... | collective-permute-start | bytes 393224 | tf_op jit(solution)/shard_map/ppermute | solution.py:446
  40.1 9.1 %collective-permute-start.11 = (f32[2,128,128]{2,1,0:T(8,128)S(1)}, f32[2,128,128]{2,1,0:T(8,128)S(1)}, u32[]{:S(2)}, u32[]{:S(2)}) collective-permute-start(f32[2,128,128]{2,1,0:T(8,128)S(1)} %get-tuple-element.60.refs_2_), channel_id=1, source_target_pairs={{0,1},{1,0},{2,3},{3,2},{4,5},{5,4},{6,7},{7,6},{8,9},{9,8},{10,11... | collective-permute-start | bytes 393224 | tf_op jit(solution)/shard_map/ppermute | solution.py:446
  44.8 4.5 %collective-permute-start.12 = (f32[2,128,128]{2,1,0:T(8,128)S(1)}, f32[2,128,128]{2,1,0:T(8,128)S(1)}, u32[]{:S(2)}, u32[]{:S(2)}) collective-permute-start(f32[2,128,128]{2,1,0:T(8,128)S(1)} %collective-permute-done.9.refs_3_), channel_id=1, source_target_pairs={{0,1},{1,0},{2,3},{3,2},{4,5},{5,4},{6,7},{7,6},{8,9},{9,8},{10,11... | collective-permute-start | bytes 393224 | tf_op jit(solution)/shard_map/ppermute | solution.py:446
  46.3 3.0 %collective-permute-start.13 = (f32[2,128,128]{2,1,0:T(8,128)S(1)}, f32[2,128,128]{2,1,0:T(8,128)S(1)}, u32[]{:S(2)}, u32[]{:S(2)}) collective-permute-start(f32[2,128,128]{2,1,0:T(8,128)S(1)} %collective-permute-done.10.refs_4_), channel_id=1, source_target_pairs={{0,1},{1,0},{2,3},{3,2},{4,5},{5,4},{6,7},{7,6},{8,9},{9,8},{10,11... | collective-permute-start | bytes 393224 | tf_op jit(solution)/shard_map/ppermute | solution.py:446
  47.5 2.7 %collective-permute-start.8 = (f32[2,128,128]{2,1,0:T(8,128)S(1)}, f32[2,128,128]{2,1,0:T(8,128)S(1)}, u32[]{:S(2)}, u32[]{:S(2)}) collective-permute-start(f32[2,128,128]{2,1,0:T(8,128)S(1)} %collective-permute-done.7.refs_5_), channel_id=1, source_target_pairs={{0,1},{1,0},{2,3},{3,2},{4,5},{5,4},{6,7},{7,6},{8,9},{9,8},{10,11... | collective-permute-start | bytes 393224 | tf_op jit(solution)/shard_map/ppermute | solution.py:446

commit v5 on v4

--- a/solution.py
+++ b/solution.py
@@ -75,12 +75,6 @@
     return mm(
         jnp.concatenate([a[0], a[1], a[0]], axis=1), jnp.concatenate([b[0], b[0], b[1]], axis=0)
     )
-
-
-def mm_half(a, b):
-    rows = a[0].shape[0]
-    out = mm(jnp.concatenate(a, axis=0), b)
-    return out[:rows] + out[rows:]
 
 
 def mm3(a, b):
@@ -279,9 +273,9 @@
     for i, (key, key_t, n_row, b_row, from_row, end) in enumerate(details):
         inverse_ref[i] = solved[i]
         through = fold(mm(key_t, across(*split(solved[i] * end))))
-        mapped = mm_half(split(through * (b_row * from_row * n_row)), key)
+        mapped = mm2(through * (b_row * from_row * n_row), key)
         map_ref[i, :, :D] = from_row[:, BLOCK - 1 :] * eye - mapped
-        map_ref[i, :, D:] = mm_half(split(through * b_row), columns(v_ref, heads[i]))
+        map_ref[i, :, D:] = mm2(through * b_row, columns(v_ref, heads[i]))
 
 
 def chip_kernel(n_sub, keep_ref, recv_ref, *out_refs):

time: 51.8 us -> 51.6 us (level)
  no operation moved by 1% of the time
where the time goes in v5:
time: 51.6 us; the launch traced here: 51.2 us
  starting transfers between devices  18 us (35%)
  Pallas kernels  17.6 us (34%)
  waiting for transfers between devices  15.4 us (30%)
    ppermute x14, starting transfers between devices, permute(): return lax.ppermute(x, AXES, pairs)  18 us
    pallas_call x10, Pallas kernels, call(): pl.pallas_call(kernel, out_shape=outs, in_specs=[VMEM] * len(args) if spe...  17.6 us
    ppermute x14, waiting for transfers between devices, permute(): return lax.ppermute(x, AXES, pairs)  15.4 us
  transfers between devices with their start and end apart: 14, of which 5 were waited for; matrix products, arithmetic and copies ran while one was open for 0% of the time, Pallas kernels for 20%

profile of v5, /device:TPU:25, one launch (start us, length us, event | category | flops | bytes accessed | tf_op | source)
XLA Modules:
  0.0 51.2 jit_solution(15454129921658415221)
XLA Ops:
  0.0 5.3 %first_maps.1 = (f32[8,128,256]{2,1,0:T(8,128)S(1)}, f32[8,128,128]{2,1,0:T(8,128)S(1)}, bf16[128,1024]{1,0:T(8,128)(2,1)S(1)}, bf16[128,2048]{1,0:T(8,128)(2,1)...) custom-call(s32[8]{0:T(128)} %refs_0_.1, ...), custom_call_target="tpu_custom_call" | custom-call | flops 1476395008 | bytes 3265568 | tf_op jit(solution)/shard_map/first_maps/pallas_call | solution.py:401
  5.3 0.7 %collective-permute-start = (f32[8,128,256]{2,1,0:T(8,128)S(1)}, f32[8,128,256]{2,1,0:T(8,128)S(1)}, u32[]{:S(2)}, u32[]{:S(2)}) collective-permute-start(f32[8,128,256]{2,1,0:T(8,128)S(1)} %get-tuple-element.45), channel_id=1, source_target_pairs={{0,1},{1,0},{2,3},{3,2},{4,5},{5,4},{6,7},{7,6},{8,9},{9,8},{10,11... | collective-permute-start | bytes 3145736 | tf_op jit(solution)/shard_map/ppermute | solution.py:440
  6.0 3.8 %second_maps.1 = (f32[8,128,256]{2,1,0:T(8,128)S(1)}, f32[8,128,128]{2,1,0:T(8,128)S(1)}) custom-call(bf16[128,1024]{1,0:T(8,128)(2,1)S(1)} %get-tuple-element.35.refs_0_.k_ref, bf16[128,2048]{1,0:T(8,128)(2,1)S(1)} %get-tuple-element.36.refs_1_.v_ref, f32[16,128]{1,0:T(8,128)S(1)} %get-tuple-element.37.refs_2_.refs_0_, ...), custom_call_target="tpu_custom_call" | custom-call | flops 1476395008 | bytes 2461696 | tf_op jit(solution)/shard_map/second_maps/pallas_call | solution.py:401
  9.8 0.0 copy-start
  9.8 0.1 collective-permute-start.1
  9.9 0.0 collective-permute-done.refs_8_.recv_ref
  9.9 0.5 %chip.1 = (f32[2,128,256]{2,1,0:T(8,128)S(1)}, f32[2,128,256]{2,1,0:T(8,128)S(1)}, f32[2,128,256]{2,1,0:T(8,128)S(1)}, f32[2,128,256]{2,1,0:T(8,128)S(1)}) custom-call(f32[8,128,256]{2,1,0:T(8,128)S(1)} %get-tuple-element.46.keep_ref, f32[8,128,256]{2,1,0:T(8,128)S(1)} %collective-permute-done.refs_8_.recv_ref), custom_call_target="tpu_custom_call" | custom-call | flops 201326592 | bytes 3145728 | tf_op jit(solution)/shard_map/chip/pallas_call | solution.py:401
  10.5 1.3 %collective-permute-start.2 = (f32[2,128,256]{2,1,0:T(8,128)S(1)}, f32[2,128,256]{2,1,0:T(8,128)S(1)}, u32[]{:S(2)}, u32[]{:S(2)}) collective-permute-start(f32[2,128,256]{2,1,0:T(8,128)S(1)} %get-tuple-element.49), channel_id=1, source_target_pairs={{0,2},{1,3},{2,0},{3,1},{4,6},{5,7},{6,4},{7,5},{8,10},{9,11},{10,... | collective-permute-start | bytes 786440 | tf_op jit(solution)/shard_map/ppermute | solution.py:440
  11.7 1.2 %collective-permute-start.3 = (f32[2,128,256]{2,1,0:T(8,128)S(1)}, f32[2,128,256]{2,1,0:T(8,128)S(1)}, u32[]{:S(2)}, u32[]{:S(2)}) collective-permute-start(f32[2,128,256]{2,1,0:T(8,128)S(1)} %get-tuple-element.50), channel_id=1, source_target_pairs={{0,4},{1,5},{2,6},{3,7},{4,0},{5,1},{6,2},{7,3},{8,12},{9,13},{10,... | collective-permute-start | bytes 786440 | tf_op jit(solution)/shard_map/ppermute | solution.py:440
  13.0 0.2 collective-permute-start.4
  13.2 4.8 %readout.1 = (f32[8,128,256]{2,1,0:T(8,128)S(1)}, f32[8,128,256]{2,1,0:T(8,128)S(1)}) custom-call(bf16[128,1024]{1,0:T(8,128)(2,1)S(1)} %copy-done, bf16[128,1024]{1,0:T(8,128)(2,1)S(1)} %get-tuple-element.35.refs_0_.k_ref, bf16[128,2048]{1,0:T(8,128)(2,1)S(1)} %get-tuple-element.36.refs_1_.v_ref, f32[16,128]{1,0:T(8,128)S(1)} %get-tuple-element.37.refs_2_.refs_0_, ...), custom_call_target="tpu_custom_call" | custom-call | flops 872415232 | bytes 6393856 | tf_op jit(solution)/shard_map/readout/pallas_call | solution.py:401
  18.0 0.0 collective-permute-done.2.r1
  18.0 0.8 %collective-permute-done.3.r2 = f32[2,128,256]{2,1,0:T(8,128)S(1)} collective-permute-done((f32[2,128,256]{2,1,0:T(8,128)S(1)}, f32[2,128,256]{2,1,0:T(8,128)S(1)}, u32[]{:S(2)}, u32[]{:S(2)}) %collective-permute-start.3) | collective-permute-done | bytes 262176 | tf_op jit(solution)/shard_map/ppermute | solution.py:440
  18.8 5.7 %collective-permute-done.4.r3 = f32[2,128,256]{2,1,0:T(8,128)S(1)} collective-permute-done((f32[2,128,256]{2,1,0:T(8,128)S(1)}, f32[2,128,256]{2,1,0:T(8,128)S(1)}, u32[]{:S(2)}, u32[]{:S(2)}) %collective-permute-start.4) | collective-permute-done | bytes 262176 | tf_op jit(solution)/shard_map/ppermute | solution.py:440
  24.5 0.7 %group.1 = (f32[2,128,128]{2,1,0:T(8,128)S(1)}, f32[2,2,128,256]{3,2,1,0:T(8,128)S(1)}, f32[2,128,256]{2,1,0:T(8,128)S(1)}, f32[2,128,256]{2,1,0:T(8,128)S(1)}) custom-call(f32[2,128,256]{2,1,0:T(8,128)S(1)} %get-tuple-element.48.r0, f32[2,128,256]{2,1,0:T(8,128)S(1)} %collective-permute-done.2.r1, f32[2,128,256]{2,1,0:T(8,128)S(1)} %collective-permute-done.3.r2, ...), custom_call_target="tpu_custom_call" | custom-call | flops 125829120 | bytes 3276800 | tf_op jit(solution)/shard_map/group/pallas_call | solution.py:401
  25.2 1.3 %collective-permute-start.5 = (f32[2,128,128]{2,1,0:T(8,128)S(1)}, f32[2,128,128]{2,1,0:T(8,128)S(1)}, u32[]{:S(2)}, u32[]{:S(2)}) collective-permute-start(f32[2,128,128]{2,1,0:T(8,128)S(1)} %get-tuple-element.58.add_ref), channel_id=1, source_target_pairs={{0,8},{1,9},{2,10},{3,11},{4,12},{5,13},{6,14},{7,15},{8,16},{9,17... | collective-permute-start | bytes 393224 | tf_op jit(solution)/shard_map/ppermute | solution.py:440
  26.5 0.3 ahead.1
  26.8 4.1 %collective-permute-done.5.state_ref = f32[2,128,128]{2,1,0:T(8,128)S(1)} collective-permute-done((f32[2,128,128]{2,1,0:T(8,128)S(1)}, f32[2,128,128]{2,1,0:T(8,128)S(1)}, u32[]{:S(2)}, u32[]{:S(2)}) %collective-permute-start.5) | collective-permute-done | bytes 131104 | tf_op jit(solution)/shard_map/ppermute | solution.py:440
  31.0 0.2 step.1
  31.2 1.3 %collective-permute-start.6 = (f32[2,128,128]{2,1,0:T(8,128)S(1)}, f32[2,128,128]{2,1,0:T(8,128)S(1)}, u32[]{:S(2)}, u32[]{:S(2)}) collective-permute-start(f32[2,128,128]{2,1,0:T(8,128)S(1)} %step.1), channel_id=1, source_target_pairs={{0,8},{1,9},{2,10},{3,11},{4,12},{5,13},{6,14},{7,15},{8,16},{9,17... | collective-permute-start | bytes 393224 | tf_op jit(solution)/shard_map/ppermute | solution.py:440
  32.5 4.4 %collective-permute-done.6.state_ref = f32[2,128,128]{2,1,0:T(8,128)S(1)} collective-permute-done((f32[2,128,128]{2,1,0:T(8,128)S(1)}, f32[2,128,128]{2,1,0:T(8,128)S(1)}, u32[]{:S(2)}, u32[]{:S(2)}) %collective-permute-start.6) | collective-permute-done | bytes 131104 | tf_op jit(solution)/shard_map/ppermute | solution.py:440
  36.9 0.3 spread.1
  37.2 1.2 %collective-permute-start.9 = (f32[2,128,128]{2,1,0:T(8,128)S(1)}, f32[2,128,128]{2,1,0:T(8,128)S(1)}, u32[]{:S(2)}, u32[]{:S(2)}) collective-permute-start(f32[2,128,128]{2,1,0:T(8,128)S(1)} %get-tuple-element.61), channel_id=1, source_target_pairs={{0,2},{1,3},{2,0},{3,1},{4,6},{5,7},{6,4},{7,5},{8,10},{9,11},{10,... | collective-permute-start | bytes 393224 | tf_op jit(solution)/shard_map/ppermute | solution.py:440
  38.5 0.3 collective-permute-start.10
  38.8 1.2 %collective-permute-start.7 = (f32[2,128,128]{2,1,0:T(8,128)S(1)}, f32[2,128,128]{2,1,0:T(8,128)S(1)}, u32[]{:S(2)}, u32[]{:S(2)}) collective-permute-start(f32[2,128,128]{2,1,0:T(8,128)S(1)} %get-tuple-element.59), channel_id=1, source_target_pairs={{0,6},{1,7},{2,4},{3,5},{4,2},{5,3},{6,0},{7,1},{8,14},{9,15},{10,... | collective-permute-start | bytes 393224 | tf_op jit(solution)/shard_map/ppermute | solution.py:440
  39.9 4.7 %collective-permute-start.11 = (f32[2,128,128]{2,1,0:T(8,128)S(1)}, f32[2,128,128]{2,1,0:T(8,128)S(1)}, u32[]{:S(2)}, u32[]{:S(2)}) collective-permute-start(f32[2,128,128]{2,1,0:T(8,128)S(1)} %get-tuple-element.60.refs_2_), channel_id=1, source_target_pairs={{0,1},{1,0},{2,3},{3,2},{4,5},{5,4},{6,7},{7,6},{8,9},{9,8},{10,11... | collective-permute-start | bytes 393224 | tf_op jit(solution)/shard_map/ppermute | solution.py:440
  44.6 1.5 %collective-permute-start.12 = (f32[2,128,128]{2,1,0:T(8,128)S(1)}, f32[2,128,128]{2,1,0:T(8,128)S(1)}, u32[]{:S(2)}, u32[]{:S(2)}) collective-permute-start(f32[2,128,128]{2,1,0:T(8,128)S(1)} %collective-permute-done.9.refs_3_), channel_id=1, source_target_pairs={{0,1},{1,0},{2,3},{3,2},{4,5},{5,4},{6,7},{7,6},{8,9},{9,8},{10,11... | collective-permute-start | bytes 393224 | tf_op jit(solution)/shard_map/ppermute | solution.py:440
  46.1 1.2 %collective-permute-start.13 = (f32[2,128,128]{2,1,0:T(8,128)S(1)}, f32[2,128,128]{2,1,0:T(8,128)S(1)}, u32[]{:S(2)}, u32[]{:S(2)}) collective-permute-start(f32[2,128,128]{2,1,0:T(8,128)S(1)} %collective-permute-done.10.refs_4_), channel_id=1, source_target_pairs={{0,1},{1,0},{2,3},{3,2},{4,5},{5,4},{6,7},{7,6},{8,9},{9,8},{10,11... | collective-permute-start | bytes 393224 | tf_op jit(solution)/shard_map/ppermute | solution.py:440
  47.3 1.7 %collective-permute-start.8 = (f32[2,128,128]{2,1,0:T(8,128)S(1)}, f32[2,128,128]{2,1,0:T(8,128)S(1)}, u32[]{:S(2)}, u32[]{:S(2)}) collective-permute-start(f32[2,128,128]{2,1,0:T(8,128)S(1)} %collective-permute-done.7.refs_5_), channel_id=1, source_target_pairs={{0,1},{1,0},{2,3},{3,2},{4,5},{5,4},{6,7},{7,6},{8,9},{9,8},{10,11... | collective-permute-start | bytes 393224 | tf_op jit(solution)/shard_map/ppermute | solution.py:440
  49.1 0.6 %early_output.1.early_ref = bf16[14,128,128]{2,1,0:T(8,128)(2,1)S(1)} custom-call(f32[1,128]{1,0:T(1,128)S(1)} %get-tuple-element.34.gain_ref, f32[8,128,256]{2,1,0:T(8,128)S(1)} %get-tuple-element.52.after_ref.refs_0_, f32[8,128,256]{2,1,0:T(8,128)S(1)} %get-tuple-element.47.refs_1_.read_ref, f32[2,128,128]{2,1,0:T(8,128)S(1)} %get-tuple-element.60.refs_2_, ...), custom_call_target="tpu_custom_call" | custom-call | flops 176160768 | bytes 3473920 | tf_op jit(solution)/shard_map/early_output/pallas_call | solution.py:401
  49.7 0.4 collective-permute-done.8.state_ref
  50.0 1.1 %output.1 = bf16[128,2048]{1,0:T(8,128)(2,1)} custom-call(f32[1,128]{1,0:T(1,128)S(1)} %get-tuple-element.34.gain_ref, f32[8,128,256]{2,1,0:T(8,128)S(1)} %get-tuple-element.47.refs_1_.read_ref, f32[2,128,128]{2,1,0:T(8,128)S(1)} %collective-permute-done.8.state_ref, bf16[14,128,128]{2,1,0:T(8,128)(2,1)S(1)} %early_output.1.early_ref), custom_call_target="tpu_custom_call" | custom-call | flops 25165824 | bytes 2163200 | tf_op jit(solution)/shard_map/output/pallas_call | solution.py:401
  (8 shorter events, 0.0 us)
Async XLA Ops:
  5.3 4.7 %collective-permute-start = (f32[8,128,256]{2,1,0:T(8,128)S(1)}, f32[8,128,256]{2,1,0:T(8,128)S(1)}, u32[]{:S(2)}, u32[]{:S(2)}) collective-permute-start(f32[8,128,256]{2,1,0:T(8,128)S(1)} %get-tuple-element.45), channel_id=1, source_target_pairs={{0,1},{1,0},{2,3},{3,2},{4,5},{5,4},{6,7},{7,6},{8,9},{9,8},{10,11... | collective-permute-start | bytes 3145736 | tf_op jit(solution)/shard_map/ppermute | solution.py:440
  9.8 3.4 %copy-start = (bf16[128,1024]{1,0:T(8,128)(2,1)S(1)}, bf16[128,1024]{1,0:T(8,128)(2,1)}, u32[]{:S(2)}) copy-start(bf16[128,1024]{1,0:T(8,128)(2,1)} %q_ref.1) | copy-start | bytes 786436
  9.8 3.4 %collective-permute-start.1 = (f32[8,128,256]{2,1,0:T(8,128)S(1)}, f32[8,128,256]{2,1,0:T(8,128)S(1)}, u32[]{:S(2)}, u32[]{:S(2)}) collective-permute-start(f32[8,128,256]{2,1,0:T(8,128)S(1)} %get-tuple-element.46.keep_ref), channel_id=1, source_target_pairs={{0,1},{1,0},{2,3},{3,2},{4,5},{5,4},{6,7},{7,6},{8,9},{9,8},{10,11... | collective-permute-start | bytes 3145736 | tf_op jit(solution)/shard_map/ppermute | solution.py:440
  10.5 7.5 %collective-permute-start.2 = (f32[2,128,256]{2,1,0:T(8,128)S(1)}, f32[2,128,256]{2,1,0:T(8,128)S(1)}, u32[]{:S(2)}, u32[]{:S(2)}) collective-permute-start(f32[2,128,256]{2,1,0:T(8,128)S(1)} %get-tuple-element.49), channel_id=1, source_target_pairs={{0,2},{1,3},{2,0},{3,1},{4,6},{5,7},{6,4},{7,5},{8,10},{9,11},{10,... | collective-permute-start | bytes 786440 | tf_op jit(solution)/shard_map/ppermute | solution.py:440
  11.7 7.1 %collective-permute-start.3 = (f32[2,128,256]{2,1,0:T(8,128)S(1)}, f32[2,128,256]{2,1,0:T(8,128)S(1)}, u32[]{:S(2)}, u32[]{:S(2)}) collective-permute-start(f32[2,128,256]{2,1,0:T(8,128)S(1)} %get-tuple-element.50), channel_id=1, source_target_pairs={{0,4},{1,5},{2,6},{3,7},{4,0},{5,1},{6,2},{7,3},{8,12},{9,13},{10,... | collective-permute-start | bytes 786440 | tf_op jit(solution)/shard_map/ppermute | solution.py:440
  13.0 11.6 %collective-permute-start.4 = (f32[2,128,256]{2,1,0:T(8,128)S(1)}, f32[2,128,256]{2,1,0:T(8,128)S(1)}, u32[]{:S(2)}, u32[]{:S(2)}) collective-permute-start(f32[2,128,256]{2,1,0:T(8,128)S(1)} %get-tuple-element.51), channel_id=1, source_target_pairs={{0,6},{1,7},{2,4},{3,5},{4,2},{5,3},{6,0},{7,1},{8,14},{9,15},{10,... | collective-permute-start | bytes 786440 | tf_op jit(solution)/shard_map/ppermute | solution.py:440
  25.2 5.7 %collective-permute-start.5 = (f32[2,128,128]{2,1,0:T(8,128)S(1)}, f32[2,128,128]{2,1,0:T(8,128)S(1)}, u32[]{:S(2)}, u32[]{:S(2)}) collective-permute-start(f32[2,128,128]{2,1,0:T(8,128)S(1)} %get-tuple-element.58.add_ref), channel_id=1, source_target_pairs={{0,8},{1,9},{2,10},{3,11},{4,12},{5,13},{6,14},{7,15},{8,16},{9,17... | collective-permute-start | bytes 393224 | tf_op jit(solution)/shard_map/ppermute | solution.py:440
  31.2 5.7 %collective-permute-start.6 = (f32[2,128,128]{2,1,0:T(8,128)S(1)}, f32[2,128,128]{2,1,0:T(8,128)S(1)}, u32[]{:S(2)}, u32[]{:S(2)}) collective-permute-start(f32[2,128,128]{2,1,0:T(8,128)S(1)} %step.1), channel_id=1, source_target_pairs={{0,8},{1,9},{2,10},{3,11},{4,12},{5,13},{6,14},{7,15},{8,16},{9,17... | collective-permute-start | bytes 393224 | tf_op jit(solution)/shard_map/ppermute | solution.py:440
  37.2 7.4 %collective-permute-start.9 = (f32[2,128,128]{2,1,0:T(8,128)S(1)}, f32[2,128,128]{2,1,0:T(8,128)S(1)}, u32[]{:S(2)}, u32[]{:S(2)}) collective-permute-start(f32[2,128,128]{2,1,0:T(8,128)S(1)} %get-tuple-element.61), channel_id=1, source_target_pairs={{0,2},{1,3},{2,0},{3,1},{4,6},{5,7},{6,4},{7,5},{8,10},{9,11},{10,... | collective-permute-start | bytes 393224 | tf_op jit(solution)/shard_map/ppermute | solution.py:440
  38.5 7.6 %collective-permute-start.10 = (f32[2,128,128]{2,1,0:T(8,128)S(1)}, f32[2,128,128]{2,1,0:T(8,128)S(1)}, u32[]{:S(2)}, u32[]{:S(2)}) collective-permute-start(f32[2,128,128]{2,1,0:T(8,128)S(1)} %get-tuple-element.62), channel_id=1, source_target_pairs={{0,4},{1,5},{2,6},{3,7},{4,0},{5,1},{6,2},{7,3},{8,12},{9,13},{10,... | collective-permute-start | bytes 393224 | tf_op jit(solution)/shard_map/ppermute | solution.py:440
  38.8 8.6 %collective-permute-start.7 = (f32[2,128,128]{2,1,0:T(8,128)S(1)}, f32[2,128,128]{2,1,0:T(8,128)S(1)}, u32[]{:S(2)}, u32[]{:S(2)}) collective-permute-start(f32[2,128,128]{2,1,0:T(8,128)S(1)} %get-tuple-element.59), channel_id=1, source_target_pairs={{0,6},{1,7},{2,4},{3,5},{4,2},{5,3},{6,0},{7,1},{8,14},{9,15},{10,... | collective-permute-start | bytes 393224 | tf_op jit(solution)/shard_map/ppermute | solution.py:440
  39.9 9.1 %collective-permute-start.11 = (f32[2,128,128]{2,1,0:T(8,128)S(1)}, f32[2,128,128]{2,1,0:T(8,128)S(1)}, u32[]{:S(2)}, u32[]{:S(2)}) collective-permute-start(f32[2,128,128]{2,1,0:T(8,128)S(1)} %get-tuple-element.60.refs_2_), channel_id=1, source_target_pairs={{0,1},{1,0},{2,3},{3,2},{4,5},{5,4},{6,7},{7,6},{8,9},{9,8},{10,11... | collective-permute-start | bytes 393224 | tf_op jit(solution)/shard_map/ppermute | solution.py:440
  44.6 4.5 %collective-permute-start.12 = (f32[2,128,128]{2,1,0:T(8,128)S(1)}, f32[2,128,128]{2,1,0:T(8,128)S(1)}, u32[]{:S(2)}, u32[]{:S(2)}) collective-permute-start(f32[2,128,128]{2,1,0:T(8,128)S(1)} %collective-permute-done.9.refs_3_), channel_id=1, source_target_pairs={{0,1},{1,0},{2,3},{3,2},{4,5},{5,4},{6,7},{7,6},{8,9},{9,8},{10,11... | collective-permute-start | bytes 393224 | tf_op jit(solution)/shard_map/ppermute | solution.py:440
  46.1 3.0 %collective-permute-start.13 = (f32[2,128,128]{2,1,0:T(8,128)S(1)}, f32[2,128,128]{2,1,0:T(8,128)S(1)}, u32[]{:S(2)}, u32[]{:S(2)}) collective-permute-start(f32[2,128,128]{2,1,0:T(8,128)S(1)} %collective-permute-done.10.refs_4_), channel_id=1, source_target_pairs={{0,1},{1,0},{2,3},{3,2},{4,5},{5,4},{6,7},{7,6},{8,9},{9,8},{10,11... | collective-permute-start | bytes 393224 | tf_op jit(solution)/shard_map/ppermute | solution.py:440
  47.3 2.7 %collective-permute-start.8 = (f32[2,128,128]{2,1,0:T(8,128)S(1)}, f32[2,128,128]{2,1,0:T(8,128)S(1)}, u32[]{:S(2)}, u32[]{:S(2)}) collective-permute-start(f32[2,128,128]{2,1,0:T(8,128)S(1)} %collective-permute-done.7.refs_5_), channel_id=1, source_target_pairs={{0,1},{1,0},{2,3},{3,2},{4,5},{5,4},{6,7},{7,6},{8,9},{9,8},{10,11... | collective-permute-start | bytes 393224 | tf_op jit(solution)/shard_map/ppermute | solution.py:440
